TPU v7x, 32 devices: a whole 2x2x4 slice. The times are simulated.
32 devices in a mesh: dp: 2 (over y), expert: 16 (over z, x, core).
Axes of the slice: x: 2, y: 2, z: 4, core: 2. Of those that a mesh axis runs over, the one named last changes fastest.
Arguments:
- cell_rows: bfloat16 [2, 4096, 1024], P(None, ('dp', 'expert')), may hold values from -6 to 6
- cotangent: bfloat16 [2, 4096, 1024], P(None, ('dp', 'expert')), may hold values from -0.75 to 0.75
- cluster_ids: int32 [2, 4096, 1], P(None, ('dp', 'expert')), may hold values from 0 to 15; in each aligned block of 128 rows (0 to 127, 128 to 255, ..., all dimensions but the last counted through in order) at most 8 rows name the same one
- enc_weight: bfloat16 [1024, 1024], replicated, may hold values from -0.1875 to 0.1875
- up_weight: bfloat16 [16, 1024, 2048], P('expert'), may hold values from -0.1875 to 0.1875
- down_weight: bfloat16 [16, 1024, 2048], P('expert'), may hold values from -0.125 to 0.125
Outputs:
- enc_grad: float32 [1024, 1024], P(('dp', 'expert'))
- up_grad: bfloat16 [16, 1024, 2048], P('expert', 'dp')
- down_grad: bfloat16 [16, 1024, 2048], P('expert', 'dp')
Inputs may be any that keep to these rules, and one draw needn't show every extreme that they name: `cluster_ids`: in each micro-batch the 128 rows of one device name one cluster at most 8 times, a bound that some block reaches.
All inputs are finite; a program needn't handle non-finite values.
Results may differ from a plain program's by a relative error of at most 0.014.
Values may be sent and summed in bfloat16 or wider, within the bound.
No kernel may reach another device: no remote copies, remote signals or barrier semaphores. Data moves between devices by JAX's collectives and lax.ppermute only.
A program may use at most 128 MiB of HBM per device.

v0:
```python
import functools

import jax
import jax.numpy as jnp
from jax import lax
from jax.experimental import pallas as pl
from jax.experimental.pallas import tpu as pltpu
from jax.sharding import PartitionSpec as P

epsilon = 1e-06
contract_rows = (((0,), (0,)), ((), ()))
contract_last = (((1,), (1,)), ((), ()))


def silu_pair(pre_value):
    gate_value = jax.nn.sigmoid(pre_value)
    return (pre_value * gate_value, gate_value * (1.0 + pre_value * (1.0 - gate_value)))


def swap(piece, distance):
    pairs = [(i, i ^ distance) for i in range(lax.axis_size("expert"))]
    return lax.ppermute(piece, "expert", pairs)


def place_kernel(experts, low, high, capacity, me_ref, ids_ref, *refs):
    rows_refs, here_refs, refs = refs[:2], refs[2:4], refs[4:]
    near_refs, direct_refs, placer_ref = refs[: 2 * (low - 1)], refs[2 * (low - 1) : -1], refs[-1]
    batches, rows = ids_ref.shape
    width = rows_refs[0].shape[1]
    bucket = batches * capacity
    piece = high * bucket
    slots = experts * bucket
    earlier = (
        lax.broadcasted_iota(jnp.int32, (rows, rows), 0)
        < lax.broadcasted_iota(jnp.int32, (rows, rows), 1)
    )
    earlier = jnp.where(earlier, 1.0, 0.0).astype(jnp.bfloat16)
    for batch_index in range(batches):
        label = ids_ref[batch_index : batch_index + 1, :]
        named = lax.broadcasted_iota(jnp.int32, (experts, rows), 0) == label
        onehot = jnp.where(named, 1.0, 0.0)
        before = jnp.dot(onehot.astype(jnp.bfloat16), earlier, preferred_element_type=jnp.float32)
        rank = jnp.sum(before * onehot, axis=0, keepdims=True).astype(jnp.int32)
        away = label ^ me_ref[0]
        place = (away & (low - 1)) * high + (away >> (low.bit_length() - 1))
        slot = place * bucket + batch_index * capacity + rank
        hit = lax.broadcasted_iota(jnp.int32, (slots, rows), 0) == slot
        placer_ref[:, batch_index * rows : (batch_index + 1) * rows] = jnp.where(
            hit, 1.0, 0.0
        ).astype(jnp.bfloat16)
    for kind in range(2):
        placed = jnp.dot(
            placer_ref[...], rows_refs[kind][...], preferred_element_type=jnp.float32
        ).astype(jnp.bfloat16)
        here_refs[kind][...] = placed[:bucket]
        for step in range(1, high):
            direct_refs[step - 1][:, kind * width : (kind + 1) * width] = placed[
                step * bucket : (step + 1) * bucket
            ]
        for step in range(1, low):
            near_refs[kind * (low - 1) + step - 1][...] = placed[
                step * piece : (step + 1) * piece
            ]


def body(cell_rows, cotangent, cluster_ids, enc_weight, up_weight, down_weight):
    experts = lax.axis_size("expert")
    dp_count = lax.axis_size("dp")
    me = lax.axis_index("expert")
    batch_count, local_rows, model_width = cell_rows.shape
    capacity = max(2, local_rows // 16)
    bucket = batch_count * capacity
    slot_count = experts * bucket
    all_rows = batch_count * local_rows
    high = min(4, experts)
    low = experts // high
    w_up = up_weight[0]
    w_down = down_weight[0]
    fence = lax.optimization_barrier

    vmem = pl.BlockSpec(memory_space=pltpu.VMEM)
    shapes = [(bucket, model_width)] * 2 + [(high * bucket, model_width)] * (2 * (low - 1))
    shapes += [(bucket, 2 * model_width)] * (high - 1)
    placed = pl.pallas_call(
        functools.partial(place_kernel, experts, low, high, capacity),
        out_shape=[jax.ShapeDtypeStruct(shape, jnp.bfloat16) for shape in shapes],
        in_specs=[pl.BlockSpec(memory_space=pltpu.SMEM), vmem, vmem, vmem],
        out_specs=[vmem] * len(shapes),
        scratch_shapes=[pltpu.VMEM((slot_count, all_rows), jnp.bfloat16)],
    )(
        me.astype(jnp.int32)[None],
        cluster_ids[:, :, 0],
        cell_rows.reshape(all_rows, model_width),
        cotangent.reshape(all_rows, model_width),
    )
    here, placed = placed[:2], placed[2:]
    cells_placed, grads_placed = placed[: low - 1], placed[low - 1 : 2 * (low - 1)]
    direct_placed = placed[2 * (low - 1) :]

    def copies(rows):
        pieces = []
        for shift in range(1, dp_count):
            ring = [(i, (i + shift) % dp_count) for i in range(dp_count)]
            pieces.append(lax.ppermute(rows, "dp", ring))
        return pieces

    def forward(features):
        pre_enc = jnp.dot(features, enc_weight, preferred_element_type=jnp.float32)
        silu_enc, slope_enc = silu_pair(pre_enc)
        encoded = features.astype(jnp.float32) + silu_enc
        inverse = lax.rsqrt(jnp.mean(encoded * encoded, axis=1, keepdims=True) + epsilon)
        norm_rows = (encoded * inverse).astype(jnp.bfloat16)
        pre_exp = jnp.dot(norm_rows, w_up, preferred_element_type=jnp.float32)
        silu_exp, slope_exp = silu_pair(pre_exp)
        return encoded, inverse, slope_enc, norm_rows, silu_exp.astype(jnp.bfloat16), slope_exp

    def stack(*pieces):
        return jnp.concatenate(pieces, axis=0)

    def send_near(pieces):
        return [swap(pieces[step - 1], step) for step in range(low - 1, 0, -1)]

    def far_pieces(near):
        return [
            stack(*[piece[step * bucket : (step + 1) * bucket] for piece in near])
            for step in range(high - 1, 0, -1)
        ]

    def send_far(pieces):
        return [swap(piece, step * low) for piece, step in zip(pieces, range(high - 1, 0, -1))]

    def here_and_near(own, near):
        return stack(own, *[piece[:bucket] for piece in near])

    cells_near = send_near(cells_placed)
    direct_placed, cells_near[-1] = fence((direct_placed, cells_near[-1]))
    direct = [swap(direct_placed[step - 1], step * low) for step in range(high - 1, 0, -1)]
    cells_near, direct, here, grads_placed = fence((cells_near, direct, here, grads_placed))
    cells_first, direct, cells_far, grads_placed = fence(
        (
            here_and_near(here[0], cells_near),
            stack(*direct),
            far_pieces(cells_near),
            grads_placed,
        )
    )
    cells_first_copies = copies(cells_first)
    grads_near = send_near(grads_placed)
    cells_far = send_far(cells_far)
    direct_copies = copies(direct)
    grads_near, cells_first_copies = fence((grads_near, cells_first_copies))
    grads_first = here_and_near(here[1], grads_near)
    grads_first_copies = copies(grads_first)
    grads_far = send_far(far_pieces(grads_near))
    came = (cells_first_copies, direct_copies, grads_first_copies)
    cells_far, came = fence((cells_far, came))
    cells_far, came = fence((stack(*cells_far), came))
    cells_far_copies = copies(cells_far)
    features = stack(cells_first, direct[:, :model_width], cells_far)
    grads_far, own_forward = fence((grads_far, forward(features)))
    grads_far, own_forward = fence((stack(*grads_far), own_forward))
    grads_far_copies = copies(grads_far)

    share = model_width // dp_count
    start = lax.axis_index("dp") * share
    block = share // experts

    def my_columns(rows):
        return lax.dynamic_slice_in_dim(rows, start, share, axis=1)

    stages = low.bit_length() - 1
    column = jnp.arange(share, dtype=jnp.int32)
    rank = column // block
    away = rank & (high - 1)
    away = away << stages
    for stage in range(stages):
        away = away | (((rank // high) >> (stages - 1 - stage)) & 1) << stage
    wanted = start + (away ^ me) * block + column % block
    picker = (jnp.arange(model_width, dtype=jnp.int32)[:, None] == wanted[None, :]).astype(
        jnp.bfloat16
    )

    norm_parts, pre_grad_parts, active_parts, grad_parts = [], [], [], []
    enc_parts = []

    def backward(features, grad_rows, values):
        encoded, inverse, slope_enc, norm_rows, active, slope_exp = values
        act_grad = jnp.dot(grad_rows, w_down, preferred_element_type=jnp.float32)
        pre_grad = (act_grad * slope_exp).astype(jnp.bfloat16)
        norm_grad = lax.dot_general(
            pre_grad, w_up, contract_last, preferred_element_type=jnp.float32
        )
        enc_rows_grad = inverse * norm_grad - inverse * inverse * inverse * encoded * jnp.mean(
            norm_grad * encoded, axis=1, keepdims=True
        )
        enc_pre_grad = (enc_rows_grad * slope_enc).astype(jnp.bfloat16)
        picked = jnp.dot(features, picker, preferred_element_type=jnp.float32).astype(jnp.bfloat16)
        enc_parts.append((picked, enc_pre_grad))
        norm_parts.append(my_columns(norm_rows))
        pre_grad_parts.append(pre_grad)
        active_parts.append(active)
        grad_parts.append(my_columns(grad_rows))

    backward(features, stack(grads_first, direct[:, model_width:], grads_far), own_forward)
    cells_far_copies, enc_parts[0] = fence((cells_far_copies, enc_parts[0]))
    for cells_first, direct, grads_first, cells_far, grads_far in zip(
        *came, cells_far_copies, grads_far_copies
    ):
        features = stack(cells_first, direct[:, :model_width], cells_far)
        grad_rows = stack(grads_first, direct[:, model_width:], grads_far)
        backward(features, grad_rows, forward(features))

    def enc_terms(first, last):
        total = None
        for picked, enc_pre_grad in enc_parts:
            term = lax.dot_general(
                picked[:, first:last],
                enc_pre_grad,
                contract_rows,
                preferred_element_type=jnp.float32,
            )
            total = term if total is None else total + term
        return total

    kept = share
    total = None
    for stage in range(stages):
        kept //= 2
        if total is None:
            sent, total = enc_terms(kept, 2 * kept), enc_terms(0, kept)
        else:
            sent, total = total[kept:], total[:kept]
        total = total + swap(sent.astype(jnp.bfloat16), 1 << stage).astype(jnp.float32)
    if total is None:
        total = enc_terms(0, share)
    sent = total.astype(jnp.bfloat16)
    total = total[:block]
    for step in range(1, high):
        piece = sent[step * block : (step + 1) * block]
        total = total + swap(piece, step * low).astype(jnp.float32)

    def rows_product(left, right):
        return lax.dot_general(
            jnp.concatenate(left, axis=0),
            jnp.concatenate(right, axis=0),
            contract_rows,
            preferred_element_type=jnp.float32,
        ).astype(jnp.bfloat16)

    up_sum = rows_product(norm_parts, pre_grad_parts)
    down_sum = rows_product(grad_parts, active_parts)
    return (total, up_sum[None], down_sum[None])


def solution(mesh):
    in_specs = (
        P(None, ("dp", "expert"), None),
        P(None, ("dp", "expert"), None),
        P(None, ("dp", "expert"), None),
        P(),
        P("expert", None, None),
        P("expert", None, None),
    )
    out_specs = (P(("dp", "expert"), None), P("expert", "dp", None), P("expert", "dp", None))
    return jax.shard_map(body, mesh=mesh, in_specs=in_specs, out_specs=out_specs, check_vma=False)
```

profile of v0, /device:TPU:0, one launch (start us, length us, event | category | flops | bytes accessed | tf_op | source)
XLA Modules:
  0.0 78.2 jit_solution(7512948492004434116)
XLA Ops:
  0.6 2.7 %shard_map.85 = (bf16[16,1024]{1,0:T(8,128)(2,1)}, bf16[16,1024]{1,0:T(8,128)(2,1)}, bf16[64,1024]{1,0:T(8,128)(2,1)}, bf16[64,1024]{1,0:T(8,128)(2,1)}, bf16[64...) custom-call(s32[1]{0:T(128)} %bitcast.me_ref, ...), custom_call_target="tpu_custom_call" | custom-call | tf_op jit(solution)/shard_map/pallas_call | solution.py:84
  3.9 2.6 %collective-permute-start = (bf16[64,1024]{1,0:T(8,128)(2,1)}, bf16[64,1024]{1,0:T(8,128)(2,1)S(1)}, u32[]{:S(2)}, u32[]{:S(2)}) collective-permute-start(bf16[64,1024]{1,0:T(8,128)(2,1)} %get-tuple-element.70), channel_id=1, source_target_pairs={{0,3},{1,2},{2,1},{3,0},{4,7},{5,6},{6,5},{7,4},{8,11},{9,10},{10,... | collective-permute-start | bytes 393224 | tf_op jit(solution)/shard_map/ppermute | solution.py:22
  6.5 4.1 %collective-permute-start.3 = (bf16[16,2048]{1,0:T(8,128)(2,1)}, bf16[16,2048]{1,0:T(8,128)(2,1)S(1)}, u32[]{:S(2)}, u32[]{:S(2)}) collective-permute-start(bf16[16,2048]{1,0:T(8,128)(2,1)} %get-tuple-element.77), channel_id=1, source_target_pairs={{0,12},{1,13},{2,14},{3,15},{4,8},{5,9},{6,10},{7,11},{8,4},{9,5},... | collective-permute-start | bytes 196616 | tf_op jit(solution)/shard_map/ppermute | solution.py:22
  11.2 2.3 %collective-permute-done.1 = bf16[64,1024]{1,0:T(8,128)(2,1)S(1)} collective-permute-done((bf16[64,1024]{1,0:T(8,128)(2,1)}, bf16[64,1024]{1,0:T(8,128)(2,1)S(1)}, u32[]{:S(2)}, u32[]{:S(2)}) %collective-permute-start.1) | collective-permute-done | bytes 131104 | tf_op jit(solution)/shard_map/ppermute | solution.py:22
  13.5 2.8 %collective-permute-done.4 = bf16[16,2048]{1,0:T(8,128)(2,1)S(1)} collective-permute-done((bf16[16,2048]{1,0:T(8,128)(2,1)}, bf16[16,2048]{1,0:T(8,128)(2,1)S(1)}, u32[]{:S(2)}, u32[]{:S(2)}) %collective-permute-start.4) | collective-permute-done | bytes 65568 | tf_op jit(solution)/shard_map/ppermute | solution.py:22
  21.2 1.6 %collective-permute-start.12 = (bf16[64,1024]{1,0:T(8,128)(2,1)S(1)}, bf16[64,1024]{1,0:T(8,128)(2,1)}, u32[]{:S(2)}, u32[]{:S(2)}) collective-permute-start(bf16[64,1024]{1,0:T(8,128)(2,1)S(1)} %pad_maximum_fusion.6), channel_id=1, source_target_pairs={{0,16},{16,0},{1,17},{17,1},{2,18},{18,2},{3,19},{19,3},{4,20},{20... | collective-permute-start | bytes 393224 | tf_op jit(solution)/shard_map/ppermute | solution.py:104
  22.8 2.7 %collective-permute-start.6 = (bf16[48,1024]{1,0:T(8,128)(2,1)}, bf16[48,1024]{1,0:T(8,128)(2,1)S(1)}, u32[]{:S(2)}, u32[]{:S(2)}) collective-permute-start(bf16[48,1024]{1,0:T(8,128)(2,1)} %pad_maximum_fusion.8), channel_id=1, source_target_pairs={{0,12},{1,13},{2,14},{3,15},{4,8},{5,9},{6,10},{7,11},{8,4},{9,5},... | collective-permute-start | bytes 294920 | tf_op jit(solution)/shard_map/ppermute | solution.py:22
  25.5 1.5 %collective-permute-start.7 = (bf16[48,1024]{1,0:T(8,128)(2,1)}, bf16[48,1024]{1,0:T(8,128)(2,1)S(1)}, u32[]{:S(2)}, u32[]{:S(2)}) collective-permute-start(bf16[48,1024]{1,0:T(8,128)(2,1)} %pad_maximum_fusion.9), channel_id=1, source_target_pairs={{0,8},{1,9},{2,10},{3,11},{4,12},{5,13},{6,14},{7,15},{8,0},{9,1},... | collective-permute-start | bytes 294920 | tf_op jit(solution)/shard_map/ppermute | solution.py:22
  29.3 1.5 %collective-permute-start.13 = (bf16[48,2048]{1,0:T(8,128)(2,1)S(1)}, bf16[48,2048]{1,0:T(8,128)(2,1)S(1)}, u32[]{:S(2)}, u32[]{:S(2)}) collective-permute-start(bf16[48,2048]{1,0:T(8,128)(2,1)S(1)} %pad_maximum_fusion.5), channel_id=1, source_target_pairs={{0,16},{16,0},{1,17},{17,1},{2,18},{18,2},{3,19},{19,3},{4,20},{20... | collective-permute-start | bytes 589832 | tf_op jit(solution)/shard_map/ppermute | solution.py:104
  31.5 2.1 %collective-permute-start.16 = (bf16[48,1024]{1,0:T(8,128)(2,1)S(1)}, bf16[48,1024]{1,0:T(8,128)(2,1)S(1)}, u32[]{:S(2)}, u32[]{:S(2)}) collective-permute-start(bf16[48,1024]{1,0:T(8,128)(2,1)S(1)} %pad_maximum_fusion.11), channel_id=1, source_target_pairs={{0,12},{1,13},{2,14},{3,15},{4,8},{5,9},{6,10},{7,11},{8,4},{9,5},... | collective-permute-start | bytes 294920 | tf_op jit(solution)/shard_map/ppermute | solution.py:22
  33.6 1.5 %collective-permute-done.7 = bf16[48,1024]{1,0:T(8,128)(2,1)S(1)} collective-permute-done((bf16[48,1024]{1,0:T(8,128)(2,1)}, bf16[48,1024]{1,0:T(8,128)(2,1)S(1)}, u32[]{:S(2)}, u32[]{:S(2)}) %collective-permute-start.7) | collective-permute-done | bytes 98336 | tf_op jit(solution)/shard_map/ppermute | solution.py:22
  35.1 2.1 %collective-permute-start.18 = (bf16[48,1024]{1,0:T(8,128)(2,1)S(1)}, bf16[48,1024]{1,0:T(8,128)(2,1)S(1)}, u32[]{:S(2)}, u32[]{:S(2)}) collective-permute-start(bf16[48,1024]{1,0:T(8,128)(2,1)S(1)} %pad_maximum_fusion.13), channel_id=1, source_target_pairs={{0,4},{1,5},{2,6},{3,7},{4,0},{5,1},{6,2},{7,3},{8,12},{9,13},{10,... | collective-permute-start | bytes 294920 | tf_op jit(solution)/shard_map/ppermute | solution.py:22
  38.7 1.6 %collective-permute-start.15 = (bf16[144,1024]{1,0:T(8,128)(2,1)S(1)}, bf16[144,1024]{1,0:T(8,128)(2,1)S(1)}, u32[]{:S(2)}, u32[]{:S(2)}) collective-permute-start(bf16[144,1024]{1,0:T(8,128)(2,1)S(1)} %pad_maximum_fusion.3), channel_id=1, source_target_pairs={{0,16},{16,0},{1,17},{17,1},{2,18},{18,2},{3,19},{19,3},{4,20},{20... | collective-permute-start | bytes 884744 | tf_op jit(solution)/shard_map/ppermute | solution.py:104
  42.5 1.8 %add_multiply_fusion = (f32[256,2048]{1,0:T(8,128)S(1)}, bf16[256,2048]{1,0:T(8,128)(2,1)S(1)}) fusion(bf16[256,1024]{1,0:T(8,128)(2,1)S(1)} %multiply_convert_fusion.5, bf16[1,1024,2048]{2,1,0:T(8,128)(2,1)S(1)} %copy-done.3), kind=kOutput, calls=%fused_computation.28 | convolution fusion | flops 1078460416 | bytes 7864320 | tf_op jit(solution)/shard_map/dot_general | solution.py:113
  48.5 2.0 %multiply_reduce_fusion.1 = (f32[256]{0:T(256)S(1)}, f32[256,1024]{1,0:T(8,128)S(1)}, f32[256,1024]{1,0:T(8,128)S(1)}) fusion(bf16[144,1024]{1,0:T(8,128)(2,1)S(1)} %collective-permute-done.15, bf16[48,1024]{1,0:T(8,128)(2,1)S(1)} %get-tuple-element.150, bf16[64,1024]{1,0:T(8,128)(2,1)} %collective-permute-done.12, bf16[1024,1024]{1,0:T(8,128)(2,1)S(1)} %copy-done), kind=kOutput, calls=%fused_computation.43 | convolution fusion | flops 541851392 | bytes 4719616 | tf_op jit(solution)/shard_map/dot_general | solution.py:108
  50.7 1.5 %multiply_convert_fusion = (bf16[256,2048]{1,0:T(8,128)(2,1)S(1)}, f32[256,2048]{1,0:T(8,128)S(1)}) fusion(bf16[256,1024]{1,0:T(8,128)(2,1)S(1)} %multiply_convert_fusion.3, bf16[1,1024,2048]{2,1,0:T(8,128)(2,1)S(1)} %copy-done.3), kind=kOutput, calls=%fused_computation.26 | convolution fusion | flops 1076363264 | bytes 7864320 | tf_op jit(solution)/shard_map/dot_general | solution.py:113
  53.6 1.5 %fusion.20 = bf16[256,2048]{1,0:T(8,128)(2,1)S(1)} fusion(bf16[1,1024,2048]{2,1,0:T(8,128)(2,1)S(1)} %copy-done.1, f32[256,2048]{1,0:T(8,128)S(1)} %get-tuple-element.188, bf16[144,1024]{1,0:T(8,128)(2,1)S(1)} %collective-permute-done.19, bf16[48,1024]{1,0:T(8,128)(2,1)S(1)} %get-tuple-element.149, bf16[64,1024]{1,0:T(8,128)(2,1)S(1)} %collective-permute-done.14), kind=kOutput, calls=%fused_computation.18 | convolution fusion | flops 1080033280 | bytes 7864320 | tf_op jit(solution)/shard_map/dot_general | solution.py:188
  55.1 1.6 %multiply_reduce_fusion = (f32[256]{0:T(256)S(1)}, f32[256,1024]{1,0:T(8,128)S(1)}) fusion(f32[256,1024]{1,0:T(8,128)S(1)} %get-tuple-element.140, bf16[256,2048]{1,0:T(8,128)(2,1)S(1)} %fusion.20, bf16[1,1024,2048]{2,1,0:T(8,128)(2,1)S(1)} %copy-done.3), kind=kOutput, calls=%fused_computation.41 | convolution fusion | flops 1074265856 | bytes 7341056 | tf_op jit(solution)/shard_map/dot_general | solution.py:190
  61.6 2.6 %fusion.18 = bf16[1,512,2048]{2,1,0:T(8,128)(2,1)} fusion(bf16[256,2048]{1,0:T(8,128)(2,1)S(1)} %fusion.20, bf16[256,2048]{1,0:T(8,128)(2,1)S(1)} %fusion.23, bf16[256,512]{1,0:T(8,128)(2,1)S(1)} %constant_dynamic-slice_fusion.2, bf16[256,512]{1,0:T(8,128)(2,1)S(1)} %constant_dynamic-slice_fusion.3), kind=kOutput, calls=%fused_computation.16 | convolution fusion | flops 1080033280 | bytes 4718592 | tf_op jit(solution)/shard_map/dot_general | solution.py:243
  64.2 4.5 %collective-permute-done.21 = bf16[128,1024]{1,0:T(8,128)(2,1)S(1)} collective-permute-done((bf16[128,1024]{1,0:T(8,128)(2,1)S(1)}, bf16[128,1024]{1,0:T(8,128)(2,1)S(1)}, u32[]{:S(2)}, u32[]{:S(2)}) %collective-permute-start.21) | collective-permute-done | bytes 262176 | tf_op jit(solution)/shard_map/ppermute | solution.py:22
  68.8 2.1 %collective-permute-start.24 = (bf16[32,1024]{1,0:T(8,128)(2,1)S(1)}, bf16[32,1024]{1,0:T(8,128)(2,1)S(1)}, u32[]{:S(2)}, u32[]{:S(2)}) collective-permute-start(bf16[32,1024]{1,0:T(8,128)(2,1)S(1)} %get-tuple-element.147), channel_id=1, source_target_pairs={{0,12},{1,13},{2,14},{3,15},{4,8},{5,9},{6,10},{7,11},{8,4},{9,5},... | collective-permute-start | bytes 196616 | tf_op jit(solution)/shard_map/ppermute | solution.py:22
  71.2 2.0 %collective-permute-start.22 = (bf16[32,1024]{1,0:T(8,128)(2,1)S(1)}, bf16[32,1024]{1,0:T(8,128)(2,1)S(1)}, u32[]{:S(2)}, u32[]{:S(2)}) collective-permute-start(bf16[32,1024]{1,0:T(8,128)(2,1)S(1)} %get-tuple-element.146), channel_id=1, source_target_pairs={{0,4},{1,5},{2,6},{3,7},{4,0},{5,1},{6,2},{7,3},{8,12},{9,13},{10,... | collective-permute-start | bytes 196616 | tf_op jit(solution)/shard_map/ppermute | solution.py:22
  73.3 2.6 %fusion.19 = bf16[1,512,2048]{2,1,0:T(8,128)(2,1)} fusion(bf16[256,2048]{1,0:T(8,128)(2,1)S(1)} %get-tuple-element.187, bf16[256,2048]{1,0:T(8,128)(2,1)S(1)} %get-tuple-element.136, bf16[256,512]{1,0:T(8,128)(2,1)S(1)} %constant_dynamic-slice_fusion, bf16[256,512]{1,0:T(8,128)(2,1)S(1)} %constant_dynamic-slice_fusion.1), kind=kOutput, calls=%fused_computation.17 | convolution fusion | flops 1080033280 | bytes 4718592 | tf_op jit(solution)/shard_map/dot_general | solution.py:243
  75.9 1.6 %collective-permute-done.23 = bf16[32,1024]{1,0:T(8,128)(2,1)S(1)} collective-permute-done((bf16[32,1024]{1,0:T(8,128)(2,1)S(1)}, bf16[32,1024]{1,0:T(8,128)(2,1)S(1)}, u32[]{:S(2)}, u32[]{:S(2)}) %collective-permute-start.23) | collective-permute-done | bytes 65568 | tf_op jit(solution)/shard_map/ppermute | solution.py:22
  (89 shorter events, 24.3 us)
Async XLA Ops:
  3.4 3.1 %collective-permute-start.2 = (bf16[64,1024]{1,0:T(8,128)(2,1)}, bf16[64,1024]{1,0:T(8,128)(2,1)S(1)}, u32[]{:S(2)}, u32[]{:S(2)}) collective-permute-start(bf16[64,1024]{1,0:T(8,128)(2,1)} %get-tuple-element.75), channel_id=1, source_target_pairs={{0,1},{1,0},{2,3},{3,2},{4,5},{5,4},{6,7},{7,6},{8,9},{9,8},{10,11... | collective-permute-start | bytes 393224 | tf_op jit(solution)/shard_map/ppermute | solution.py:22
  3.9 7.3 %collective-permute-start = (bf16[64,1024]{1,0:T(8,128)(2,1)}, bf16[64,1024]{1,0:T(8,128)(2,1)S(1)}, u32[]{:S(2)}, u32[]{:S(2)}) collective-permute-start(bf16[64,1024]{1,0:T(8,128)(2,1)} %get-tuple-element.70), channel_id=1, source_target_pairs={{0,3},{1,2},{2,1},{3,0},{4,7},{5,6},{6,5},{7,4},{8,11},{9,10},{10,... | collective-permute-start | bytes 393224 | tf_op jit(solution)/shard_map/ppermute | solution.py:22
  6.5 7.1 %collective-permute-start.1 = (bf16[64,1024]{1,0:T(8,128)(2,1)}, bf16[64,1024]{1,0:T(8,128)(2,1)S(1)}, u32[]{:S(2)}, u32[]{:S(2)}) collective-permute-start(bf16[64,1024]{1,0:T(8,128)(2,1)} %get-tuple-element.71), channel_id=1, source_target_pairs={{0,2},{1,3},{2,0},{3,1},{4,6},{5,7},{6,4},{7,5},{8,10},{9,11},{10,... | collective-permute-start | bytes 393224 | tf_op jit(solution)/shard_map/ppermute | solution.py:22
  6.5 7.0 %collective-permute-start.3 = (bf16[16,2048]{1,0:T(8,128)(2,1)}, bf16[16,2048]{1,0:T(8,128)(2,1)S(1)}, u32[]{:S(2)}, u32[]{:S(2)}) collective-permute-start(bf16[16,2048]{1,0:T(8,128)(2,1)} %get-tuple-element.77), channel_id=1, source_target_pairs={{0,12},{1,13},{2,14},{3,15},{4,8},{5,9},{6,10},{7,11},{8,4},{9,5},... | collective-permute-start | bytes 196616 | tf_op jit(solution)/shard_map/ppermute | solution.py:22
  10.6 5.8 %collective-permute-start.4 = (bf16[16,2048]{1,0:T(8,128)(2,1)}, bf16[16,2048]{1,0:T(8,128)(2,1)S(1)}, u32[]{:S(2)}, u32[]{:S(2)}) collective-permute-start(bf16[16,2048]{1,0:T(8,128)(2,1)} %get-tuple-element.78), channel_id=1, source_target_pairs={{0,8},{1,9},{2,10},{3,11},{4,12},{5,13},{6,14},{7,15},{8,0},{9,1},... | collective-permute-start | bytes 196616 | tf_op jit(solution)/shard_map/ppermute | solution.py:22
  10.6 5.8 %collective-permute-start.5 = (bf16[16,2048]{1,0:T(8,128)(2,1)}, bf16[16,2048]{1,0:T(8,128)(2,1)S(1)}, u32[]{:S(2)}, u32[]{:S(2)}) collective-permute-start(bf16[16,2048]{1,0:T(8,128)(2,1)} %get-tuple-element.79), channel_id=1, source_target_pairs={{0,4},{1,5},{2,6},{3,7},{4,0},{5,1},{6,2},{7,3},{8,12},{9,13},{10,... | collective-permute-start | bytes 196616 | tf_op jit(solution)/shard_map/ppermute | solution.py:22
  19.3 6.2 %collective-permute-start.9 = (bf16[64,1024]{1,0:T(8,128)(2,1)}, bf16[64,1024]{1,0:T(8,128)(2,1)S(1)}, u32[]{:S(2)}, u32[]{:S(2)}) collective-permute-start(bf16[64,1024]{1,0:T(8,128)(2,1)} %get-tuple-element.98), channel_id=1, source_target_pairs={{0,3},{1,2},{2,1},{3,0},{4,7},{5,6},{6,5},{7,4},{8,11},{9,10},{10,... | collective-permute-start | bytes 393224 | tf_op jit(solution)/shard_map/ppermute | solution.py:22
  20.2 7.9 %collective-permute-start.10 = (bf16[64,1024]{1,0:T(8,128)(2,1)}, bf16[64,1024]{1,0:T(8,128)(2,1)S(1)}, u32[]{:S(2)}, u32[]{:S(2)}) collective-permute-start(bf16[64,1024]{1,0:T(8,128)(2,1)} %get-tuple-element.99), channel_id=1, source_target_pairs={{0,2},{1,3},{2,0},{3,1},{4,6},{5,7},{6,4},{7,5},{8,10},{9,11},{10,... | collective-permute-start | bytes 393224 | tf_op jit(solution)/shard_map/ppermute | solution.py:22
  21.0 8.3 %collective-permute-start.11 = (bf16[64,1024]{1,0:T(8,128)(2,1)}, bf16[64,1024]{1,0:T(8,128)(2,1)S(1)}, u32[]{:S(2)}, u32[]{:S(2)}) collective-permute-start(bf16[64,1024]{1,0:T(8,128)(2,1)} %get-tuple-element.100), channel_id=1, source_target_pairs={{0,1},{1,0},{2,3},{3,2},{4,5},{5,4},{6,7},{7,6},{8,9},{9,8},{10,11... | collective-permute-start | bytes 393224 | tf_op jit(solution)/shard_map/ppermute | solution.py:22
  21.2 9.6 %collective-permute-start.12 = (bf16[64,1024]{1,0:T(8,128)(2,1)S(1)}, bf16[64,1024]{1,0:T(8,128)(2,1)}, u32[]{:S(2)}, u32[]{:S(2)}) collective-permute-start(bf16[64,1024]{1,0:T(8,128)(2,1)S(1)} %pad_maximum_fusion.6), channel_id=1, source_target_pairs={{0,16},{16,0},{1,17},{17,1},{2,18},{18,2},{3,19},{19,3},{4,20},{20... | collective-permute-start | bytes 393224 | tf_op jit(solution)/shard_map/ppermute | solution.py:104
  22.8 8.7 %collective-permute-start.6 = (bf16[48,1024]{1,0:T(8,128)(2,1)}, bf16[48,1024]{1,0:T(8,128)(2,1)S(1)}, u32[]{:S(2)}, u32[]{:S(2)}) collective-permute-start(bf16[48,1024]{1,0:T(8,128)(2,1)} %pad_maximum_fusion.8), channel_id=1, source_target_pairs={{0,12},{1,13},{2,14},{3,15},{4,8},{5,9},{6,10},{7,11},{8,4},{9,5},... | collective-permute-start | bytes 294920 | tf_op jit(solution)/shard_map/ppermute | solution.py:22
  25.5 9.7 %collective-permute-start.7 = (bf16[48,1024]{1,0:T(8,128)(2,1)}, bf16[48,1024]{1,0:T(8,128)(2,1)S(1)}, u32[]{:S(2)}, u32[]{:S(2)}) collective-permute-start(bf16[48,1024]{1,0:T(8,128)(2,1)} %pad_maximum_fusion.9), channel_id=1, source_target_pairs={{0,8},{1,9},{2,10},{3,11},{4,12},{5,13},{6,14},{7,15},{8,0},{9,1},... | collective-permute-start | bytes 294920 | tf_op jit(solution)/shard_map/ppermute | solution.py:22
  28.2 7.0 %collective-permute-start.8 = (bf16[48,1024]{1,0:T(8,128)(2,1)S(1)}, bf16[48,1024]{1,0:T(8,128)(2,1)S(1)}, u32[]{:S(2)}, u32[]{:S(2)}) collective-permute-start(bf16[48,1024]{1,0:T(8,128)(2,1)S(1)} %pad_maximum_fusion.10), channel_id=1, source_target_pairs={{0,4},{1,5},{2,6},{3,7},{4,0},{5,1},{6,2},{7,3},{8,12},{9,13},{10,... | collective-permute-start | bytes 294920 | tf_op jit(solution)/shard_map/ppermute | solution.py:22
  29.3 7.9 %collective-permute-start.13 = (bf16[48,2048]{1,0:T(8,128)(2,1)S(1)}, bf16[48,2048]{1,0:T(8,128)(2,1)S(1)}, u32[]{:S(2)}, u32[]{:S(2)}) collective-permute-start(bf16[48,2048]{1,0:T(8,128)(2,1)S(1)} %pad_maximum_fusion.5), channel_id=1, source_target_pairs={{0,16},{16,0},{1,17},{17,1},{2,18},{18,2},{3,19},{19,3},{4,20},{20... | collective-permute-start | bytes 589832 | tf_op jit(solution)/shard_map/ppermute | solution.py:104
  30.9 7.8 %collective-permute-start.14 = (bf16[64,1024]{1,0:T(8,128)(2,1)S(1)}, bf16[64,1024]{1,0:T(8,128)(2,1)S(1)}, u32[]{:S(2)}, u32[]{:S(2)}) collective-permute-start(bf16[64,1024]{1,0:T(8,128)(2,1)S(1)} %pad_maximum_fusion.7), channel_id=1, source_target_pairs={{0,16},{16,0},{1,17},{17,1},{2,18},{18,2},{3,19},{19,3},{4,20},{20... | collective-permute-start | bytes 393224 | tf_op jit(solution)/shard_map/ppermute | solution.py:104
  31.5 13.3 %collective-permute-start.16 = (bf16[48,1024]{1,0:T(8,128)(2,1)S(1)}, bf16[48,1024]{1,0:T(8,128)(2,1)S(1)}, u32[]{:S(2)}, u32[]{:S(2)}) collective-permute-start(bf16[48,1024]{1,0:T(8,128)(2,1)S(1)} %pad_maximum_fusion.11), channel_id=1, source_target_pairs={{0,12},{1,13},{2,14},{3,15},{4,8},{5,9},{6,10},{7,11},{8,4},{9,5},... | collective-permute-start | bytes 294920 | tf_op jit(solution)/shard_map/ppermute | solution.py:22
  35.1 9.7 %collective-permute-start.17 = (bf16[48,1024]{1,0:T(8,128)(2,1)S(1)}, bf16[48,1024]{1,0:T(8,128)(2,1)S(1)}, u32[]{:S(2)}, u32[]{:S(2)}) collective-permute-start(bf16[48,1024]{1,0:T(8,128)(2,1)S(1)} %pad_maximum_fusion.12), channel_id=1, source_target_pairs={{0,8},{1,9},{2,10},{3,11},{4,12},{5,13},{6,14},{7,15},{8,0},{9,1},... | collective-permute-start | bytes 294920 | tf_op jit(solution)/shard_map/ppermute | solution.py:22
  35.1 9.7 %collective-permute-start.18 = (bf16[48,1024]{1,0:T(8,128)(2,1)S(1)}, bf16[48,1024]{1,0:T(8,128)(2,1)S(1)}, u32[]{:S(2)}, u32[]{:S(2)}) collective-permute-start(bf16[48,1024]{1,0:T(8,128)(2,1)S(1)} %pad_maximum_fusion.13), channel_id=1, source_target_pairs={{0,4},{1,5},{2,6},{3,7},{4,0},{5,1},{6,2},{7,3},{8,12},{9,13},{10,... | collective-permute-start | bytes 294920 | tf_op jit(solution)/shard_map/ppermute | solution.py:22
  38.7 9.8 %collective-permute-start.15 = (bf16[144,1024]{1,0:T(8,128)(2,1)S(1)}, bf16[144,1024]{1,0:T(8,128)(2,1)S(1)}, u32[]{:S(2)}, u32[]{:S(2)}) collective-permute-start(bf16[144,1024]{1,0:T(8,128)(2,1)S(1)} %pad_maximum_fusion.3), channel_id=1, source_target_pairs={{0,16},{16,0},{1,17},{17,1},{2,18},{18,2},{3,19},{19,3},{4,20},{20... | collective-permute-start | bytes 884744 | tf_op jit(solution)/shard_map/ppermute | solution.py:104
  44.9 8.8 %collective-permute-start.19 = (bf16[144,1024]{1,0:T(8,128)(2,1)S(1)}, bf16[144,1024]{1,0:T(8,128)(2,1)S(1)}, u32[]{:S(2)}, u32[]{:S(2)}) collective-permute-start(bf16[144,1024]{1,0:T(8,128)(2,1)S(1)} %pad_maximum_fusion.4), channel_id=1, source_target_pairs={{0,16},{16,0},{1,17},{17,1},{2,18},{18,2},{3,19},{19,3},{4,20},{20... | collective-permute-start | bytes 884744 | tf_op jit(solution)/shard_map/ppermute | solution.py:104
  60.3 8.4 %collective-permute-start.21 = (bf16[128,1024]{1,0:T(8,128)(2,1)S(1)}, bf16[128,1024]{1,0:T(8,128)(2,1)S(1)}, u32[]{:S(2)}, u32[]{:S(2)}) collective-permute-start(bf16[128,1024]{1,0:T(8,128)(2,1)S(1)} %slice.180), channel_id=1, source_target_pairs={{0,2},{1,3},{2,0},{3,1},{4,6},{5,7},{6,4},{7,5},{8,10},{9,11},{10,... | collective-permute-start | bytes 786440 | tf_op jit(solution)/shard_map/ppermute | solution.py:22
  68.8 7.1 %collective-permute-start.24 = (bf16[32,1024]{1,0:T(8,128)(2,1)S(1)}, bf16[32,1024]{1,0:T(8,128)(2,1)S(1)}, u32[]{:S(2)}, u32[]{:S(2)}) collective-permute-start(bf16[32,1024]{1,0:T(8,128)(2,1)S(1)} %get-tuple-element.147), channel_id=1, source_target_pairs={{0,12},{1,13},{2,14},{3,15},{4,8},{5,9},{6,10},{7,11},{8,4},{9,5},... | collective-permute-start | bytes 196616 | tf_op jit(solution)/shard_map/ppermute | solution.py:22
  70.9 6.6 %collective-permute-start.23 = (bf16[32,1024]{1,0:T(8,128)(2,1)S(1)}, bf16[32,1024]{1,0:T(8,128)(2,1)S(1)}, u32[]{:S(2)}, u32[]{:S(2)}) collective-permute-start(bf16[32,1024]{1,0:T(8,128)(2,1)S(1)} %get-tuple-element.148), channel_id=1, source_target_pairs={{0,8},{1,9},{2,10},{3,11},{4,12},{5,13},{6,14},{7,15},{8,0},{9,1},... | collective-permute-start | bytes 196616 | tf_op jit(solution)/shard_map/ppermute | solution.py:22
  71.2 6.2 %collective-permute-start.22 = (bf16[32,1024]{1,0:T(8,128)(2,1)S(1)}, bf16[32,1024]{1,0:T(8,128)(2,1)S(1)}, u32[]{:S(2)}, u32[]{:S(2)}) collective-permute-start(bf16[32,1024]{1,0:T(8,128)(2,1)S(1)} %get-tuple-element.146), channel_id=1, source_target_pairs={{0,4},{1,5},{2,6},{3,7},{4,0},{5,1},{6,2},{7,3},{8,12},{9,13},{10,... | collective-permute-start | bytes 196616 | tf_op jit(solution)/shard_map/ppermute | solution.py:22
  (5 other events, 74.3 us)
where the time goes:
time: 78.5 us; the launch traced here: 78.2 us
  starting transfers between devices  30.7 us (39%)
  matrix products  20.6 us (26%)
  waiting for transfers between devices  17 us (22%)
  other arithmetic  4.1 us (5%)
  Pallas kernels  2.74 us (3%)
  local copies, waits for them, and re-layouts  1.97 us (3%)
  between operations  1 us (1%)
    ppermute x20, starting transfers between devices, swap(): return lax.ppermute(piece, 'expert', pairs)  24.9 us
    ppermute x20, waiting for transfers between devices, swap(): return lax.ppermute(piece, 'expert', pairs)  15.5 us
    ppermute x5, starting transfers between devices, copies(): pieces.append(lax.ppermute(rows, 'dp', ring))  5.8 us
    dot_general x2, matrix products, rows_product(): lax.dot_general(jnp.concatenate(left, axis=0), jnp.concatenate(right, axi...  5.22 us
    dot_general x2, matrix products, forward(): pre_exp = jnp.dot(norm_rows, w_up, preferred_element_type=jnp.float32)  3.27 us
    dot_general x2, matrix products, forward(): pre_enc = jnp.dot(features, enc_weight, preferred_element_type=jnp.float32)  3.12 us
    dot_general x2, matrix products, backward(): lax.dot_general(pre_grad, w_up, contract_last, preferred_element_type=jnp...  2.96 us
    dot_general x2, matrix products, backward(): act_grad = jnp.dot(grad_rows, w_down, preferred_element_type=jnp.float32)  2.78 us
  transfers between devices with their start and end apart: 25, of which 8 were waited for; matrix products, arithmetic and copies ran while one was open for 22% of the time, Pallas kernels for 0%

commit v1 on v0

--- a/solution.py
+++ b/solution.py
@@ -22,7 +22,7 @@
     return lax.ppermute(piece, "expert", pairs)
 
 
-def place_kernel(experts, low, high, capacity, me_ref, ids_ref, *refs):
+def place_kernel(experts, low, high, capacity, direct_steps, me_ref, ids_ref, *refs):
     rows_refs, here_refs, refs = refs[:2], refs[2:4], refs[4:]
     near_refs, direct_refs, placer_ref = refs[: 2 * (low - 1)], refs[2 * (low - 1) : -1], refs[-1]
     batches, rows = ids_ref.shape
@@ -52,9 +52,9 @@
         placed = jnp.dot(
             placer_ref[...], rows_refs[kind][...], preferred_element_type=jnp.float32
         ).astype(jnp.bfloat16)
-        here_refs[kind][...] = placed[:bucket]
-        for step in range(1, high):
-            direct_refs[step - 1][:, kind * width : (kind + 1) * width] = placed[
+        here_refs[kind][...] = placed[:piece]
+        for direct_ref, step in zip(direct_refs, direct_steps):
+            direct_ref[:, kind * width : (kind + 1) * width] = placed[
                 step * bucket : (step + 1) * bucket
             ]
         for step in range(1, low):
@@ -79,10 +79,11 @@
     fence = lax.optimization_barrier
 
     vmem = pl.BlockSpec(memory_space=pltpu.VMEM)
-    shapes = [(bucket, model_width)] * 2 + [(high * bucket, model_width)] * (2 * (low - 1))
-    shapes += [(bucket, 2 * model_width)] * (high - 1)
+    direct_steps = sorted({1, high - 1}, reverse=True)
+    shapes = [(high * bucket, model_width)] * (2 * low)
+    shapes += [(bucket, 2 * model_width)] * len(direct_steps)
     placed = pl.pallas_call(
-        functools.partial(place_kernel, experts, low, high, capacity),
+        functools.partial(place_kernel, experts, low, high, capacity, direct_steps),
         out_shape=[jax.ShapeDtypeStruct(shape, jnp.bfloat16) for shape in shapes],
         in_specs=[pl.BlockSpec(memory_space=pltpu.SMEM), vmem, vmem, vmem],
         out_specs=[vmem] * len(shapes),
@@ -120,9 +121,14 @@
     def send_near(pieces):
         return [swap(pieces[step - 1], step) for step in range(low - 1, 0, -1)]
 
-    def far_pieces(near):
+    def far_pieces(own, near):
         return [
-            stack(*[piece[step * bucket : (step + 1) * bucket] for piece in near])
+            stack(
+                *[
+                    piece[step * bucket : (step + 1) * bucket]
+                    for piece in (near if step in direct_steps else [own] + near)
+                ]
+            )
             for step in range(high - 1, 0, -1)
         ]
 
@@ -130,17 +136,17 @@
         return [swap(piece, step * low) for piece, step in zip(pieces, range(high - 1, 0, -1))]
 
     def here_and_near(own, near):
-        return stack(own, *[piece[:bucket] for piece in near])
+        return stack(*[piece[:bucket] for piece in [own] + near])
 
     cells_near = send_near(cells_placed)
     direct_placed, cells_near[-1] = fence((direct_placed, cells_near[-1]))
-    direct = [swap(direct_placed[step - 1], step * low) for step in range(high - 1, 0, -1)]
+    direct = [swap(piece, step * low) for piece, step in zip(direct_placed, direct_steps)]
     cells_near, direct, here, grads_placed = fence((cells_near, direct, here, grads_placed))
     cells_first, direct, cells_far, grads_placed = fence(
         (
             here_and_near(here[0], cells_near),
             stack(*direct),
-            far_pieces(cells_near),
+            far_pieces(here[0], cells_near),
             grads_placed,
         )
     )
@@ -151,14 +157,18 @@
     grads_near, cells_first_copies = fence((grads_near, cells_first_copies))
     grads_first = here_and_near(here[1], grads_near)
     grads_first_copies = copies(grads_first)
-    grads_far = send_far(far_pieces(grads_near))
+    grads_far = send_far(far_pieces(here[1], grads_near))
     came = (cells_first_copies, direct_copies, grads_first_copies)
     cells_far, came = fence((cells_far, came))
     cells_far, came = fence((stack(*cells_far), came))
     cells_far_copies = copies(cells_far)
     features = stack(cells_first, direct[:, :model_width], cells_far)
-    grads_far, own_forward = fence((grads_far, forward(features)))
-    grads_far, own_forward = fence((stack(*grads_far), own_forward))
+    early = [
+        (stack(cells, both[:, :model_width]), stack(grads, both[:, model_width:]))
+        for cells, both, grads in zip(*came)
+    ]
+    grads_far, early, own_forward = fence((grads_far, early, forward(features)))
+    grads_far, early, own_forward = fence((stack(*grads_far), early, own_forward))
     grads_far_copies = copies(grads_far)
 
     share = model_width // dp_count
@@ -203,12 +213,11 @@
 
     backward(features, stack(grads_first, direct[:, model_width:], grads_far), own_forward)
     cells_far_copies, enc_parts[0] = fence((cells_far_copies, enc_parts[0]))
-    for cells_first, direct, grads_first, cells_far, grads_far in zip(
-        *came, cells_far_copies, grads_far_copies
+    for (cells_early, grads_early), cells_far, grads_far in zip(
+        early, cells_far_copies, grads_far_copies
     ):
-        features = stack(cells_first, direct[:, :model_width], cells_far)
-        grad_rows = stack(grads_first, direct[:, model_width:], grads_far)
-        backward(features, grad_rows, forward(features))
+        features = stack(cells_early, cells_far)
+        backward(features, stack(grads_early, grads_far), forward(features))
 
     def enc_terms(first, last):
         total = None

time: 78.5 us -> 77.4 us (0.986)
  starting transfers between devices: 30.7 us -> 32.7 us
  matrix products: 20.6 us -> 18.8 us
  local copies, waits for them, and re-layouts: 1.97 us -> 3.55 us
  other arithmetic: 4.1 us -> 2.55 us
  waiting for transfers between devices: 17 us -> 15.7 us
    ppermute x20 -> x19, starting transfers between devices: 24.9 us -> 27 us  [swap(): return lax.ppermute(piece, 'expert', pairs)]
    concatenate x12 -> x13, other arithmetic: 2.2 us -> 0.17 us  [stack(): return jnp.concatenate(pieces, axis=0)]
    unnamed x12 -> x21, local copies, waits for them, and re-layouts: 1 us -> 2.51 us
    ppermute x5, waiting for transfers between devices: 1.47 us -> 0.28 us  [copies(): pieces.append(lax.ppermute(rows, 'dp', ring))]
    dot_general x2, matrix products: 3.12 us -> 2.13 us  [forward(): pre_enc = jnp.dot(features, enc_weight, preferred_element_type=jnp.float32)]
    dot_general x2, matrix products: 2 us -> 1.09 us  [backward(): jnp.dot(features, picker, preferred_element_type=jnp.float32)]
    ppermute x20 -> x19, waiting for transfers between devices: 15.5 us -> 15.4 us  [swap(): return lax.ppermute(piece, 'expert', pairs)]
  transfers between devices with their start and end apart: 25 -> 24, of which waited for: 8 -> 12; matrix products, arithmetic and copies ran while one was open for 22% -> 20% of each run, Pallas kernels for 0% -> 0%
where the time goes in v1:
time: 77.4 us; the launch traced here: 77.1 us
  starting transfers between devices  32.7 us (42%)
  matrix products  18.8 us (24%)
  waiting for transfers between devices  15.7 us (20%)
  local copies, waits for them, and re-layouts  3.55 us (5%)
  Pallas kernels  2.75 us (4%)
  other arithmetic  2.55 us (3%)
  between operations  1.09 us (1%)
    ppermute x19, starting transfers between devices, swap(): return lax.ppermute(piece, 'expert', pairs)  27 us
    ppermute x19, waiting for transfers between devices, swap(): return lax.ppermute(piece, 'expert', pairs)  15.4 us
    ppermute x5, starting transfers between devices, copies(): pieces.append(lax.ppermute(rows, 'dp', ring))  5.72 us
    dot_general x2, matrix products, rows_product(): lax.dot_general(jnp.concatenate(left, axis=0), jnp.concatenate(right, axi...  5.2 us
    dot_general x2, matrix products, forward(): pre_exp = jnp.dot(norm_rows, w_up, preferred_element_type=jnp.float32)  3.2 us
    dot_general x2, matrix products, backward(): act_grad = jnp.dot(grad_rows, w_down, preferred_element_type=jnp.float32)  2.96 us
    dot_general x2, matrix products, backward(): lax.dot_general(pre_grad, w_up, contract_last, preferred_element_type=jnp...  2.9 us
    pallas_call x1, Pallas kernels, body(): pl.pallas_call(functools.partial(place_kernel, experts, low, high, capaci...  2.75 us
  transfers between devices with their start and end apart: 24, of which 12 were waited for; matrix products, arithmetic and copies ran while one was open for 20% of the time, Pallas kernels for 0%

profile of v1, /device:TPU:0, one launch (start us, length us, event | category | flops | bytes accessed | tf_op | source)
XLA Modules:
  0.0 77.1 jit_solution(1659691835593609191)
XLA Ops:
  0.6 2.7 %shard_map.85 = (bf16[64,1024]{1,0:T(8,128)(2,1)}, bf16[64,1024]{1,0:T(8,128)(2,1)}, bf16[64,1024]{1,0:T(8,128)(2,1)}, bf16[64,1024]{1,0:T(8,128)(2,1)}, bf16[64...) custom-call(s32[1]{0:T(128)} %bitcast.me_ref, ...), custom_call_target="tpu_custom_call" | custom-call | tf_op jit(solution)/shard_map/pallas_call | solution.py:85
  3.9 2.6 %collective-permute-start = (bf16[64,1024]{1,0:T(8,128)(2,1)}, bf16[64,1024]{1,0:T(8,128)(2,1)S(1)}, u32[]{:S(2)}, u32[]{:S(2)}) collective-permute-start(bf16[64,1024]{1,0:T(8,128)(2,1)} %get-tuple-element.71), channel_id=1, source_target_pairs={{0,3},{1,2},{2,1},{3,0},{4,7},{5,6},{6,5},{7,4},{8,11},{9,10},{10,... | collective-permute-start | bytes 393224 | tf_op jit(solution)/shard_map/ppermute | solution.py:22
  6.6 4.1 %collective-permute-start.3 = (bf16[16,2048]{1,0:T(8,128)(2,1)}, bf16[16,2048]{1,0:T(8,128)(2,1)S(1)}, u32[]{:S(2)}, u32[]{:S(2)}) collective-permute-start(bf16[16,2048]{1,0:T(8,128)(2,1)} %get-tuple-element.77), channel_id=1, source_target_pairs={{0,12},{1,13},{2,14},{3,15},{4,8},{5,9},{6,10},{7,11},{8,4},{9,5},... | collective-permute-start | bytes 196616 | tf_op jit(solution)/shard_map/ppermute | solution.py:22
  10.7 2.9 %collective-permute-done.1 = bf16[64,1024]{1,0:T(8,128)(2,1)S(1)} collective-permute-done((bf16[64,1024]{1,0:T(8,128)(2,1)}, bf16[64,1024]{1,0:T(8,128)(2,1)S(1)}, u32[]{:S(2)}, u32[]{:S(2)}) %collective-permute-start.1) | collective-permute-done | bytes 131104 | tf_op jit(solution)/shard_map/ppermute | solution.py:22
  16.2 1.6 %collective-permute-start.9 = (bf16[64,1024]{1,0:T(8,128)(2,1)S(1)}, bf16[64,1024]{1,0:T(8,128)(2,1)S(1)}, u32[]{:S(2)}, u32[]{:S(2)}) collective-permute-start(bf16[64,1024]{1,0:T(8,128)(2,1)S(1)} %copy-done.5), channel_id=1, source_target_pairs={{0,2},{1,3},{2,0},{3,1},{4,6},{5,7},{6,4},{7,5},{8,10},{9,11},{10,... | collective-permute-start | bytes 393224 | tf_op jit(solution)/shard_map/ppermute | solution.py:22
  18.0 1.5 %collective-permute-start.11 = (bf16[64,1024]{1,0:T(8,128)(2,1)S(1)}, bf16[64,1024]{1,0:T(8,128)(2,1)S(1)}, u32[]{:S(2)}, u32[]{:S(2)}) collective-permute-start(bf16[64,1024]{1,0:T(8,128)(2,1)S(1)} %pad_maximum_fusion.5), channel_id=1, source_target_pairs={{0,16},{16,0},{1,17},{17,1},{2,18},{18,2},{3,19},{19,3},{4,20},{20... | collective-permute-start | bytes 393224 | tf_op jit(solution)/shard_map/ppermute | solution.py:105
  19.6 2.3 %collective-permute-start.5 = (bf16[48,1024]{1,0:T(8,128)(2,1)S(1)}, bf16[48,1024]{1,0:T(8,128)(2,1)S(1)}, u32[]{:S(2)}, u32[]{:S(2)}) collective-permute-start(bf16[48,1024]{1,0:T(8,128)(2,1)S(1)} %pad_maximum_fusion.10), channel_id=1, source_target_pairs={{0,12},{1,13},{2,14},{3,15},{4,8},{5,9},{6,10},{7,11},{8,4},{9,5},... | collective-permute-start | bytes 294920 | tf_op jit(solution)/shard_map/ppermute | solution.py:22
  23.2 1.6 %collective-permute-done.9 = bf16[64,1024]{1,0:T(8,128)(2,1)S(1)} collective-permute-done((bf16[64,1024]{1,0:T(8,128)(2,1)S(1)}, bf16[64,1024]{1,0:T(8,128)(2,1)S(1)}, u32[]{:S(2)}, u32[]{:S(2)}) %collective-permute-start.9) | collective-permute-done | bytes 131104 | tf_op jit(solution)/shard_map/ppermute | solution.py:22
  25.7 1.5 %collective-permute-start.12 = (bf16[32,2048]{1,0:T(8,128)(2,1)S(1)}, bf16[32,2048]{1,0:T(8,128)(2,1)S(1)}, u32[]{:S(2)}, u32[]{:S(2)}) collective-permute-start(bf16[32,2048]{1,0:T(8,128)(2,1)S(1)} %pad_maximum_fusion.6), channel_id=1, source_target_pairs={{0,16},{16,0},{1,17},{17,1},{2,18},{18,2},{3,19},{19,3},{4,20},{20... | collective-permute-start | bytes 393224 | tf_op jit(solution)/shard_map/ppermute | solution.py:105
  27.9 1.9 %collective-permute-start.15 = (bf16[48,1024]{1,0:T(8,128)(2,1)S(1)}, bf16[48,1024]{1,0:T(8,128)(2,1)S(1)}, u32[]{:S(2)}, u32[]{:S(2)}) collective-permute-start(bf16[48,1024]{1,0:T(8,128)(2,1)S(1)} %pad_maximum_fusion.12), channel_id=1, source_target_pairs={{0,12},{1,13},{2,14},{3,15},{4,8},{5,9},{6,10},{7,11},{8,4},{9,5},... | collective-permute-start | bytes 294920 | tf_op jit(solution)/shard_map/ppermute | solution.py:22
  30.0 4.2 %collective-permute-start.16 = (bf16[64,1024]{1,0:T(8,128)(2,1)S(1)}, bf16[64,1024]{1,0:T(8,128)(2,1)S(1)}, u32[]{:S(2)}, u32[]{:S(2)}) collective-permute-start(bf16[64,1024]{1,0:T(8,128)(2,1)S(1)} %pad_maximum_fusion.9), channel_id=1, source_target_pairs={{0,8},{1,9},{2,10},{3,11},{4,12},{5,13},{6,14},{7,15},{8,0},{9,1},... | collective-permute-start | bytes 393224 | tf_op jit(solution)/shard_map/ppermute | solution.py:22
  34.2 2.1 %collective-permute-done.6 = bf16[64,1024]{1,0:T(8,128)(2,1)S(1)} collective-permute-done((bf16[64,1024]{1,0:T(8,128)(2,1)S(1)}, bf16[64,1024]{1,0:T(8,128)(2,1)S(1)}, u32[]{:S(2)}, u32[]{:S(2)}) %collective-permute-start.6) | collective-permute-done | bytes 131104 | tf_op jit(solution)/shard_map/ppermute | solution.py:22
  36.9 2.0 %collective-permute-start.14 = (bf16[160,1024]{1,0:T(8,128)(2,1)S(1)}, bf16[160,1024]{1,0:T(8,128)(2,1)S(1)}, u32[]{:S(2)}, u32[]{:S(2)}) collective-permute-start(bf16[160,1024]{1,0:T(8,128)(2,1)S(1)} %pad_maximum_fusion.1), channel_id=1, source_target_pairs={{0,16},{16,0},{1,17},{17,1},{2,18},{18,2},{3,19},{19,3},{4,20},{20... | collective-permute-start | bytes 983048 | tf_op jit(solution)/shard_map/ppermute | solution.py:105
  41.1 1.8 %add_multiply_fusion = (f32[256,2048]{1,0:T(8,128)S(1)}, bf16[256,2048]{1,0:T(8,128)(2,1)S(1)}) fusion(bf16[256,1024]{1,0:T(8,128)(2,1)S(1)} %multiply_convert_fusion.5, bf16[1,1024,2048]{2,1,0:T(8,128)(2,1)S(1)} %copy-done.3), kind=kOutput, calls=%fused_computation.28 | convolution fusion | flops 1078460416 | bytes 7864320 | tf_op jit(solution)/shard_map/dot_general | solution.py:114
  43.9 1.5 %copy-done.1 = bf16[1,1024,2048]{2,1,0:T(8,128)(2,1)S(1)} copy-done((bf16[1,1024,2048]{2,1,0:T(8,128)(2,1)S(1)}, bf16[1,1024,2048]{2,1,0:T(8,128)(2,1)}, u32[]{:S(2)}) %copy-start.1) | copy-done | bytes 4194328
  52.1 1.7 %fusion.20 = bf16[256,2048]{1,0:T(8,128)(2,1)S(1)} fusion(bf16[256,1024]{1,0:T(8,128)(2,1)S(1)} %constant_dynamic-update-slice_fusion.7, bf16[1,1024,2048]{2,1,0:T(8,128)(2,1)S(1)} %copy-done.1, f32[256,2048]{1,0:T(8,128)S(1)} %get-tuple-element.194), kind=kOutput, calls=%fused_computation.18 | convolution fusion | flops 1078460416 | bytes 7864320 | tf_op jit(solution)/shard_map/dot_general | solution.py:198
  53.7 1.5 %multiply_reduce_fusion = (f32[256]{0:T(256)S(1)}, f32[256,1024]{1,0:T(8,128)S(1)}) fusion(f32[256,1024]{1,0:T(8,128)S(1)} %get-tuple-element.190, bf16[256,1024]{1,0:T(8,128)(2,1)S(1)} %constant_dynamic-update-slice_fusion.5, bf16[256,2048]{1,0:T(8,128)(2,1)S(1)} %fusion.20, bf16[1,1024,2048]{2,1,0:T(8,128)(2,1)S(1)} %copy-done.3), kind=kOutput, calls=%fused_computation.41 | convolution fusion | flops 1075838720 | bytes 7865344 | tf_op jit(solution)/shard_map/dot_general | solution.py:200
  57.3 1.5 %collective-permute-done.19 = bf16[256,1024]{1,0:T(8,128)(2,1)S(1)} collective-permute-done((bf16[256,1024]{1,0:T(8,128)(2,1)S(1)}, bf16[256,1024]{1,0:T(8,128)(2,1)S(1)}, u32[]{:S(2)}, u32[]{:S(2)}) %collective-permute-start.19) | collective-permute-done | bytes 524320 | tf_op jit(solution)/shard_map/ppermute | solution.py:22
  59.1 2.3 %collective-permute-start.20 = (bf16[128,1024]{1,0:T(8,128)(2,1)S(1)}, bf16[128,1024]{1,0:T(8,128)(2,1)S(1)}, u32[]{:S(2)}, u32[]{:S(2)}) collective-permute-start(bf16[128,1024]{1,0:T(8,128)(2,1)S(1)} %slice.197), channel_id=1, source_target_pairs={{0,2},{1,3},{2,0},{3,1},{4,6},{5,7},{6,4},{7,5},{8,10},{9,11},{10,... | collective-permute-start | bytes 786440 | tf_op jit(solution)/shard_map/ppermute | solution.py:22
  61.4 2.6 %fusion.18 = bf16[1,512,2048]{2,1,0:T(8,128)(2,1)} fusion(bf16[256,2048]{1,0:T(8,128)(2,1)S(1)} %fusion.20, bf16[256,2048]{1,0:T(8,128)(2,1)S(1)} %fusion.23, bf16[256,512]{1,0:T(8,128)(2,1)S(1)} %constant_dynamic-slice_fusion.2, bf16[256,512]{1,0:T(8,128)(2,1)S(1)} %constant_dynamic-slice_fusion.3), kind=kOutput, calls=%fused_computation.16 | convolution fusion | flops 1080033280 | bytes 4718592 | tf_op jit(solution)/shard_map/dot_general | solution.py:252
  64.0 4.0 %collective-permute-done.20 = bf16[128,1024]{1,0:T(8,128)(2,1)S(1)} collective-permute-done((bf16[128,1024]{1,0:T(8,128)(2,1)S(1)}, bf16[128,1024]{1,0:T(8,128)(2,1)S(1)}, u32[]{:S(2)}, u32[]{:S(2)}) %collective-permute-start.20) | collective-permute-done | bytes 262176 | tf_op jit(solution)/shard_map/ppermute | solution.py:22
  68.1 1.8 %collective-permute-start.23 = (bf16[32,1024]{1,0:T(8,128)(2,1)S(1)}, bf16[32,1024]{1,0:T(8,128)(2,1)S(1)}, u32[]{:S(2)}, u32[]{:S(2)}) collective-permute-start(bf16[32,1024]{1,0:T(8,128)(2,1)S(1)} %get-tuple-element.147), channel_id=1, source_target_pairs={{0,12},{1,13},{2,14},{3,15},{4,8},{5,9},{6,10},{7,11},{8,4},{9,5},... | collective-permute-start | bytes 196616 | tf_op jit(solution)/shard_map/ppermute | solution.py:22
  70.1 2.5 %collective-permute-start.21 = (bf16[32,1024]{1,0:T(8,128)(2,1)S(1)}, bf16[32,1024]{1,0:T(8,128)(2,1)S(1)}, u32[]{:S(2)}, u32[]{:S(2)}) collective-permute-start(bf16[32,1024]{1,0:T(8,128)(2,1)S(1)} %get-tuple-element.146), channel_id=1, source_target_pairs={{0,4},{1,5},{2,6},{3,7},{4,0},{5,1},{6,2},{7,3},{8,12},{9,13},{10,... | collective-permute-start | bytes 196616 | tf_op jit(solution)/shard_map/ppermute | solution.py:22
  72.6 2.6 %fusion.19 = bf16[1,512,2048]{2,1,0:T(8,128)(2,1)} fusion(bf16[256,2048]{1,0:T(8,128)(2,1)S(1)} %get-tuple-element.193, bf16[256,2048]{1,0:T(8,128)(2,1)S(1)} %get-tuple-element.138, bf16[256,512]{1,0:T(8,128)(2,1)S(1)} %constant_dynamic-slice_fusion, bf16[256,512]{1,0:T(8,128)(2,1)S(1)} %constant_dynamic-slice_fusion.1), kind=kOutput, calls=%fused_computation.17 | convolution fusion | flops 1080033280 | bytes 4718592 | tf_op jit(solution)/shard_map/dot_general | solution.py:252
  (99 shorter events, 21.3 us)
Async XLA Ops:
  3.4 3.2 %collective-permute-start.2 = (bf16[64,1024]{1,0:T(8,128)(2,1)}, bf16[64,1024]{1,0:T(8,128)(2,1)S(1)}, u32[]{:S(2)}, u32[]{:S(2)}) collective-permute-start(bf16[64,1024]{1,0:T(8,128)(2,1)} %get-tuple-element.75), channel_id=1, source_target_pairs={{0,1},{1,0},{2,3},{3,2},{4,5},{5,4},{6,7},{7,6},{8,9},{9,8},{10,11... | collective-permute-start | bytes 393224 | tf_op jit(solution)/shard_map/ppermute | solution.py:22
  3.9 6.8 %collective-permute-start = (bf16[64,1024]{1,0:T(8,128)(2,1)}, bf16[64,1024]{1,0:T(8,128)(2,1)S(1)}, u32[]{:S(2)}, u32[]{:S(2)}) collective-permute-start(bf16[64,1024]{1,0:T(8,128)(2,1)} %get-tuple-element.71), channel_id=1, source_target_pairs={{0,3},{1,2},{2,1},{3,0},{4,7},{5,6},{6,5},{7,4},{8,11},{9,10},{10,... | collective-permute-start | bytes 393224 | tf_op jit(solution)/shard_map/ppermute | solution.py:22
  6.6 7.1 %collective-permute-start.1 = (bf16[64,1024]{1,0:T(8,128)(2,1)}, bf16[64,1024]{1,0:T(8,128)(2,1)S(1)}, u32[]{:S(2)}, u32[]{:S(2)}) collective-permute-start(bf16[64,1024]{1,0:T(8,128)(2,1)} %get-tuple-element.72), channel_id=1, source_target_pairs={{0,2},{1,3},{2,0},{3,1},{4,6},{5,7},{6,4},{7,5},{8,10},{9,11},{10,... | collective-permute-start | bytes 393224 | tf_op jit(solution)/shard_map/ppermute | solution.py:22
  6.6 7.2 %collective-permute-start.3 = (bf16[16,2048]{1,0:T(8,128)(2,1)}, bf16[16,2048]{1,0:T(8,128)(2,1)S(1)}, u32[]{:S(2)}, u32[]{:S(2)}) collective-permute-start(bf16[16,2048]{1,0:T(8,128)(2,1)} %get-tuple-element.77), channel_id=1, source_target_pairs={{0,12},{1,13},{2,14},{3,15},{4,8},{5,9},{6,10},{7,11},{8,4},{9,5},... | collective-permute-start | bytes 196616 | tf_op jit(solution)/shard_map/ppermute | solution.py:22
  10.7 4.5 %collective-permute-start.4 = (bf16[16,2048]{1,0:T(8,128)(2,1)}, bf16[16,2048]{1,0:T(8,128)(2,1)S(1)}, u32[]{:S(2)}, u32[]{:S(2)}) collective-permute-start(bf16[16,2048]{1,0:T(8,128)(2,1)} %get-tuple-element.78), channel_id=1, source_target_pairs={{0,4},{1,5},{2,6},{3,7},{4,0},{5,1},{6,2},{7,3},{8,12},{9,13},{10,... | collective-permute-start | bytes 196616 | tf_op jit(solution)/shard_map/ppermute | solution.py:22
  16.1 5.8 %collective-permute-start.8 = (bf16[64,1024]{1,0:T(8,128)(2,1)S(1)}, bf16[64,1024]{1,0:T(8,128)(2,1)S(1)}, u32[]{:S(2)}, u32[]{:S(2)}) collective-permute-start(bf16[64,1024]{1,0:T(8,128)(2,1)S(1)} %copy-done.6), channel_id=1, source_target_pairs={{0,3},{1,2},{2,1},{3,0},{4,7},{5,6},{6,5},{7,4},{8,11},{9,10},{10,... | collective-permute-start | bytes 393224 | tf_op jit(solution)/shard_map/ppermute | solution.py:22
  16.2 8.6 %collective-permute-start.9 = (bf16[64,1024]{1,0:T(8,128)(2,1)S(1)}, bf16[64,1024]{1,0:T(8,128)(2,1)S(1)}, u32[]{:S(2)}, u32[]{:S(2)}) collective-permute-start(bf16[64,1024]{1,0:T(8,128)(2,1)S(1)} %copy-done.5), channel_id=1, source_target_pairs={{0,2},{1,3},{2,0},{3,1},{4,6},{5,7},{6,4},{7,5},{8,10},{9,11},{10,... | collective-permute-start | bytes 393224 | tf_op jit(solution)/shard_map/ppermute | solution.py:22
  17.8 7.9 %collective-permute-start.10 = (bf16[64,1024]{1,0:T(8,128)(2,1)S(1)}, bf16[64,1024]{1,0:T(8,128)(2,1)S(1)}, u32[]{:S(2)}, u32[]{:S(2)}) collective-permute-start(bf16[64,1024]{1,0:T(8,128)(2,1)S(1)} %copy-done.4), channel_id=1, source_target_pairs={{0,1},{1,0},{2,3},{3,2},{4,5},{5,4},{6,7},{7,6},{8,9},{9,8},{10,11... | collective-permute-start | bytes 393224 | tf_op jit(solution)/shard_map/ppermute | solution.py:22
  18.0 9.2 %collective-permute-start.11 = (bf16[64,1024]{1,0:T(8,128)(2,1)S(1)}, bf16[64,1024]{1,0:T(8,128)(2,1)S(1)}, u32[]{:S(2)}, u32[]{:S(2)}) collective-permute-start(bf16[64,1024]{1,0:T(8,128)(2,1)S(1)} %pad_maximum_fusion.5), channel_id=1, source_target_pairs={{0,16},{16,0},{1,17},{17,1},{2,18},{18,2},{3,19},{19,3},{4,20},{20... | collective-permute-start | bytes 393224 | tf_op jit(solution)/shard_map/ppermute | solution.py:105
  19.6 8.4 %collective-permute-start.5 = (bf16[48,1024]{1,0:T(8,128)(2,1)S(1)}, bf16[48,1024]{1,0:T(8,128)(2,1)S(1)}, u32[]{:S(2)}, u32[]{:S(2)}) collective-permute-start(bf16[48,1024]{1,0:T(8,128)(2,1)S(1)} %pad_maximum_fusion.10), channel_id=1, source_target_pairs={{0,12},{1,13},{2,14},{3,15},{4,8},{5,9},{6,10},{7,11},{8,4},{9,5},... | collective-permute-start | bytes 294920 | tf_op jit(solution)/shard_map/ppermute | solution.py:22
  21.9 14.4 %collective-permute-start.6 = (bf16[64,1024]{1,0:T(8,128)(2,1)S(1)}, bf16[64,1024]{1,0:T(8,128)(2,1)S(1)}, u32[]{:S(2)}, u32[]{:S(2)}) collective-permute-start(bf16[64,1024]{1,0:T(8,128)(2,1)S(1)} %pad_maximum_fusion.7), channel_id=1, source_target_pairs={{0,8},{1,9},{2,10},{3,11},{4,12},{5,13},{6,14},{7,15},{8,0},{9,1},... | collective-permute-start | bytes 393224 | tf_op jit(solution)/shard_map/ppermute | solution.py:22
  24.8 5.3 %collective-permute-start.7 = (bf16[48,1024]{1,0:T(8,128)(2,1)S(1)}, bf16[48,1024]{1,0:T(8,128)(2,1)S(1)}, u32[]{:S(2)}, u32[]{:S(2)}) collective-permute-start(bf16[48,1024]{1,0:T(8,128)(2,1)S(1)} %pad_maximum_fusion.11), channel_id=1, source_target_pairs={{0,4},{1,5},{2,6},{3,7},{4,0},{5,1},{6,2},{7,3},{8,12},{9,13},{10,... | collective-permute-start | bytes 294920 | tf_op jit(solution)/shard_map/ppermute | solution.py:22
  25.7 11.1 %collective-permute-start.12 = (bf16[32,2048]{1,0:T(8,128)(2,1)S(1)}, bf16[32,2048]{1,0:T(8,128)(2,1)S(1)}, u32[]{:S(2)}, u32[]{:S(2)}) collective-permute-start(bf16[32,2048]{1,0:T(8,128)(2,1)S(1)} %pad_maximum_fusion.6), channel_id=1, source_target_pairs={{0,16},{16,0},{1,17},{17,1},{2,18},{18,2},{3,19},{19,3},{4,20},{20... | collective-permute-start | bytes 393224 | tf_op jit(solution)/shard_map/ppermute | solution.py:105
  27.3 9.5 %collective-permute-start.13 = (bf16[64,1024]{1,0:T(8,128)(2,1)S(1)}, bf16[64,1024]{1,0:T(8,128)(2,1)S(1)}, u32[]{:S(2)}, u32[]{:S(2)}) collective-permute-start(bf16[64,1024]{1,0:T(8,128)(2,1)S(1)} %pad_maximum_fusion.8), channel_id=1, source_target_pairs={{0,16},{16,0},{1,17},{17,1},{2,18},{18,2},{3,19},{19,3},{4,20},{20... | collective-permute-start | bytes 393224 | tf_op jit(solution)/shard_map/ppermute | solution.py:105
  27.9 15.0 %collective-permute-start.15 = (bf16[48,1024]{1,0:T(8,128)(2,1)S(1)}, bf16[48,1024]{1,0:T(8,128)(2,1)S(1)}, u32[]{:S(2)}, u32[]{:S(2)}) collective-permute-start(bf16[48,1024]{1,0:T(8,128)(2,1)S(1)} %pad_maximum_fusion.12), channel_id=1, source_target_pairs={{0,12},{1,13},{2,14},{3,15},{4,8},{5,9},{6,10},{7,11},{8,4},{9,5},... | collective-permute-start | bytes 294920 | tf_op jit(solution)/shard_map/ppermute | solution.py:22
  30.0 13.1 %collective-permute-start.16 = (bf16[64,1024]{1,0:T(8,128)(2,1)S(1)}, bf16[64,1024]{1,0:T(8,128)(2,1)S(1)}, u32[]{:S(2)}, u32[]{:S(2)}) collective-permute-start(bf16[64,1024]{1,0:T(8,128)(2,1)S(1)} %pad_maximum_fusion.9), channel_id=1, source_target_pairs={{0,8},{1,9},{2,10},{3,11},{4,12},{5,13},{6,14},{7,15},{8,0},{9,1},... | collective-permute-start | bytes 393224 | tf_op jit(solution)/shard_map/ppermute | solution.py:22
  36.3 6.9 %collective-permute-start.17 = (bf16[48,1024]{1,0:T(8,128)(2,1)S(1)}, bf16[48,1024]{1,0:T(8,128)(2,1)S(1)}, u32[]{:S(2)}, u32[]{:S(2)}) collective-permute-start(bf16[48,1024]{1,0:T(8,128)(2,1)S(1)} %pad_maximum_fusion.13), channel_id=1, source_target_pairs={{0,4},{1,5},{2,6},{3,7},{4,0},{5,1},{6,2},{7,3},{8,12},{9,13},{10,... | collective-permute-start | bytes 294920 | tf_op jit(solution)/shard_map/ppermute | solution.py:22
  36.9 11.5 %collective-permute-start.14 = (bf16[160,1024]{1,0:T(8,128)(2,1)S(1)}, bf16[160,1024]{1,0:T(8,128)(2,1)S(1)}, u32[]{:S(2)}, u32[]{:S(2)}) collective-permute-start(bf16[160,1024]{1,0:T(8,128)(2,1)S(1)} %pad_maximum_fusion.1), channel_id=1, source_target_pairs={{0,16},{16,0},{1,17},{17,1},{2,18},{18,2},{3,19},{19,3},{4,20},{20... | collective-permute-start | bytes 983048 | tf_op jit(solution)/shard_map/ppermute | solution.py:105
  43.8 8.3 %collective-permute-start.18 = (bf16[160,1024]{1,0:T(8,128)(2,1)S(1)}, bf16[160,1024]{1,0:T(8,128)(2,1)S(1)}, u32[]{:S(2)}, u32[]{:S(2)}) collective-permute-start(bf16[160,1024]{1,0:T(8,128)(2,1)S(1)} %pad_maximum_fusion.2), channel_id=1, source_target_pairs={{0,16},{16,0},{1,17},{17,1},{2,18},{18,2},{3,19},{19,3},{4,20},{20... | collective-permute-start | bytes 983048 | tf_op jit(solution)/shard_map/ppermute | solution.py:105
  56.7 2.0 %collective-permute-start.19 = (bf16[256,1024]{1,0:T(8,128)(2,1)S(1)}, bf16[256,1024]{1,0:T(8,128)(2,1)S(1)}, u32[]{:S(2)}, u32[]{:S(2)}) collective-permute-start(bf16[256,1024]{1,0:T(8,128)(2,1)S(1)} %fusion.35), channel_id=1, source_target_pairs={{0,1},{1,0},{2,3},{3,2},{4,5},{5,4},{6,7},{7,6},{8,9},{9,8},{10,11... | collective-permute-start | bytes 1572872 | tf_op jit(solution)/shard_map/ppermute | solution.py:22
  59.1 8.9 %collective-permute-start.20 = (bf16[128,1024]{1,0:T(8,128)(2,1)S(1)}, bf16[128,1024]{1,0:T(8,128)(2,1)S(1)}, u32[]{:S(2)}, u32[]{:S(2)}) collective-permute-start(bf16[128,1024]{1,0:T(8,128)(2,1)S(1)} %slice.197), channel_id=1, source_target_pairs={{0,2},{1,3},{2,0},{3,1},{4,6},{5,7},{6,4},{7,5},{8,10},{9,11},{10,... | collective-permute-start | bytes 786440 | tf_op jit(solution)/shard_map/ppermute | solution.py:22
  68.1 7.1 %collective-permute-start.23 = (bf16[32,1024]{1,0:T(8,128)(2,1)S(1)}, bf16[32,1024]{1,0:T(8,128)(2,1)S(1)}, u32[]{:S(2)}, u32[]{:S(2)}) collective-permute-start(bf16[32,1024]{1,0:T(8,128)(2,1)S(1)} %get-tuple-element.147), channel_id=1, source_target_pairs={{0,12},{1,13},{2,14},{3,15},{4,8},{5,9},{6,10},{7,11},{8,4},{9,5},... | collective-permute-start | bytes 196616 | tf_op jit(solution)/shard_map/ppermute | solution.py:22
  69.9 6.5 %collective-permute-start.22 = (bf16[32,1024]{1,0:T(8,128)(2,1)S(1)}, bf16[32,1024]{1,0:T(8,128)(2,1)S(1)}, u32[]{:S(2)}, u32[]{:S(2)}) collective-permute-start(bf16[32,1024]{1,0:T(8,128)(2,1)S(1)} %get-tuple-element.148), channel_id=1, source_target_pairs={{0,8},{1,9},{2,10},{3,11},{4,12},{5,13},{6,14},{7,15},{8,0},{9,1},... | collective-permute-start | bytes 196616 | tf_op jit(solution)/shard_map/ppermute | solution.py:22
  70.1 6.4 %collective-permute-start.21 = (bf16[32,1024]{1,0:T(8,128)(2,1)S(1)}, bf16[32,1024]{1,0:T(8,128)(2,1)S(1)}, u32[]{:S(2)}, u32[]{:S(2)}) collective-permute-start(bf16[32,1024]{1,0:T(8,128)(2,1)S(1)} %get-tuple-element.146), channel_id=1, source_target_pairs={{0,4},{1,5},{2,6},{3,7},{4,0},{5,1},{6,2},{7,3},{8,12},{9,13},{10,... | collective-permute-start | bytes 196616 | tf_op jit(solution)/shard_map/ppermute | solution.py:22
  (7 other events, 100.9 us)

commit v2 on v1

--- a/solution.py
+++ b/solution.py
@@ -153,19 +153,25 @@
     cells_first_copies = copies(cells_first)
     grads_near = send_near(grads_placed)
     cells_far = send_far(cells_far)
-    direct_copies = copies(direct)
+    direct_cells, direct_grads = direct[:, :model_width], direct[:, model_width:]
     grads_near, cells_first_copies = fence((grads_near, cells_first_copies))
     grads_first = here_and_near(here[1], grads_near)
-    grads_first_copies = copies(grads_first)
-    grads_far = send_far(far_pieces(here[1], grads_near))
-    came = (cells_first_copies, direct_copies, grads_first_copies)
-    cells_far, came = fence((cells_far, came))
-    cells_far, came = fence((stack(*cells_far), came))
+    grads_far = far_pieces(here[1], grads_near)
+    second_copies = copies(stack(grads_first, direct_cells, direct_grads))
+    *grads_far, grads_last = send_far(grads_far[:-1]) + grads_far[-1:]
+    came = (cells_first_copies, second_copies)
+    cells_far, came, grads_last = fence((cells_far, came, grads_last))
+    cells_far, came, grads_last = fence((stack(*cells_far), came, grads_last))
     cells_far_copies = copies(cells_far)
-    features = stack(cells_first, direct[:, :model_width], cells_far)
+    grads_far += [swap(grads_last, low)]
+    features = stack(cells_first, direct_cells, cells_far)
+    first_rows, direct_rows = cells_first.shape[0], direct.shape[0]
     early = [
-        (stack(cells, both[:, :model_width]), stack(grads, both[:, model_width:]))
-        for cells, both, grads in zip(*came)
+        (
+            stack(cells, second[first_rows:-direct_rows]),
+            stack(second[:first_rows], second[-direct_rows:]),
+        )
+        for cells, second in zip(*came)
     ]
     grads_far, early, own_forward = fence((grads_far, early, forward(features)))
     grads_far, early, own_forward = fence((stack(*grads_far), early, own_forward))
@@ -211,7 +217,7 @@
         active_parts.append(active)
         grad_parts.append(my_columns(grad_rows))
 
-    backward(features, stack(grads_first, direct[:, model_width:], grads_far), own_forward)
+    backward(features, stack(grads_first, direct_grads, grads_far), own_forward)
     cells_far_copies, enc_parts[0] = fence((cells_far_copies, enc_parts[0]))
     for (cells_early, grads_early), cells_far, grads_far in zip(
         early, cells_far_copies, grads_far_copies

time: 77.4 us -> 79.1 us (1.022)
  waiting for transfers between devices: 15.7 us -> 24.2 us
  starting transfers between devices: 32.7 us -> 26.9 us
  local copies, waits for them, and re-layouts: 3.55 us -> 2.68 us
    ppermute x19, waiting for transfers between devices: 15.4 us -> 22.2 us  [swap(): return lax.ppermute(piece, 'expert', pairs)]
    ppermute x19, starting transfers between devices: 27 us -> 22.2 us  [swap(): return lax.ppermute(piece, 'expert', pairs)]
    ppermute x5 -> x4, waiting for transfers between devices: 0.28 us -> 1.97 us  [copies(): pieces.append(lax.ppermute(rows, 'dp', ring))]
    ppermute x5 -> x4, starting transfers between devices: 5.72 us -> 4.73 us  [copies(): pieces.append(lax.ppermute(rows, 'dp', ring))]
    unnamed x21, local copies, waits for them, and re-layouts: 2.51 us -> 1.63 us
  transfers between devices with their start and end apart: 24 -> 23, of which waited for: 12 -> 11; matrix products, arithmetic and copies ran while one was open for 20% -> 20% of each run, Pallas kernels for 0% -> 0%
where the time goes in v2:
time: 79.1 us; the launch traced here: 78.9 us
  starting transfers between devices  26.9 us (34%)
  waiting for transfers between devices  24.2 us (31%)
  matrix products  18.8 us (24%)
  Pallas kernels  2.75 us (3%)
  local copies, waits for them, and re-layouts  2.68 us (3%)
  other arithmetic  2.52 us (3%)
  between operations  1.1 us (1%)
    ppermute x19, waiting for transfers between devices, swap(): return lax.ppermute(piece, 'expert', pairs)  22.2 us
    ppermute x19, starting transfers between devices, swap(): return lax.ppermute(piece, 'expert', pairs)  22.2 us
    dot_general x2, matrix products, rows_product(): lax.dot_general(jnp.concatenate(left, axis=0), jnp.concatenate(right, axi...  5.2 us
    ppermute x4, starting transfers between devices, copies(): pieces.append(lax.ppermute(rows, 'dp', ring))  4.73 us
    dot_general x2, matrix products, forward(): pre_exp = jnp.dot(norm_rows, w_up, preferred_element_type=jnp.float32)  3.2 us
    dot_general x2, matrix products, backward(): act_grad = jnp.dot(grad_rows, w_down, preferred_element_type=jnp.float32)  2.96 us
    dot_general x2, matrix products, backward(): lax.dot_general(pre_grad, w_up, contract_last, preferred_element_type=jnp...  2.9 us
    pallas_call x1, Pallas kernels, body(): pl.pallas_call(functools.partial(place_kernel, experts, low, high, capaci...  2.75 us
  transfers between devices with their start and end apart: 23, of which 11 were waited for; matrix products, arithmetic and copies ran while one was open for 20% of the time, Pallas kernels for 0%

profile of v2, /device:TPU:0, one launch (start us, length us, event | category | flops | bytes accessed | tf_op | source)
XLA Modules:
  0.0 78.9 jit_solution(8010105045626206627)
XLA Ops:
  0.6 2.7 %shard_map.85 = (bf16[64,1024]{1,0:T(8,128)(2,1)}, bf16[64,1024]{1,0:T(8,128)(2,1)}, bf16[64,1024]{1,0:T(8,128)(2,1)}, bf16[64,1024]{1,0:T(8,128)(2,1)}, bf16[64...) custom-call(s32[1]{0:T(128)} %bitcast.me_ref, ...), custom_call_target="tpu_custom_call" | custom-call | tf_op jit(solution)/shard_map/pallas_call | solution.py:85
  3.9 2.6 %collective-permute-start = (bf16[64,1024]{1,0:T(8,128)(2,1)}, bf16[64,1024]{1,0:T(8,128)(2,1)S(1)}, u32[]{:S(2)}, u32[]{:S(2)}) collective-permute-start(bf16[64,1024]{1,0:T(8,128)(2,1)} %get-tuple-element.71), channel_id=1, source_target_pairs={{0,3},{1,2},{2,1},{3,0},{4,7},{5,6},{6,5},{7,4},{8,11},{9,10},{10,... | collective-permute-start | bytes 393224 | tf_op jit(solution)/shard_map/ppermute | solution.py:22
  6.6 4.1 %collective-permute-start.3 = (bf16[16,2048]{1,0:T(8,128)(2,1)}, bf16[16,2048]{1,0:T(8,128)(2,1)S(1)}, u32[]{:S(2)}, u32[]{:S(2)}) collective-permute-start(bf16[16,2048]{1,0:T(8,128)(2,1)} %get-tuple-element.77), channel_id=1, source_target_pairs={{0,12},{1,13},{2,14},{3,15},{4,8},{5,9},{6,10},{7,11},{8,4},{9,5},... | collective-permute-start | bytes 196616 | tf_op jit(solution)/shard_map/ppermute | solution.py:22
  10.7 2.9 %collective-permute-done.1 = bf16[64,1024]{1,0:T(8,128)(2,1)S(1)} collective-permute-done((bf16[64,1024]{1,0:T(8,128)(2,1)}, bf16[64,1024]{1,0:T(8,128)(2,1)S(1)}, u32[]{:S(2)}, u32[]{:S(2)}) %collective-permute-start.1) | collective-permute-done | bytes 131104 | tf_op jit(solution)/shard_map/ppermute | solution.py:22
  13.8 1.4 %collective-permute-done.4 = bf16[16,2048]{1,0:T(8,128)(2,1)S(1)} collective-permute-done((bf16[16,2048]{1,0:T(8,128)(2,1)}, bf16[16,2048]{1,0:T(8,128)(2,1)S(1)}, u32[]{:S(2)}, u32[]{:S(2)}) %collective-permute-start.4) | collective-permute-done | bytes 65568 | tf_op jit(solution)/shard_map/ppermute | solution.py:22
  16.2 1.6 %collective-permute-start.9 = (bf16[64,1024]{1,0:T(8,128)(2,1)S(1)}, bf16[64,1024]{1,0:T(8,128)(2,1)S(1)}, u32[]{:S(2)}, u32[]{:S(2)}) collective-permute-start(bf16[64,1024]{1,0:T(8,128)(2,1)S(1)} %copy-done.5), channel_id=1, source_target_pairs={{0,2},{1,3},{2,0},{3,1},{4,6},{5,7},{6,4},{7,5},{8,10},{9,11},{10,... | collective-permute-start | bytes 393224 | tf_op jit(solution)/shard_map/ppermute | solution.py:22
  18.0 1.5 %collective-permute-start.11 = (bf16[64,1024]{1,0:T(8,128)(2,1)S(1)}, bf16[64,1024]{1,0:T(8,128)(2,1)S(1)}, u32[]{:S(2)}, u32[]{:S(2)}) collective-permute-start(bf16[64,1024]{1,0:T(8,128)(2,1)S(1)} %pad_maximum_fusion.5), channel_id=1, source_target_pairs={{0,16},{16,0},{1,17},{17,1},{2,18},{18,2},{3,19},{19,3},{4,20},{20... | collective-permute-start | bytes 393224 | tf_op jit(solution)/shard_map/ppermute | solution.py:105
  19.6 2.3 %collective-permute-start.5 = (bf16[48,1024]{1,0:T(8,128)(2,1)S(1)}, bf16[48,1024]{1,0:T(8,128)(2,1)S(1)}, u32[]{:S(2)}, u32[]{:S(2)}) collective-permute-start(bf16[48,1024]{1,0:T(8,128)(2,1)S(1)} %pad_maximum_fusion.9), channel_id=1, source_target_pairs={{0,12},{1,13},{2,14},{3,15},{4,8},{5,9},{6,10},{7,11},{8,4},{9,5},... | collective-permute-start | bytes 294920 | tf_op jit(solution)/shard_map/ppermute | solution.py:22
  23.2 1.6 %collective-permute-done.9 = bf16[64,1024]{1,0:T(8,128)(2,1)S(1)} collective-permute-done((bf16[64,1024]{1,0:T(8,128)(2,1)S(1)}, bf16[64,1024]{1,0:T(8,128)(2,1)S(1)}, u32[]{:S(2)}, u32[]{:S(2)}) %collective-permute-start.9) | collective-permute-done | bytes 131104 | tf_op jit(solution)/shard_map/ppermute | solution.py:22
  25.8 1.6 %collective-permute-start.12 = (bf16[128,1024]{1,0:T(8,128)(2,1)S(1)}, bf16[128,1024]{1,0:T(8,128)(2,1)S(1)}, u32[]{:S(2)}, u32[]{:S(2)}) collective-permute-start(bf16[128,1024]{1,0:T(8,128)(2,1)S(1)} %slice_dynamic-update-slice_fusion.1), channel_id=1, source_target_pairs={{0,16},{16,0},{1,17},{17,1},{2,18},{18,2},{3,19},{19,3},{4,20},{20... | collective-permute-start | bytes 786440 | tf_op jit(solution)/shard_map/ppermute | solution.py:105
  27.4 1.9 %collective-permute-start.14 = (bf16[48,1024]{1,0:T(8,128)(2,1)S(1)}, bf16[48,1024]{1,0:T(8,128)(2,1)S(1)}, u32[]{:S(2)}, u32[]{:S(2)}) collective-permute-start(bf16[48,1024]{1,0:T(8,128)(2,1)S(1)} %pad_maximum_fusion.12), channel_id=1, source_target_pairs={{0,12},{1,13},{2,14},{3,15},{4,8},{5,9},{6,10},{7,11},{8,4},{9,5},... | collective-permute-start | bytes 294920 | tf_op jit(solution)/shard_map/ppermute | solution.py:22
  30.1 7.6 %collective-permute-done.6 = bf16[64,1024]{1,0:T(8,128)(2,1)S(1)} collective-permute-done((bf16[64,1024]{1,0:T(8,128)(2,1)S(1)}, bf16[64,1024]{1,0:T(8,128)(2,1)S(1)}, u32[]{:S(2)}, u32[]{:S(2)}) %collective-permute-start.6) | collective-permute-done | bytes 131104 | tf_op jit(solution)/shard_map/ppermute | solution.py:22
  40.1 1.5 %copy-done.3 = bf16[1,1024,2048]{2,1,0:T(8,128)(2,1)S(1)} copy-done((bf16[1,1024,2048]{2,1,0:T(8,128)(2,1)S(1)}, bf16[1,1024,2048]{2,1,0:T(8,128)(2,1)}, u32[]{:S(2)}) %copy-start.3) | copy-done | bytes 4194328
  41.6 1.8 %add_multiply_fusion = (f32[256,2048]{1,0:T(8,128)S(1)}, bf16[256,2048]{1,0:T(8,128)(2,1)S(1)}) fusion(bf16[256,1024]{1,0:T(8,128)(2,1)S(1)} %multiply_convert_fusion.5, bf16[1,1024,2048]{2,1,0:T(8,128)(2,1)S(1)} %copy-done.3), kind=kOutput, calls=%fused_computation.28 | convolution fusion | flops 1078460416 | bytes 7864320 | tf_op jit(solution)/shard_map/dot_general | solution.py:114
  49.7 1.4 %multiply_convert_fusion = (bf16[256,2048]{1,0:T(8,128)(2,1)S(1)}, f32[256,2048]{1,0:T(8,128)S(1)}) fusion(bf16[256,1024]{1,0:T(8,128)(2,1)S(1)} %multiply_convert_fusion.3, bf16[1,1024,2048]{2,1,0:T(8,128)(2,1)S(1)} %copy-done.3), kind=kOutput, calls=%fused_computation.26 | convolution fusion | flops 1076363264 | bytes 7864320 | tf_op jit(solution)/shard_map/dot_general | solution.py:114
  51.7 2.0 %collective-permute-done.17 = bf16[160,1024]{1,0:T(8,128)(2,1)S(1)} collective-permute-done((bf16[160,1024]{1,0:T(8,128)(2,1)S(1)}, bf16[160,1024]{1,0:T(8,128)(2,1)S(1)}, u32[]{:S(2)}, u32[]{:S(2)}) %collective-permute-start.17) | collective-permute-done | bytes 327712 | tf_op jit(solution)/shard_map/ppermute | solution.py:105
  53.7 1.7 %fusion.20 = bf16[256,2048]{1,0:T(8,128)(2,1)S(1)} fusion(bf16[256,1024]{1,0:T(8,128)(2,1)S(1)} %constant_dynamic-update-slice_fusion.12, bf16[1,1024,2048]{2,1,0:T(8,128)(2,1)S(1)} %copy-done.1, f32[256,2048]{1,0:T(8,128)S(1)} %get-tuple-element.195), kind=kOutput, calls=%fused_computation.18 | convolution fusion | flops 1078460416 | bytes 7864320 | tf_op jit(solution)/shard_map/dot_general | solution.py:204
  55.4 1.5 %multiply_reduce_fusion = (f32[256]{0:T(256)S(1)}, f32[256,1024]{1,0:T(8,128)S(1)}) fusion(f32[256,1024]{1,0:T(8,128)S(1)} %get-tuple-element.191, bf16[256,1024]{1,0:T(8,128)(2,1)S(1)} %constant_dynamic-update-slice_fusion.10, bf16[256,2048]{1,0:T(8,128)(2,1)S(1)} %fusion.20, bf16[1,1024,2048]{2,1,0:T(8,128)(2,1)S(1)} %copy-done.3), kind=kOutput, calls=%fused_computation.41 | convolution fusion | flops 1075838720 | bytes 7865344 | tf_op jit(solution)/shard_map/dot_general | solution.py:206
  58.9 1.5 %collective-permute-done.18 = bf16[256,1024]{1,0:T(8,128)(2,1)S(1)} collective-permute-done((bf16[256,1024]{1,0:T(8,128)(2,1)S(1)}, bf16[256,1024]{1,0:T(8,128)(2,1)S(1)}, u32[]{:S(2)}, u32[]{:S(2)}) %collective-permute-start.18) | collective-permute-done | bytes 524320 | tf_op jit(solution)/shard_map/ppermute | solution.py:22
  62.0 2.6 %fusion.18 = bf16[1,512,2048]{2,1,0:T(8,128)(2,1)} fusion(bf16[256,2048]{1,0:T(8,128)(2,1)S(1)} %fusion.20, bf16[256,2048]{1,0:T(8,128)(2,1)S(1)} %fusion.23, bf16[256,512]{1,0:T(8,128)(2,1)S(1)} %constant_dynamic-slice_fusion.2, bf16[256,512]{1,0:T(8,128)(2,1)S(1)} %constant_dynamic-slice_fusion.3), kind=kOutput, calls=%fused_computation.16 | convolution fusion | flops 1080033280 | bytes 4718592 | tf_op jit(solution)/shard_map/dot_general | solution.py:258
  64.6 4.5 %collective-permute-done.19 = bf16[128,1024]{1,0:T(8,128)(2,1)S(1)} collective-permute-done((bf16[128,1024]{1,0:T(8,128)(2,1)S(1)}, bf16[128,1024]{1,0:T(8,128)(2,1)S(1)}, u32[]{:S(2)}, u32[]{:S(2)}) %collective-permute-start.19) | collective-permute-done | bytes 262176 | tf_op jit(solution)/shard_map/ppermute | solution.py:22
  69.2 2.3 %collective-permute-start.22 = (bf16[32,1024]{1,0:T(8,128)(2,1)S(1)}, bf16[32,1024]{1,0:T(8,128)(2,1)S(1)}, u32[]{:S(2)}, u32[]{:S(2)}) collective-permute-start(bf16[32,1024]{1,0:T(8,128)(2,1)S(1)} %get-tuple-element.147), channel_id=1, source_target_pairs={{0,12},{1,13},{2,14},{3,15},{4,8},{5,9},{6,10},{7,11},{8,4},{9,5},... | collective-permute-start | bytes 196616 | tf_op jit(solution)/shard_map/ppermute | solution.py:22
  73.7 2.6 %fusion.19 = bf16[1,512,2048]{2,1,0:T(8,128)(2,1)} fusion(bf16[256,2048]{1,0:T(8,128)(2,1)S(1)} %get-tuple-element.194, bf16[256,2048]{1,0:T(8,128)(2,1)S(1)} %get-tuple-element.138, bf16[256,512]{1,0:T(8,128)(2,1)S(1)} %constant_dynamic-slice_fusion, bf16[256,512]{1,0:T(8,128)(2,1)S(1)} %constant_dynamic-slice_fusion.1), kind=kOutput, calls=%fused_computation.17 | convolution fusion | flops 1080033280 | bytes 4718592 | tf_op jit(solution)/shard_map/dot_general | solution.py:258
  76.3 1.9 %collective-permute-done.21 = bf16[32,1024]{1,0:T(8,128)(2,1)S(1)} collective-permute-done((bf16[32,1024]{1,0:T(8,128)(2,1)S(1)}, bf16[32,1024]{1,0:T(8,128)(2,1)S(1)}, u32[]{:S(2)}, u32[]{:S(2)}) %collective-permute-start.21) | collective-permute-done | bytes 65568 | tf_op jit(solution)/shard_map/ppermute | solution.py:22
  (98 shorter events, 20.7 us)
Async XLA Ops:
  0.6 37.7 %copy-start = (bf16[1024,1024]{1,0:T(8,128)(2,1)S(1)}, bf16[1024,1024]{1,0:T(8,128)(2,1)}, u32[]{:S(2)}) copy-start(bf16[1024,1024]{1,0:T(8,128)(2,1)} %param.9) | copy-start | bytes 6291460
  3.4 3.2 %collective-permute-start.2 = (bf16[64,1024]{1,0:T(8,128)(2,1)}, bf16[64,1024]{1,0:T(8,128)(2,1)S(1)}, u32[]{:S(2)}, u32[]{:S(2)}) collective-permute-start(bf16[64,1024]{1,0:T(8,128)(2,1)} %get-tuple-element.75), channel_id=1, source_target_pairs={{0,1},{1,0},{2,3},{3,2},{4,5},{5,4},{6,7},{7,6},{8,9},{9,8},{10,11... | collective-permute-start | bytes 393224 | tf_op jit(solution)/shard_map/ppermute | solution.py:22
  3.9 6.8 %collective-permute-start = (bf16[64,1024]{1,0:T(8,128)(2,1)}, bf16[64,1024]{1,0:T(8,128)(2,1)S(1)}, u32[]{:S(2)}, u32[]{:S(2)}) collective-permute-start(bf16[64,1024]{1,0:T(8,128)(2,1)} %get-tuple-element.71), channel_id=1, source_target_pairs={{0,3},{1,2},{2,1},{3,0},{4,7},{5,6},{6,5},{7,4},{8,11},{9,10},{10,... | collective-permute-start | bytes 393224 | tf_op jit(solution)/shard_map/ppermute | solution.py:22
  6.6 7.1 %collective-permute-start.1 = (bf16[64,1024]{1,0:T(8,128)(2,1)}, bf16[64,1024]{1,0:T(8,128)(2,1)S(1)}, u32[]{:S(2)}, u32[]{:S(2)}) collective-permute-start(bf16[64,1024]{1,0:T(8,128)(2,1)} %get-tuple-element.72), channel_id=1, source_target_pairs={{0,2},{1,3},{2,0},{3,1},{4,6},{5,7},{6,4},{7,5},{8,10},{9,11},{10,... | collective-permute-start | bytes 393224 | tf_op jit(solution)/shard_map/ppermute | solution.py:22
  6.6 7.2 %collective-permute-start.3 = (bf16[16,2048]{1,0:T(8,128)(2,1)}, bf16[16,2048]{1,0:T(8,128)(2,1)S(1)}, u32[]{:S(2)}, u32[]{:S(2)}) collective-permute-start(bf16[16,2048]{1,0:T(8,128)(2,1)} %get-tuple-element.77), channel_id=1, source_target_pairs={{0,12},{1,13},{2,14},{3,15},{4,8},{5,9},{6,10},{7,11},{8,4},{9,5},... | collective-permute-start | bytes 196616 | tf_op jit(solution)/shard_map/ppermute | solution.py:22
  10.7 4.5 %collective-permute-start.4 = (bf16[16,2048]{1,0:T(8,128)(2,1)}, bf16[16,2048]{1,0:T(8,128)(2,1)S(1)}, u32[]{:S(2)}, u32[]{:S(2)}) collective-permute-start(bf16[16,2048]{1,0:T(8,128)(2,1)} %get-tuple-element.78), channel_id=1, source_target_pairs={{0,4},{1,5},{2,6},{3,7},{4,0},{5,1},{6,2},{7,3},{8,12},{9,13},{10,... | collective-permute-start | bytes 196616 | tf_op jit(solution)/shard_map/ppermute | solution.py:22
  16.1 5.8 %collective-permute-start.8 = (bf16[64,1024]{1,0:T(8,128)(2,1)S(1)}, bf16[64,1024]{1,0:T(8,128)(2,1)S(1)}, u32[]{:S(2)}, u32[]{:S(2)}) collective-permute-start(bf16[64,1024]{1,0:T(8,128)(2,1)S(1)} %copy-done.6), channel_id=1, source_target_pairs={{0,3},{1,2},{2,1},{3,0},{4,7},{5,6},{6,5},{7,4},{8,11},{9,10},{10,... | collective-permute-start | bytes 393224 | tf_op jit(solution)/shard_map/ppermute | solution.py:22
  16.2 8.6 %collective-permute-start.9 = (bf16[64,1024]{1,0:T(8,128)(2,1)S(1)}, bf16[64,1024]{1,0:T(8,128)(2,1)S(1)}, u32[]{:S(2)}, u32[]{:S(2)}) collective-permute-start(bf16[64,1024]{1,0:T(8,128)(2,1)S(1)} %copy-done.5), channel_id=1, source_target_pairs={{0,2},{1,3},{2,0},{3,1},{4,6},{5,7},{6,4},{7,5},{8,10},{9,11},{10,... | collective-permute-start | bytes 393224 | tf_op jit(solution)/shard_map/ppermute | solution.py:22
  17.7 7.9 %collective-permute-start.10 = (bf16[64,1024]{1,0:T(8,128)(2,1)S(1)}, bf16[64,1024]{1,0:T(8,128)(2,1)S(1)}, u32[]{:S(2)}, u32[]{:S(2)}) collective-permute-start(bf16[64,1024]{1,0:T(8,128)(2,1)S(1)} %copy-done.4), channel_id=1, source_target_pairs={{0,1},{1,0},{2,3},{3,2},{4,5},{5,4},{6,7},{7,6},{8,9},{9,8},{10,11... | collective-permute-start | bytes 393224 | tf_op jit(solution)/shard_map/ppermute | solution.py:22
  18.0 7.7 %collective-permute-start.11 = (bf16[64,1024]{1,0:T(8,128)(2,1)S(1)}, bf16[64,1024]{1,0:T(8,128)(2,1)S(1)}, u32[]{:S(2)}, u32[]{:S(2)}) collective-permute-start(bf16[64,1024]{1,0:T(8,128)(2,1)S(1)} %pad_maximum_fusion.5), channel_id=1, source_target_pairs={{0,16},{16,0},{1,17},{17,1},{2,18},{18,2},{3,19},{19,3},{4,20},{20... | collective-permute-start | bytes 393224 | tf_op jit(solution)/shard_map/ppermute | solution.py:105
  19.6 9.7 %collective-permute-start.5 = (bf16[48,1024]{1,0:T(8,128)(2,1)S(1)}, bf16[48,1024]{1,0:T(8,128)(2,1)S(1)}, u32[]{:S(2)}, u32[]{:S(2)}) collective-permute-start(bf16[48,1024]{1,0:T(8,128)(2,1)S(1)} %pad_maximum_fusion.9), channel_id=1, source_target_pairs={{0,12},{1,13},{2,14},{3,15},{4,8},{5,9},{6,10},{7,11},{8,4},{9,5},... | collective-permute-start | bytes 294920 | tf_op jit(solution)/shard_map/ppermute | solution.py:22
  21.9 15.8 %collective-permute-start.6 = (bf16[64,1024]{1,0:T(8,128)(2,1)S(1)}, bf16[64,1024]{1,0:T(8,128)(2,1)S(1)}, u32[]{:S(2)}, u32[]{:S(2)}) collective-permute-start(bf16[64,1024]{1,0:T(8,128)(2,1)S(1)} %pad_maximum_fusion.7), channel_id=1, source_target_pairs={{0,8},{1,9},{2,10},{3,11},{4,12},{5,13},{6,14},{7,15},{8,0},{9,1},... | collective-permute-start | bytes 393224 | tf_op jit(solution)/shard_map/ppermute | solution.py:22
  24.8 5.4 %collective-permute-start.7 = (bf16[48,1024]{1,0:T(8,128)(2,1)S(1)}, bf16[48,1024]{1,0:T(8,128)(2,1)S(1)}, u32[]{:S(2)}, u32[]{:S(2)}) collective-permute-start(bf16[48,1024]{1,0:T(8,128)(2,1)S(1)} %pad_maximum_fusion.10), channel_id=1, source_target_pairs={{0,4},{1,5},{2,6},{3,7},{4,0},{5,1},{6,2},{7,3},{8,12},{9,13},{10,... | collective-permute-start | bytes 294920 | tf_op jit(solution)/shard_map/ppermute | solution.py:22
  25.8 11.9 %collective-permute-start.12 = (bf16[128,1024]{1,0:T(8,128)(2,1)S(1)}, bf16[128,1024]{1,0:T(8,128)(2,1)S(1)}, u32[]{:S(2)}, u32[]{:S(2)}) collective-permute-start(bf16[128,1024]{1,0:T(8,128)(2,1)S(1)} %slice_dynamic-update-slice_fusion.1), channel_id=1, source_target_pairs={{0,16},{16,0},{1,17},{17,1},{2,18},{18,2},{3,19},{19,3},{4,20},{20... | collective-permute-start | bytes 786440 | tf_op jit(solution)/shard_map/ppermute | solution.py:105
  27.4 16.1 %collective-permute-start.14 = (bf16[48,1024]{1,0:T(8,128)(2,1)S(1)}, bf16[48,1024]{1,0:T(8,128)(2,1)S(1)}, u32[]{:S(2)}, u32[]{:S(2)}) collective-permute-start(bf16[48,1024]{1,0:T(8,128)(2,1)S(1)} %pad_maximum_fusion.12), channel_id=1, source_target_pairs={{0,12},{1,13},{2,14},{3,15},{4,8},{5,9},{6,10},{7,11},{8,4},{9,5},... | collective-permute-start | bytes 294920 | tf_op jit(solution)/shard_map/ppermute | solution.py:22
  29.3 14.2 %collective-permute-start.15 = (bf16[64,1024]{1,0:T(8,128)(2,1)S(1)}, bf16[64,1024]{1,0:T(8,128)(2,1)S(1)}, u32[]{:S(2)}, u32[]{:S(2)}) collective-permute-start(bf16[64,1024]{1,0:T(8,128)(2,1)S(1)} %pad_maximum_fusion.8), channel_id=1, source_target_pairs={{0,8},{1,9},{2,10},{3,11},{4,12},{5,13},{6,14},{7,15},{8,0},{9,1},... | collective-permute-start | bytes 393224 | tf_op jit(solution)/shard_map/ppermute | solution.py:22
  37.7 6.3 %collective-permute-start.16 = (bf16[48,1024]{1,0:T(8,128)(2,1)S(1)}, bf16[48,1024]{1,0:T(8,128)(2,1)S(1)}, u32[]{:S(2)}, u32[]{:S(2)}) collective-permute-start(bf16[48,1024]{1,0:T(8,128)(2,1)S(1)} %pad_maximum_fusion.11), channel_id=1, source_target_pairs={{0,4},{1,5},{2,6},{3,7},{4,0},{5,1},{6,2},{7,3},{8,12},{9,13},{10,... | collective-permute-start | bytes 294920 | tf_op jit(solution)/shard_map/ppermute | solution.py:22
  37.8 10.5 %collective-permute-start.13 = (bf16[160,1024]{1,0:T(8,128)(2,1)S(1)}, bf16[160,1024]{1,0:T(8,128)(2,1)S(1)}, u32[]{:S(2)}, u32[]{:S(2)}) collective-permute-start(bf16[160,1024]{1,0:T(8,128)(2,1)S(1)} %pad_maximum_fusion.1), channel_id=1, source_target_pairs={{0,16},{16,0},{1,17},{17,1},{2,18},{18,2},{3,19},{19,3},{4,20},{20... | collective-permute-start | bytes 983048 | tf_op jit(solution)/shard_map/ppermute | solution.py:105
  44.1 9.5 %collective-permute-start.17 = (bf16[160,1024]{1,0:T(8,128)(2,1)S(1)}, bf16[160,1024]{1,0:T(8,128)(2,1)S(1)}, u32[]{:S(2)}, u32[]{:S(2)}) collective-permute-start(bf16[160,1024]{1,0:T(8,128)(2,1)S(1)} %pad_maximum_fusion.2), channel_id=1, source_target_pairs={{0,16},{16,0},{1,17},{17,1},{2,18},{18,2},{3,19},{19,3},{4,20},{20... | collective-permute-start | bytes 983048 | tf_op jit(solution)/shard_map/ppermute | solution.py:105
  58.4 2.0 %collective-permute-start.18 = (bf16[256,1024]{1,0:T(8,128)(2,1)S(1)}, bf16[256,1024]{1,0:T(8,128)(2,1)S(1)}, u32[]{:S(2)}, u32[]{:S(2)}) collective-permute-start(bf16[256,1024]{1,0:T(8,128)(2,1)S(1)} %fusion.35), channel_id=1, source_target_pairs={{0,1},{1,0},{2,3},{3,2},{4,5},{5,4},{6,7},{7,6},{8,9},{9,8},{10,11... | collective-permute-start | bytes 1572872 | tf_op jit(solution)/shard_map/ppermute | solution.py:22
  60.7 8.4 %collective-permute-start.19 = (bf16[128,1024]{1,0:T(8,128)(2,1)S(1)}, bf16[128,1024]{1,0:T(8,128)(2,1)S(1)}, u32[]{:S(2)}, u32[]{:S(2)}) collective-permute-start(bf16[128,1024]{1,0:T(8,128)(2,1)S(1)} %slice.207), channel_id=1, source_target_pairs={{0,2},{1,3},{2,0},{3,1},{4,6},{5,7},{6,4},{7,5},{8,10},{9,11},{10,... | collective-permute-start | bytes 786440 | tf_op jit(solution)/shard_map/ppermute | solution.py:22
  69.2 7.0 %collective-permute-start.22 = (bf16[32,1024]{1,0:T(8,128)(2,1)S(1)}, bf16[32,1024]{1,0:T(8,128)(2,1)S(1)}, u32[]{:S(2)}, u32[]{:S(2)}) collective-permute-start(bf16[32,1024]{1,0:T(8,128)(2,1)S(1)} %get-tuple-element.147), channel_id=1, source_target_pairs={{0,12},{1,13},{2,14},{3,15},{4,8},{5,9},{6,10},{7,11},{8,4},{9,5},... | collective-permute-start | bytes 196616 | tf_op jit(solution)/shard_map/ppermute | solution.py:22
  71.6 6.6 %collective-permute-start.21 = (bf16[32,1024]{1,0:T(8,128)(2,1)S(1)}, bf16[32,1024]{1,0:T(8,128)(2,1)S(1)}, u32[]{:S(2)}, u32[]{:S(2)}) collective-permute-start(bf16[32,1024]{1,0:T(8,128)(2,1)S(1)} %get-tuple-element.148), channel_id=1, source_target_pairs={{0,8},{1,9},{2,10},{3,11},{4,12},{5,13},{6,14},{7,15},{8,0},{9,1},... | collective-permute-start | bytes 196616 | tf_op jit(solution)/shard_map/ppermute | solution.py:22
  72.5 5.8 %collective-permute-start.20 = (bf16[32,1024]{1,0:T(8,128)(2,1)S(1)}, bf16[32,1024]{1,0:T(8,128)(2,1)S(1)}, u32[]{:S(2)}, u32[]{:S(2)}) collective-permute-start(bf16[32,1024]{1,0:T(8,128)(2,1)S(1)} %get-tuple-element.146), channel_id=1, source_target_pairs={{0,4},{1,5},{2,6},{3,7},{4,0},{5,1},{6,2},{7,3},{8,12},{9,13},{10,... | collective-permute-start | bytes 196616 | tf_op jit(solution)/shard_map/ppermute | solution.py:22
  (6 other events, 64.1 us)

commit v3 on v2

--- a/solution.py
+++ b/solution.py
@@ -154,16 +154,15 @@
     grads_near = send_near(grads_placed)
     cells_far = send_far(cells_far)
     direct_cells, direct_grads = direct[:, :model_width], direct[:, model_width:]
-    grads_near, cells_first_copies = fence((grads_near, cells_first_copies))
     grads_first = here_and_near(here[1], grads_near)
+    second_copies = copies(stack(grads_first, direct_cells, direct_grads))
     grads_far = far_pieces(here[1], grads_near)
-    second_copies = copies(stack(grads_first, direct_cells, direct_grads))
-    *grads_far, grads_last = send_far(grads_far[:-1]) + grads_far[-1:]
+    cells_far[:-1], grads_far = fence((cells_far[:-1], grads_far))
+    grads_far = send_far(grads_far)
     came = (cells_first_copies, second_copies)
-    cells_far, came, grads_last = fence((cells_far, came, grads_last))
-    cells_far, came, grads_last = fence((stack(*cells_far), came, grads_last))
+    cells_far, came = fence((cells_far, came))
+    cells_far, came = fence((stack(*cells_far), came))
     cells_far_copies = copies(cells_far)
-    grads_far += [swap(grads_last, low)]
     features = stack(cells_first, direct_cells, cells_far)
     first_rows, direct_rows = cells_first.shape[0], direct.shape[0]
     early = [

time: 79.1 us -> 79.8 us (level)
  starting transfers between devices: 26.9 us -> 27.9 us
  waiting for transfers between devices: 24.2 us -> 23.4 us
    ppermute x19, waiting for transfers between devices: 22.2 us -> 17.4 us  [swap(): return lax.ppermute(piece, 'expert', pairs)]
    ppermute x4, waiting for transfers between devices: 1.97 us -> 6.06 us  [copies(): pieces.append(lax.ppermute(rows, 'dp', ring))]
    ppermute x19, starting transfers between devices: 22.2 us -> 23.6 us  [swap(): return lax.ppermute(piece, 'expert', pairs)]
  transfers between devices with their start and end apart: 23 -> 23, of which waited for: 11 -> 10; matrix products, arithmetic and copies ran while one was open for 20% -> 20% of each run, Pallas kernels for 0% -> 0%
where the time goes in v3:
time: 79.8 us; the launch traced here: 79.5 us
  starting transfers between devices  27.9 us (35%)
  waiting for transfers between devices  23.4 us (29%)
  matrix products  18.8 us (24%)
  local copies, waits for them, and re-layouts  3.07 us (4%)
  Pallas kernels  2.75 us (3%)
  other arithmetic  2.54 us (3%)
  between operations  1.09 us (1%)
    ppermute x19, starting transfers between devices, swap(): return lax.ppermute(piece, 'expert', pairs)  23.6 us
    ppermute x19, waiting for transfers between devices, swap(): return lax.ppermute(piece, 'expert', pairs)  17.4 us
    ppermute x4, waiting for transfers between devices, copies(): pieces.append(lax.ppermute(rows, 'dp', ring))  6.06 us
    dot_general x2, matrix products, rows_product(): lax.dot_general(jnp.concatenate(left, axis=0), jnp.concatenate(right, axi...  5.21 us
    ppermute x4, starting transfers between devices, copies(): pieces.append(lax.ppermute(rows, 'dp', ring))  4.25 us
    dot_general x2, matrix products, forward(): pre_exp = jnp.dot(norm_rows, w_up, preferred_element_type=jnp.float32)  3.2 us
    dot_general x2, matrix products, backward(): act_grad = jnp.dot(grad_rows, w_down, preferred_element_type=jnp.float32)  2.96 us
    dot_general x2, matrix products, backward(): lax.dot_general(pre_grad, w_up, contract_last, preferred_element_type=jnp...  2.9 us
  transfers between devices with their start and end apart: 23, of which 10 were waited for; matrix products, arithmetic and copies ran while one was open for 20% of the time, Pallas kernels for 0%

profile of v3, /device:TPU:0, one launch (start us, length us, event | category | flops | bytes accessed | tf_op | source)
XLA Modules:
  0.0 79.5 jit_solution(6031481339088934560)
XLA Ops:
  0.6 2.7 %shard_map.85 = (bf16[64,1024]{1,0:T(8,128)(2,1)}, bf16[64,1024]{1,0:T(8,128)(2,1)}, bf16[64,1024]{1,0:T(8,128)(2,1)}, bf16[64,1024]{1,0:T(8,128)(2,1)}, bf16[64...) custom-call(s32[1]{0:T(128)} %bitcast.me_ref, ...), custom_call_target="tpu_custom_call" | custom-call | tf_op jit(solution)/shard_map/pallas_call | solution.py:85
  3.9 2.6 %collective-permute-start = (bf16[64,1024]{1,0:T(8,128)(2,1)}, bf16[64,1024]{1,0:T(8,128)(2,1)S(1)}, u32[]{:S(2)}, u32[]{:S(2)}) collective-permute-start(bf16[64,1024]{1,0:T(8,128)(2,1)} %get-tuple-element.70), channel_id=1, source_target_pairs={{0,3},{1,2},{2,1},{3,0},{4,7},{5,6},{6,5},{7,4},{8,11},{9,10},{10,... | collective-permute-start | bytes 393224 | tf_op jit(solution)/shard_map/ppermute | solution.py:22
  6.6 4.1 %collective-permute-start.3 = (bf16[16,2048]{1,0:T(8,128)(2,1)}, bf16[16,2048]{1,0:T(8,128)(2,1)S(1)}, u32[]{:S(2)}, u32[]{:S(2)}) collective-permute-start(bf16[16,2048]{1,0:T(8,128)(2,1)} %get-tuple-element.76), channel_id=1, source_target_pairs={{0,12},{1,13},{2,14},{3,15},{4,8},{5,9},{6,10},{7,11},{8,4},{9,5},... | collective-permute-start | bytes 196616 | tf_op jit(solution)/shard_map/ppermute | solution.py:22
  10.7 2.9 %collective-permute-done.1 = bf16[64,1024]{1,0:T(8,128)(2,1)S(1)} collective-permute-done((bf16[64,1024]{1,0:T(8,128)(2,1)}, bf16[64,1024]{1,0:T(8,128)(2,1)S(1)}, u32[]{:S(2)}, u32[]{:S(2)}) %collective-permute-start.1) | collective-permute-done | bytes 131104 | tf_op jit(solution)/shard_map/ppermute | solution.py:22
  16.1 2.3 %collective-permute-start.5 = (bf16[48,1024]{1,0:T(8,128)(2,1)S(1)}, bf16[48,1024]{1,0:T(8,128)(2,1)S(1)}, u32[]{:S(2)}, u32[]{:S(2)}) collective-permute-start(bf16[48,1024]{1,0:T(8,128)(2,1)S(1)} %pad_maximum_fusion.9), channel_id=1, source_target_pairs={{0,12},{1,13},{2,14},{3,15},{4,8},{5,9},{6,10},{7,11},{8,4},{9,5},... | collective-permute-start | bytes 294920 | tf_op jit(solution)/shard_map/ppermute | solution.py:22
  20.4 3.9 %collective-permute-done.7 = bf16[64,1024]{1,0:T(8,128)(2,1)S(1)} collective-permute-done((bf16[64,1024]{1,0:T(8,128)(2,1)S(1)}, bf16[64,1024]{1,0:T(8,128)(2,1)S(1)}, u32[]{:S(2)}, u32[]{:S(2)}) %collective-permute-start.7) | collective-permute-done | bytes 131104 | tf_op jit(solution)/shard_map/ppermute | solution.py:22
  24.3 2.0 %collective-permute-start.10 = (bf16[48,1024]{1,0:T(8,128)(2,1)S(1)}, bf16[48,1024]{1,0:T(8,128)(2,1)S(1)}, u32[]{:S(2)}, u32[]{:S(2)}) collective-permute-start(bf16[48,1024]{1,0:T(8,128)(2,1)S(1)} %pad_maximum_fusion.10), channel_id=1, source_target_pairs={{0,4},{1,5},{2,6},{3,7},{4,0},{5,1},{6,2},{7,3},{8,12},{9,13},{10,... | collective-permute-start | bytes 294920 | tf_op jit(solution)/shard_map/ppermute | solution.py:22
  27.1 1.5 %collective-permute-start.11 = (bf16[64,1024]{1,0:T(8,128)(2,1)S(1)}, bf16[64,1024]{1,0:T(8,128)(2,1)S(1)}, u32[]{:S(2)}, u32[]{:S(2)}) collective-permute-start(bf16[64,1024]{1,0:T(8,128)(2,1)S(1)} %pad_maximum_fusion.5), channel_id=1, source_target_pairs={{0,16},{16,0},{1,17},{17,1},{2,18},{18,2},{3,19},{19,3},{4,20},{20... | collective-permute-start | bytes 393224 | tf_op jit(solution)/shard_map/ppermute | solution.py:105
  29.4 1.9 %collective-permute-start.14 = (bf16[48,1024]{1,0:T(8,128)(2,1)S(1)}, bf16[48,1024]{1,0:T(8,128)(2,1)S(1)}, u32[]{:S(2)}, u32[]{:S(2)}) collective-permute-start(bf16[48,1024]{1,0:T(8,128)(2,1)S(1)} %pad_maximum_fusion.11), channel_id=1, source_target_pairs={{0,12},{1,13},{2,14},{3,15},{4,8},{5,9},{6,10},{7,11},{8,4},{9,5},... | collective-permute-start | bytes 294920 | tf_op jit(solution)/shard_map/ppermute | solution.py:22
  31.3 1.7 %collective-permute-start.15 = (bf16[64,1024]{1,0:T(8,128)(2,1)S(1)}, bf16[64,1024]{1,0:T(8,128)(2,1)S(1)}, u32[]{:S(2)}, u32[]{:S(2)}) collective-permute-start(bf16[64,1024]{1,0:T(8,128)(2,1)S(1)} %pad_maximum_fusion.8), channel_id=1, source_target_pairs={{0,8},{1,9},{2,10},{3,11},{4,12},{5,13},{6,14},{7,15},{8,0},{9,1},... | collective-permute-start | bytes 393224 | tf_op jit(solution)/shard_map/ppermute | solution.py:22
  33.9 4.4 %collective-permute-done.12 = bf16[128,1024]{1,0:T(8,128)(2,1)S(1)} collective-permute-done((bf16[128,1024]{1,0:T(8,128)(2,1)S(1)}, bf16[128,1024]{1,0:T(8,128)(2,1)S(1)}, u32[]{:S(2)}, u32[]{:S(2)}) %collective-permute-start.12) | collective-permute-done | bytes 262176 | tf_op jit(solution)/shard_map/ppermute | solution.py:105
  38.3 1.6 %collective-permute-start.13 = (bf16[160,1024]{1,0:T(8,128)(2,1)S(1)}, bf16[160,1024]{1,0:T(8,128)(2,1)S(1)}, u32[]{:S(2)}, u32[]{:S(2)}) collective-permute-start(bf16[160,1024]{1,0:T(8,128)(2,1)S(1)} %pad_maximum_fusion.1), channel_id=1, source_target_pairs={{0,16},{16,0},{1,17},{17,1},{2,18},{18,2},{3,19},{19,3},{4,20},{20... | collective-permute-start | bytes 983048 | tf_op jit(solution)/shard_map/ppermute | solution.py:105
  42.1 1.8 %add_multiply_fusion = (f32[256,2048]{1,0:T(8,128)S(1)}, bf16[256,2048]{1,0:T(8,128)(2,1)S(1)}) fusion(bf16[256,1024]{1,0:T(8,128)(2,1)S(1)} %multiply_convert_fusion.5, bf16[1,1024,2048]{2,1,0:T(8,128)(2,1)S(1)} %copy-done.3), kind=kOutput, calls=%fused_computation.28 | convolution fusion | flops 1078460416 | bytes 7864320 | tf_op jit(solution)/shard_map/dot_general | solution.py:114
  50.6 1.4 %multiply_convert_fusion = (bf16[256,2048]{1,0:T(8,128)(2,1)S(1)}, f32[256,2048]{1,0:T(8,128)S(1)}) fusion(bf16[256,1024]{1,0:T(8,128)(2,1)S(1)} %multiply_convert_fusion.3, bf16[1,1024,2048]{2,1,0:T(8,128)(2,1)S(1)} %copy-done.3), kind=kOutput, calls=%fused_computation.26 | convolution fusion | flops 1076363264 | bytes 7864320 | tf_op jit(solution)/shard_map/dot_general | solution.py:114
  52.6 1.7 %collective-permute-done.17 = bf16[160,1024]{1,0:T(8,128)(2,1)S(1)} collective-permute-done((bf16[160,1024]{1,0:T(8,128)(2,1)S(1)}, bf16[160,1024]{1,0:T(8,128)(2,1)S(1)}, u32[]{:S(2)}, u32[]{:S(2)}) %collective-permute-start.17) | collective-permute-done | bytes 327712 | tf_op jit(solution)/shard_map/ppermute | solution.py:105
  54.2 1.7 %fusion.20 = bf16[256,2048]{1,0:T(8,128)(2,1)S(1)} fusion(bf16[256,1024]{1,0:T(8,128)(2,1)S(1)} %constant_dynamic-update-slice_fusion.12, bf16[1,1024,2048]{2,1,0:T(8,128)(2,1)S(1)} %copy-done.1, f32[256,2048]{1,0:T(8,128)S(1)} %get-tuple-element.193), kind=kOutput, calls=%fused_computation.18 | convolution fusion | flops 1078460416 | bytes 7864320 | tf_op jit(solution)/shard_map/dot_general | solution.py:203
  55.9 1.5 %multiply_reduce_fusion = (f32[256]{0:T(256)S(1)}, f32[256,1024]{1,0:T(8,128)S(1)}) fusion(f32[256,1024]{1,0:T(8,128)S(1)} %get-tuple-element.189, bf16[256,1024]{1,0:T(8,128)(2,1)S(1)} %constant_dynamic-update-slice_fusion.10, bf16[256,2048]{1,0:T(8,128)(2,1)S(1)} %fusion.20, bf16[1,1024,2048]{2,1,0:T(8,128)(2,1)S(1)} %copy-done.3), kind=kOutput, calls=%fused_computation.41 | convolution fusion | flops 1075838720 | bytes 7865344 | tf_op jit(solution)/shard_map/dot_general | solution.py:205
  59.4 1.5 %collective-permute-done.18 = bf16[256,1024]{1,0:T(8,128)(2,1)S(1)} collective-permute-done((bf16[256,1024]{1,0:T(8,128)(2,1)S(1)}, bf16[256,1024]{1,0:T(8,128)(2,1)S(1)}, u32[]{:S(2)}, u32[]{:S(2)}) %collective-permute-start.18) | collective-permute-done | bytes 524320 | tf_op jit(solution)/shard_map/ppermute | solution.py:22
  62.3 2.6 %fusion.18 = bf16[1,512,2048]{2,1,0:T(8,128)(2,1)} fusion(bf16[256,2048]{1,0:T(8,128)(2,1)S(1)} %fusion.20, bf16[256,2048]{1,0:T(8,128)(2,1)S(1)} %fusion.23, bf16[256,512]{1,0:T(8,128)(2,1)S(1)} %constant_dynamic-slice_fusion.2, bf16[256,512]{1,0:T(8,128)(2,1)S(1)} %constant_dynamic-slice_fusion.3), kind=kOutput, calls=%fused_computation.16 | convolution fusion | flops 1080033280 | bytes 4718592 | tf_op jit(solution)/shard_map/dot_general | solution.py:257
  64.9 4.7 %collective-permute-done.19 = bf16[128,1024]{1,0:T(8,128)(2,1)S(1)} collective-permute-done((bf16[128,1024]{1,0:T(8,128)(2,1)S(1)}, bf16[128,1024]{1,0:T(8,128)(2,1)S(1)}, u32[]{:S(2)}, u32[]{:S(2)}) %collective-permute-start.19) | collective-permute-done | bytes 262176 | tf_op jit(solution)/shard_map/ppermute | solution.py:22
  69.8 1.9 %collective-permute-start.22 = (bf16[32,1024]{1,0:T(8,128)(2,1)S(1)}, bf16[32,1024]{1,0:T(8,128)(2,1)S(1)}, u32[]{:S(2)}, u32[]{:S(2)}) collective-permute-start(bf16[32,1024]{1,0:T(8,128)(2,1)S(1)} %get-tuple-element.145), channel_id=1, source_target_pairs={{0,12},{1,13},{2,14},{3,15},{4,8},{5,9},{6,10},{7,11},{8,4},{9,5},... | collective-permute-start | bytes 196616 | tf_op jit(solution)/shard_map/ppermute | solution.py:22
  71.6 1.7 %collective-permute-start.21 = (bf16[32,1024]{1,0:T(8,128)(2,1)S(1)}, bf16[32,1024]{1,0:T(8,128)(2,1)S(1)}, u32[]{:S(2)}, u32[]{:S(2)}) collective-permute-start(bf16[32,1024]{1,0:T(8,128)(2,1)S(1)} %get-tuple-element.146), channel_id=1, source_target_pairs={{0,8},{1,9},{2,10},{3,11},{4,12},{5,13},{6,14},{7,15},{8,0},{9,1},... | collective-permute-start | bytes 196616 | tf_op jit(solution)/shard_map/ppermute | solution.py:22
  74.2 2.6 %fusion.19 = bf16[1,512,2048]{2,1,0:T(8,128)(2,1)} fusion(bf16[256,2048]{1,0:T(8,128)(2,1)S(1)} %get-tuple-element.192, bf16[256,2048]{1,0:T(8,128)(2,1)S(1)} %get-tuple-element.136, bf16[256,512]{1,0:T(8,128)(2,1)S(1)} %constant_dynamic-slice_fusion, bf16[256,512]{1,0:T(8,128)(2,1)S(1)} %constant_dynamic-slice_fusion.1), kind=kOutput, calls=%fused_computation.17 | convolution fusion | flops 1080033280 | bytes 4718592 | tf_op jit(solution)/shard_map/dot_general | solution.py:257
  76.8 2.0 %collective-permute-done.21 = bf16[32,1024]{1,0:T(8,128)(2,1)S(1)} collective-permute-done((bf16[32,1024]{1,0:T(8,128)(2,1)S(1)}, bf16[32,1024]{1,0:T(8,128)(2,1)S(1)}, u32[]{:S(2)}, u32[]{:S(2)}) %collective-permute-start.21) | collective-permute-done | bytes 65568 | tf_op jit(solution)/shard_map/ppermute | solution.py:22
  (98 shorter events, 21.9 us)
Async XLA Ops:
  0.6 39.2 %copy-start = (bf16[1024,1024]{1,0:T(8,128)(2,1)S(1)}, bf16[1024,1024]{1,0:T(8,128)(2,1)}, u32[]{:S(2)}) copy-start(bf16[1024,1024]{1,0:T(8,128)(2,1)} %param.9) | copy-start | bytes 6291460
  3.4 3.2 %collective-permute-start.2 = (bf16[64,1024]{1,0:T(8,128)(2,1)}, bf16[64,1024]{1,0:T(8,128)(2,1)S(1)}, u32[]{:S(2)}, u32[]{:S(2)}) collective-permute-start(bf16[64,1024]{1,0:T(8,128)(2,1)} %get-tuple-element.74), channel_id=1, source_target_pairs={{0,1},{1,0},{2,3},{3,2},{4,5},{5,4},{6,7},{7,6},{8,9},{9,8},{10,11... | collective-permute-start | bytes 393224 | tf_op jit(solution)/shard_map/ppermute | solution.py:22
  3.9 6.8 %collective-permute-start = (bf16[64,1024]{1,0:T(8,128)(2,1)}, bf16[64,1024]{1,0:T(8,128)(2,1)S(1)}, u32[]{:S(2)}, u32[]{:S(2)}) collective-permute-start(bf16[64,1024]{1,0:T(8,128)(2,1)} %get-tuple-element.70), channel_id=1, source_target_pairs={{0,3},{1,2},{2,1},{3,0},{4,7},{5,6},{6,5},{7,4},{8,11},{9,10},{10,... | collective-permute-start | bytes 393224 | tf_op jit(solution)/shard_map/ppermute | solution.py:22
  6.6 7.1 %collective-permute-start.1 = (bf16[64,1024]{1,0:T(8,128)(2,1)}, bf16[64,1024]{1,0:T(8,128)(2,1)S(1)}, u32[]{:S(2)}, u32[]{:S(2)}) collective-permute-start(bf16[64,1024]{1,0:T(8,128)(2,1)} %get-tuple-element.71), channel_id=1, source_target_pairs={{0,2},{1,3},{2,0},{3,1},{4,6},{5,7},{6,4},{7,5},{8,10},{9,11},{10,... | collective-permute-start | bytes 393224 | tf_op jit(solution)/shard_map/ppermute | solution.py:22
  6.6 7.2 %collective-permute-start.3 = (bf16[16,2048]{1,0:T(8,128)(2,1)}, bf16[16,2048]{1,0:T(8,128)(2,1)S(1)}, u32[]{:S(2)}, u32[]{:S(2)}) collective-permute-start(bf16[16,2048]{1,0:T(8,128)(2,1)} %get-tuple-element.76), channel_id=1, source_target_pairs={{0,12},{1,13},{2,14},{3,15},{4,8},{5,9},{6,10},{7,11},{8,4},{9,5},... | collective-permute-start | bytes 196616 | tf_op jit(solution)/shard_map/ppermute | solution.py:22
  10.7 4.5 %collective-permute-start.4 = (bf16[16,2048]{1,0:T(8,128)(2,1)}, bf16[16,2048]{1,0:T(8,128)(2,1)S(1)}, u32[]{:S(2)}, u32[]{:S(2)}) collective-permute-start(bf16[16,2048]{1,0:T(8,128)(2,1)} %get-tuple-element.77), channel_id=1, source_target_pairs={{0,4},{1,5},{2,6},{3,7},{4,0},{5,1},{6,2},{7,3},{8,12},{9,13},{10,... | collective-permute-start | bytes 196616 | tf_op jit(solution)/shard_map/ppermute | solution.py:22
  16.1 13.3 %collective-permute-start.5 = (bf16[48,1024]{1,0:T(8,128)(2,1)S(1)}, bf16[48,1024]{1,0:T(8,128)(2,1)S(1)}, u32[]{:S(2)}, u32[]{:S(2)}) collective-permute-start(bf16[48,1024]{1,0:T(8,128)(2,1)S(1)} %pad_maximum_fusion.9), channel_id=1, source_target_pairs={{0,12},{1,13},{2,14},{3,15},{4,8},{5,9},{6,10},{7,11},{8,4},{9,5},... | collective-permute-start | bytes 294920 | tf_op jit(solution)/shard_map/ppermute | solution.py:22
  18.4 11.0 %collective-permute-start.6 = (bf16[64,1024]{1,0:T(8,128)(2,1)S(1)}, bf16[64,1024]{1,0:T(8,128)(2,1)S(1)}, u32[]{:S(2)}, u32[]{:S(2)}) collective-permute-start(bf16[64,1024]{1,0:T(8,128)(2,1)S(1)} %pad_maximum_fusion.7), channel_id=1, source_target_pairs={{0,8},{1,9},{2,10},{3,11},{4,12},{5,13},{6,14},{7,15},{8,0},{9,1},... | collective-permute-start | bytes 393224 | tf_op jit(solution)/shard_map/ppermute | solution.py:22
  18.5 5.8 %collective-permute-start.7 = (bf16[64,1024]{1,0:T(8,128)(2,1)S(1)}, bf16[64,1024]{1,0:T(8,128)(2,1)S(1)}, u32[]{:S(2)}, u32[]{:S(2)}) collective-permute-start(bf16[64,1024]{1,0:T(8,128)(2,1)S(1)} %copy-done.6), channel_id=1, source_target_pairs={{0,3},{1,2},{2,1},{3,0},{4,7},{5,6},{6,5},{7,4},{8,11},{9,10},{10,... | collective-permute-start | bytes 393224 | tf_op jit(solution)/shard_map/ppermute | solution.py:22
  18.8 8.4 %collective-permute-start.8 = (bf16[64,1024]{1,0:T(8,128)(2,1)S(1)}, bf16[64,1024]{1,0:T(8,128)(2,1)S(1)}, u32[]{:S(2)}, u32[]{:S(2)}) collective-permute-start(bf16[64,1024]{1,0:T(8,128)(2,1)S(1)} %copy-done.5), channel_id=1, source_target_pairs={{0,2},{1,3},{2,0},{3,1},{4,6},{5,7},{6,4},{7,5},{8,10},{9,11},{10,... | collective-permute-start | bytes 393224 | tf_op jit(solution)/shard_map/ppermute | solution.py:22
  20.1 8.6 %collective-permute-start.9 = (bf16[64,1024]{1,0:T(8,128)(2,1)S(1)}, bf16[64,1024]{1,0:T(8,128)(2,1)S(1)}, u32[]{:S(2)}, u32[]{:S(2)}) collective-permute-start(bf16[64,1024]{1,0:T(8,128)(2,1)S(1)} %copy-done.4), channel_id=1, source_target_pairs={{0,1},{1,0},{2,3},{3,2},{4,5},{5,4},{6,7},{7,6},{8,9},{9,8},{10,11... | collective-permute-start | bytes 393224 | tf_op jit(solution)/shard_map/ppermute | solution.py:22
  24.3 8.6 %collective-permute-start.10 = (bf16[48,1024]{1,0:T(8,128)(2,1)S(1)}, bf16[48,1024]{1,0:T(8,128)(2,1)S(1)}, u32[]{:S(2)}, u32[]{:S(2)}) collective-permute-start(bf16[48,1024]{1,0:T(8,128)(2,1)S(1)} %pad_maximum_fusion.10), channel_id=1, source_target_pairs={{0,4},{1,5},{2,6},{3,7},{4,0},{5,1},{6,2},{7,3},{8,12},{9,13},{10,... | collective-permute-start | bytes 294920 | tf_op jit(solution)/shard_map/ppermute | solution.py:22
  27.1 6.7 %collective-permute-start.11 = (bf16[64,1024]{1,0:T(8,128)(2,1)S(1)}, bf16[64,1024]{1,0:T(8,128)(2,1)S(1)}, u32[]{:S(2)}, u32[]{:S(2)}) collective-permute-start(bf16[64,1024]{1,0:T(8,128)(2,1)S(1)} %pad_maximum_fusion.5), channel_id=1, source_target_pairs={{0,16},{16,0},{1,17},{17,1},{2,18},{18,2},{3,19},{19,3},{4,20},{20... | collective-permute-start | bytes 393224 | tf_op jit(solution)/shard_map/ppermute | solution.py:105
  28.8 9.5 %collective-permute-start.12 = (bf16[128,1024]{1,0:T(8,128)(2,1)S(1)}, bf16[128,1024]{1,0:T(8,128)(2,1)S(1)}, u32[]{:S(2)}, u32[]{:S(2)}) collective-permute-start(bf16[128,1024]{1,0:T(8,128)(2,1)S(1)} %slice_dynamic-update-slice_fusion.1), channel_id=1, source_target_pairs={{0,16},{16,0},{1,17},{17,1},{2,18},{18,2},{3,19},{19,3},{4,20},{20... | collective-permute-start | bytes 786440 | tf_op jit(solution)/shard_map/ppermute | solution.py:105
  29.4 14.5 %collective-permute-start.14 = (bf16[48,1024]{1,0:T(8,128)(2,1)S(1)}, bf16[48,1024]{1,0:T(8,128)(2,1)S(1)}, u32[]{:S(2)}, u32[]{:S(2)}) collective-permute-start(bf16[48,1024]{1,0:T(8,128)(2,1)S(1)} %pad_maximum_fusion.11), channel_id=1, source_target_pairs={{0,12},{1,13},{2,14},{3,15},{4,8},{5,9},{6,10},{7,11},{8,4},{9,5},... | collective-permute-start | bytes 294920 | tf_op jit(solution)/shard_map/ppermute | solution.py:22
  31.3 12.7 %collective-permute-start.15 = (bf16[64,1024]{1,0:T(8,128)(2,1)S(1)}, bf16[64,1024]{1,0:T(8,128)(2,1)S(1)}, u32[]{:S(2)}, u32[]{:S(2)}) collective-permute-start(bf16[64,1024]{1,0:T(8,128)(2,1)S(1)} %pad_maximum_fusion.8), channel_id=1, source_target_pairs={{0,8},{1,9},{2,10},{3,11},{4,12},{5,13},{6,14},{7,15},{8,0},{9,1},... | collective-permute-start | bytes 393224 | tf_op jit(solution)/shard_map/ppermute | solution.py:22
  32.9 11.0 %collective-permute-start.16 = (bf16[48,1024]{1,0:T(8,128)(2,1)S(1)}, bf16[48,1024]{1,0:T(8,128)(2,1)S(1)}, u32[]{:S(2)}, u32[]{:S(2)}) collective-permute-start(bf16[48,1024]{1,0:T(8,128)(2,1)S(1)} %pad_maximum_fusion.12), channel_id=1, source_target_pairs={{0,4},{1,5},{2,6},{3,7},{4,0},{5,1},{6,2},{7,3},{8,12},{9,13},{10,... | collective-permute-start | bytes 294920 | tf_op jit(solution)/shard_map/ppermute | solution.py:22
  38.3 10.9 %collective-permute-start.13 = (bf16[160,1024]{1,0:T(8,128)(2,1)S(1)}, bf16[160,1024]{1,0:T(8,128)(2,1)S(1)}, u32[]{:S(2)}, u32[]{:S(2)}) collective-permute-start(bf16[160,1024]{1,0:T(8,128)(2,1)S(1)} %pad_maximum_fusion.1), channel_id=1, source_target_pairs={{0,16},{16,0},{1,17},{17,1},{2,18},{18,2},{3,19},{19,3},{4,20},{20... | collective-permute-start | bytes 983048 | tf_op jit(solution)/shard_map/ppermute | solution.py:105
  44.6 9.7 %collective-permute-start.17 = (bf16[160,1024]{1,0:T(8,128)(2,1)S(1)}, bf16[160,1024]{1,0:T(8,128)(2,1)S(1)}, u32[]{:S(2)}, u32[]{:S(2)}) collective-permute-start(bf16[160,1024]{1,0:T(8,128)(2,1)S(1)} %pad_maximum_fusion.2), channel_id=1, source_target_pairs={{0,16},{16,0},{1,17},{17,1},{2,18},{18,2},{3,19},{19,3},{4,20},{20... | collective-permute-start | bytes 983048 | tf_op jit(solution)/shard_map/ppermute | solution.py:105
  58.9 2.0 %collective-permute-start.18 = (bf16[256,1024]{1,0:T(8,128)(2,1)S(1)}, bf16[256,1024]{1,0:T(8,128)(2,1)S(1)}, u32[]{:S(2)}, u32[]{:S(2)}) collective-permute-start(bf16[256,1024]{1,0:T(8,128)(2,1)S(1)} %fusion.35), channel_id=1, source_target_pairs={{0,1},{1,0},{2,3},{3,2},{4,5},{5,4},{6,7},{7,6},{8,9},{9,8},{10,11... | collective-permute-start | bytes 1572872 | tf_op jit(solution)/shard_map/ppermute | solution.py:22
  61.3 8.4 %collective-permute-start.19 = (bf16[128,1024]{1,0:T(8,128)(2,1)S(1)}, bf16[128,1024]{1,0:T(8,128)(2,1)S(1)}, u32[]{:S(2)}, u32[]{:S(2)}) collective-permute-start(bf16[128,1024]{1,0:T(8,128)(2,1)S(1)} %slice.219), channel_id=1, source_target_pairs={{0,2},{1,3},{2,0},{3,1},{4,6},{5,7},{6,4},{7,5},{8,10},{9,11},{10,... | collective-permute-start | bytes 786440 | tf_op jit(solution)/shard_map/ppermute | solution.py:22
  69.8 7.1 %collective-permute-start.22 = (bf16[32,1024]{1,0:T(8,128)(2,1)S(1)}, bf16[32,1024]{1,0:T(8,128)(2,1)S(1)}, u32[]{:S(2)}, u32[]{:S(2)}) collective-permute-start(bf16[32,1024]{1,0:T(8,128)(2,1)S(1)} %get-tuple-element.145), channel_id=1, source_target_pairs={{0,12},{1,13},{2,14},{3,15},{4,8},{5,9},{6,10},{7,11},{8,4},{9,5},... | collective-permute-start | bytes 196616 | tf_op jit(solution)/shard_map/ppermute | solution.py:22
  71.6 7.2 %collective-permute-start.21 = (bf16[32,1024]{1,0:T(8,128)(2,1)S(1)}, bf16[32,1024]{1,0:T(8,128)(2,1)S(1)}, u32[]{:S(2)}, u32[]{:S(2)}) collective-permute-start(bf16[32,1024]{1,0:T(8,128)(2,1)S(1)} %get-tuple-element.146), channel_id=1, source_target_pairs={{0,8},{1,9},{2,10},{3,11},{4,12},{5,13},{6,14},{7,15},{8,0},{9,1},... | collective-permute-start | bytes 196616 | tf_op jit(solution)/shard_map/ppermute | solution.py:22
  73.3 5.5 %collective-permute-start.20 = (bf16[32,1024]{1,0:T(8,128)(2,1)S(1)}, bf16[32,1024]{1,0:T(8,128)(2,1)S(1)}, u32[]{:S(2)}, u32[]{:S(2)}) collective-permute-start(bf16[32,1024]{1,0:T(8,128)(2,1)S(1)} %get-tuple-element.144), channel_id=1, source_target_pairs={{0,4},{1,5},{2,6},{3,7},{4,0},{5,1},{6,2},{7,3},{8,12},{9,13},{10,... | collective-permute-start | bytes 196616 | tf_op jit(solution)/shard_map/ppermute | solution.py:22
  (6 other events, 68.6 us)

commit v4 on v3

--- a/solution.py
+++ b/solution.py
@@ -95,7 +95,7 @@
         cotangent.reshape(all_rows, model_width),
     )
     here, placed = placed[:2], placed[2:]
-    cells_placed, grads_placed = placed[: low - 1], placed[low - 1 : 2 * (low - 1)]
+    cells_placed, grads_placed = placed[: low - 1], list(placed[low - 1 : 2 * (low - 1)])
     direct_placed = placed[2 * (low - 1) :]
 
     def copies(rows):
@@ -118,8 +118,8 @@
     def stack(*pieces):
         return jnp.concatenate(pieces, axis=0)
 
-    def send_near(pieces):
-        return [swap(pieces[step - 1], step) for step in range(low - 1, 0, -1)]
+    def send_near(pieces, first=1):
+        return [swap(pieces[step - first], step) for step in range(low - 1, first - 1, -1)]
 
     def far_pieces(own, near):
         return [
@@ -139,19 +139,26 @@
         return stack(*[piece[:bucket] for piece in [own] + near])
 
     cells_near = send_near(cells_placed)
-    direct_placed, cells_near[-1] = fence((direct_placed, cells_near[-1]))
+    direct_placed, grads_placed[0], cells_near[-1] = fence(
+        (direct_placed, grads_placed[0], cells_near[-1])
+    )
+    grads_near_last = swap(grads_placed[0], 1)
     direct = [swap(piece, step * low) for piece, step in zip(direct_placed, direct_steps)]
-    cells_near, direct, here, grads_placed = fence((cells_near, direct, here, grads_placed))
-    cells_first, direct, cells_far, grads_placed = fence(
+    cells_near, direct, here, grads_placed, grads_near_last = fence(
+        (cells_near, direct, here, grads_placed[1:], grads_near_last)
+    )
+    cells_first, direct, cells_far, grads_placed, grads_near_last = fence(
         (
             here_and_near(here[0], cells_near),
             stack(*direct),
             far_pieces(here[0], cells_near),
             grads_placed,
+            grads_near_last,
         )
     )
     cells_first_copies = copies(cells_first)
-    grads_near = send_near(grads_placed)
+    grads_near = send_near(grads_placed, 2) + [grads_near_last]
+    cells_far[-1], cells_first_copies = fence((cells_far[-1], cells_first_copies))
     cells_far = send_far(cells_far)
     direct_cells, direct_grads = direct[:, :model_width], direct[:, model_width:]
     grads_first = here_and_near(here[1], grads_near)

time: 79.8 us -> 77.4 us (0.970)
  waiting for transfers between devices: 23.4 us -> 20.2 us
  starting transfers between devices: 27.9 us -> 28.8 us
    ppermute x19, waiting for transfers between devices: 17.4 us -> 12.9 us  [swap(): return lax.ppermute(piece, 'expert', pairs)]
    ppermute x4, waiting for transfers between devices: 6.06 us -> 7.25 us  [copies(): pieces.append(lax.ppermute(rows, 'dp', ring))]
    ppermute x4, starting transfers between devices: 4.25 us -> 5.39 us  [copies(): pieces.append(lax.ppermute(rows, 'dp', ring))]
    unnamed x21 -> x19, local copies, waits for them, and re-layouts: 2.02 us -> 1.97 us
where the time goes in v4:
time: 77.4 us; the launch traced here: 77.2 us
  starting transfers between devices  28.8 us (37%)
  waiting for transfers between devices  20.2 us (26%)
  matrix products  18.6 us (24%)
  local copies, waits for them, and re-layouts  3.02 us (4%)
  Pallas kernels  2.74 us (4%)
  other arithmetic  2.54 us (3%)
  between operations  1.25 us (2%)
    ppermute x19, starting transfers between devices, swap(): return lax.ppermute(piece, 'expert', pairs)  23.5 us
    ppermute x19, waiting for transfers between devices, swap(): return lax.ppermute(piece, 'expert', pairs)  12.9 us
    ppermute x4, waiting for transfers between devices, copies(): pieces.append(lax.ppermute(rows, 'dp', ring))  7.25 us
    ppermute x4, starting transfers between devices, copies(): pieces.append(lax.ppermute(rows, 'dp', ring))  5.39 us
    dot_general x2, matrix products, rows_product(): lax.dot_general(jnp.concatenate(left, axis=0), jnp.concatenate(right, axi...  5.2 us
    dot_general x2, matrix products, forward(): pre_exp = jnp.dot(norm_rows, w_up, preferred_element_type=jnp.float32)  3.2 us
    dot_general x2, matrix products, backward(): lax.dot_general(pre_grad, w_up, contract_last, preferred_element_type=jnp...  2.91 us
    dot_general x2, matrix products, backward(): act_grad = jnp.dot(grad_rows, w_down, preferred_element_type=jnp.float32)  2.78 us
  transfers between devices with their start and end apart: 23, of which 10 were waited for; matrix products, arithmetic and copies ran while one was open for 20% of the time, Pallas kernels for 0%

profile of v4, /device:TPU:0, one launch (start us, length us, event | category | flops | bytes accessed | tf_op | source)
XLA Modules:
  0.0 77.2 jit_solution(17902992242297516654)
XLA Ops:
  0.6 2.7 %shard_map.85 = (bf16[64,1024]{1,0:T(8,128)(2,1)}, bf16[64,1024]{1,0:T(8,128)(2,1)}, bf16[64,1024]{1,0:T(8,128)(2,1)}, bf16[64,1024]{1,0:T(8,128)(2,1)}, bf16[64...) custom-call(s32[1]{0:T(128)} %bitcast.me_ref, ...), custom_call_target="tpu_custom_call" | custom-call | tf_op jit(solution)/shard_map/pallas_call | solution.py:85
  3.9 2.6 %collective-permute-start = (bf16[64,1024]{1,0:T(8,128)(2,1)}, bf16[64,1024]{1,0:T(8,128)(2,1)S(1)}, u32[]{:S(2)}, u32[]{:S(2)}) collective-permute-start(bf16[64,1024]{1,0:T(8,128)(2,1)} %get-tuple-element.73), channel_id=1, source_target_pairs={{0,3},{1,2},{2,1},{3,0},{4,7},{5,6},{6,5},{7,4},{8,11},{9,10},{10,... | collective-permute-start | bytes 393224 | tf_op jit(solution)/shard_map/ppermute | solution.py:22
  6.7 4.0 %collective-permute-start.3 = (bf16[16,2048]{1,0:T(8,128)(2,1)}, bf16[16,2048]{1,0:T(8,128)(2,1)S(1)}, u32[]{:S(2)}, u32[]{:S(2)}) collective-permute-start(bf16[16,2048]{1,0:T(8,128)(2,1)} %get-tuple-element.80), channel_id=1, source_target_pairs={{0,12},{1,13},{2,14},{3,15},{4,8},{5,9},{6,10},{7,11},{8,4},{9,5},... | collective-permute-start | bytes 196616 | tf_op jit(solution)/shard_map/ppermute | solution.py:22
  10.7 2.9 %collective-permute-done.1 = bf16[64,1024]{1,0:T(8,128)(2,1)S(1)} collective-permute-done((bf16[64,1024]{1,0:T(8,128)(2,1)}, bf16[64,1024]{1,0:T(8,128)(2,1)S(1)}, u32[]{:S(2)}, u32[]{:S(2)}) %collective-permute-start.1) | collective-permute-done | bytes 131104 | tf_op jit(solution)/shard_map/ppermute | solution.py:22
  16.1 2.4 %collective-permute-start.6 = (bf16[48,1024]{1,0:T(8,128)(2,1)S(1)}, bf16[48,1024]{1,0:T(8,128)(2,1)S(1)}, u32[]{:S(2)}, u32[]{:S(2)}) collective-permute-start(bf16[48,1024]{1,0:T(8,128)(2,1)S(1)} %pad_maximum_fusion.9), channel_id=1, source_target_pairs={{0,12},{1,13},{2,14},{3,15},{4,8},{5,9},{6,10},{7,11},{8,4},{9,5},... | collective-permute-start | bytes 294920 | tf_op jit(solution)/shard_map/ppermute | solution.py:22
  20.8 1.5 %collective-permute-start.10 = (bf16[64,1024]{1,0:T(8,128)(2,1)S(1)}, bf16[64,1024]{1,0:T(8,128)(2,1)S(1)}, u32[]{:S(2)}, u32[]{:S(2)}) collective-permute-start(bf16[64,1024]{1,0:T(8,128)(2,1)S(1)} %pad_maximum_fusion.5), channel_id=1, source_target_pairs={{0,16},{16,0},{1,17},{17,1},{2,18},{18,2},{3,19},{19,3},{4,20},{20... | collective-permute-start | bytes 393224 | tf_op jit(solution)/shard_map/ppermute | solution.py:105
  22.3 4.2 %collective-permute-done.10 = bf16[64,1024]{1,0:T(8,128)(2,1)S(1)} collective-permute-done((bf16[64,1024]{1,0:T(8,128)(2,1)S(1)}, bf16[64,1024]{1,0:T(8,128)(2,1)S(1)}, u32[]{:S(2)}, u32[]{:S(2)}) %collective-permute-start.10) | collective-permute-done | bytes 131104 | tf_op jit(solution)/shard_map/ppermute | solution.py:105
  28.0 1.7 %collective-permute-start.12 = (bf16[128,1024]{1,0:T(8,128)(2,1)S(1)}, bf16[128,1024]{1,0:T(8,128)(2,1)S(1)}, u32[]{:S(2)}, u32[]{:S(2)}) collective-permute-start(bf16[128,1024]{1,0:T(8,128)(2,1)S(1)} %slice_dynamic-update-slice_fusion.1), channel_id=1, source_target_pairs={{0,16},{16,0},{1,17},{17,1},{2,18},{18,2},{3,19},{19,3},{4,20},{20... | collective-permute-start | bytes 786440 | tf_op jit(solution)/shard_map/ppermute | solution.py:105
  29.7 2.4 %collective-permute-start.14 = (bf16[48,1024]{1,0:T(8,128)(2,1)S(1)}, bf16[48,1024]{1,0:T(8,128)(2,1)S(1)}, u32[]{:S(2)}, u32[]{:S(2)}) collective-permute-start(bf16[48,1024]{1,0:T(8,128)(2,1)S(1)} %pad_maximum_fusion.11), channel_id=1, source_target_pairs={{0,12},{1,13},{2,14},{3,15},{4,8},{5,9},{6,10},{7,11},{8,4},{9,5},... | collective-permute-start | bytes 294920 | tf_op jit(solution)/shard_map/ppermute | solution.py:22
  32.5 1.6 %collective-permute-start.16 = (bf16[48,1024]{1,0:T(8,128)(2,1)S(1)}, bf16[48,1024]{1,0:T(8,128)(2,1)S(1)}, u32[]{:S(2)}, u32[]{:S(2)}) collective-permute-start(bf16[48,1024]{1,0:T(8,128)(2,1)S(1)} %pad_maximum_fusion.12), channel_id=1, source_target_pairs={{0,4},{1,5},{2,6},{3,7},{4,0},{5,1},{6,2},{7,3},{8,12},{9,13},{10,... | collective-permute-start | bytes 294920 | tf_op jit(solution)/shard_map/ppermute | solution.py:22
  34.1 2.1 %collective-permute-done.12 = bf16[128,1024]{1,0:T(8,128)(2,1)S(1)} collective-permute-done((bf16[128,1024]{1,0:T(8,128)(2,1)S(1)}, bf16[128,1024]{1,0:T(8,128)(2,1)S(1)}, u32[]{:S(2)}, u32[]{:S(2)}) %collective-permute-start.12) | collective-permute-done | bytes 262176 | tf_op jit(solution)/shard_map/ppermute | solution.py:105
  36.3 1.6 %collective-permute-start.13 = (bf16[160,1024]{1,0:T(8,128)(2,1)S(1)}, bf16[160,1024]{1,0:T(8,128)(2,1)S(1)}, u32[]{:S(2)}, u32[]{:S(2)}) collective-permute-start(bf16[160,1024]{1,0:T(8,128)(2,1)S(1)} %pad_maximum_fusion.1), channel_id=1, source_target_pairs={{0,16},{16,0},{1,17},{17,1},{2,18},{18,2},{3,19},{19,3},{4,20},{20... | collective-permute-start | bytes 983048 | tf_op jit(solution)/shard_map/ppermute | solution.py:105
  40.1 1.8 %add_multiply_fusion = (f32[256,2048]{1,0:T(8,128)S(1)}, bf16[256,2048]{1,0:T(8,128)(2,1)S(1)}) fusion(bf16[256,1024]{1,0:T(8,128)(2,1)S(1)} %multiply_convert_fusion.5, bf16[1,1024,2048]{2,1,0:T(8,128)(2,1)S(1)} %copy-done.3), kind=kOutput, calls=%fused_computation.28 | convolution fusion | flops 1078460416 | bytes 7864320 | tf_op jit(solution)/shard_map/dot_general | solution.py:114
  46.2 1.4 %multiply_reduce_fusion.2 = (f32[256]{0:T(256)S(1)}, f32[256,1024]{1,0:T(8,128)S(1)}) fusion(f32[256,1024]{1,0:T(8,128)S(1)} %get-tuple-element.134, bf16[256,2048]{1,0:T(8,128)(2,1)S(1)} %fusion.23, bf16[1,1024,2048]{2,1,0:T(8,128)(2,1)S(1)} %copy-done.3), kind=kOutput, calls=%fused_computation.47 | convolution fusion | flops 1074265856 | bytes 7341056 | tf_op jit(solution)/shard_map/dot_general | solution.py:212
  49.3 1.4 %multiply_convert_fusion = (bf16[256,2048]{1,0:T(8,128)(2,1)S(1)}, f32[256,2048]{1,0:T(8,128)S(1)}) fusion(bf16[256,1024]{1,0:T(8,128)(2,1)S(1)} %multiply_convert_fusion.3, bf16[1,1024,2048]{2,1,0:T(8,128)(2,1)S(1)} %copy-done.3), kind=kOutput, calls=%fused_computation.26 | convolution fusion | flops 1076363264 | bytes 7864320 | tf_op jit(solution)/shard_map/dot_general | solution.py:114
  52.3 1.5 %fusion.20 = bf16[256,2048]{1,0:T(8,128)(2,1)S(1)} fusion(bf16[256,1024]{1,0:T(8,128)(2,1)S(1)} %constant_dynamic-update-slice_fusion.12, bf16[1,1024,2048]{2,1,0:T(8,128)(2,1)S(1)} %copy-done.1, f32[256,2048]{1,0:T(8,128)S(1)} %get-tuple-element.199), kind=kOutput, calls=%fused_computation.18 | convolution fusion | flops 1078460416 | bytes 7864320 | tf_op jit(solution)/shard_map/dot_general | solution.py:210
  53.9 1.5 %multiply_reduce_fusion = (f32[256]{0:T(256)S(1)}, f32[256,1024]{1,0:T(8,128)S(1)}) fusion(f32[256,1024]{1,0:T(8,128)S(1)} %get-tuple-element.195, bf16[256,1024]{1,0:T(8,128)(2,1)S(1)} %constant_dynamic-update-slice_fusion.10, bf16[256,2048]{1,0:T(8,128)(2,1)S(1)} %fusion.20, bf16[1,1024,2048]{2,1,0:T(8,128)(2,1)S(1)} %copy-done.3), kind=kOutput, calls=%fused_computation.41 | convolution fusion | flops 1075838720 | bytes 7865344 | tf_op jit(solution)/shard_map/dot_general | solution.py:212
  57.4 1.5 %collective-permute-done.18 = bf16[256,1024]{1,0:T(8,128)(2,1)S(1)} collective-permute-done((bf16[256,1024]{1,0:T(8,128)(2,1)S(1)}, bf16[256,1024]{1,0:T(8,128)(2,1)S(1)}, u32[]{:S(2)}, u32[]{:S(2)}) %collective-permute-start.18) | collective-permute-done | bytes 524320 | tf_op jit(solution)/shard_map/ppermute | solution.py:22
  60.5 2.6 %fusion.18 = bf16[1,512,2048]{2,1,0:T(8,128)(2,1)} fusion(bf16[256,2048]{1,0:T(8,128)(2,1)S(1)} %fusion.20, bf16[256,2048]{1,0:T(8,128)(2,1)S(1)} %fusion.23, bf16[256,512]{1,0:T(8,128)(2,1)S(1)} %constant_dynamic-slice_fusion.2, bf16[256,512]{1,0:T(8,128)(2,1)S(1)} %constant_dynamic-slice_fusion.3), kind=kOutput, calls=%fused_computation.16 | convolution fusion | flops 1080033280 | bytes 4718592 | tf_op jit(solution)/shard_map/dot_general | solution.py:264
  63.1 4.6 %collective-permute-done.19 = bf16[128,1024]{1,0:T(8,128)(2,1)S(1)} collective-permute-done((bf16[128,1024]{1,0:T(8,128)(2,1)S(1)}, bf16[128,1024]{1,0:T(8,128)(2,1)S(1)}, u32[]{:S(2)}, u32[]{:S(2)}) %collective-permute-start.19) | collective-permute-done | bytes 262176 | tf_op jit(solution)/shard_map/ppermute | solution.py:22
  67.8 3.0 %collective-permute-start.22 = (bf16[32,1024]{1,0:T(8,128)(2,1)S(1)}, bf16[32,1024]{1,0:T(8,128)(2,1)S(1)}, u32[]{:S(2)}, u32[]{:S(2)}) collective-permute-start(bf16[32,1024]{1,0:T(8,128)(2,1)S(1)} %get-tuple-element.151), channel_id=1, source_target_pairs={{0,12},{1,13},{2,14},{3,15},{4,8},{5,9},{6,10},{7,11},{8,4},{9,5},... | collective-permute-start | bytes 196616 | tf_op jit(solution)/shard_map/ppermute | solution.py:22
  70.7 1.5 %collective-permute-start.20 = (bf16[32,1024]{1,0:T(8,128)(2,1)S(1)}, bf16[32,1024]{1,0:T(8,128)(2,1)S(1)}, u32[]{:S(2)}, u32[]{:S(2)}) collective-permute-start(bf16[32,1024]{1,0:T(8,128)(2,1)S(1)} %get-tuple-element.150), channel_id=1, source_target_pairs={{0,4},{1,5},{2,6},{3,7},{4,0},{5,1},{6,2},{7,3},{8,12},{9,13},{10,... | collective-permute-start | bytes 196616 | tf_op jit(solution)/shard_map/ppermute | solution.py:22
  72.2 2.6 %fusion.19 = bf16[1,512,2048]{2,1,0:T(8,128)(2,1)} fusion(bf16[256,2048]{1,0:T(8,128)(2,1)S(1)} %get-tuple-element.198, bf16[256,2048]{1,0:T(8,128)(2,1)S(1)} %get-tuple-element.142, bf16[256,512]{1,0:T(8,128)(2,1)S(1)} %constant_dynamic-slice_fusion, bf16[256,512]{1,0:T(8,128)(2,1)S(1)} %constant_dynamic-slice_fusion.1), kind=kOutput, calls=%fused_computation.17 | convolution fusion | flops 1080033280 | bytes 4718592 | tf_op jit(solution)/shard_map/dot_general | solution.py:264
  74.8 1.6 %collective-permute-done.21 = bf16[32,1024]{1,0:T(8,128)(2,1)S(1)} collective-permute-done((bf16[32,1024]{1,0:T(8,128)(2,1)S(1)}, bf16[32,1024]{1,0:T(8,128)(2,1)S(1)}, u32[]{:S(2)}, u32[]{:S(2)}) %collective-permute-start.21) | collective-permute-done | bytes 65568 | tf_op jit(solution)/shard_map/ppermute | solution.py:22
  (96 shorter events, 21.2 us)
Async XLA Ops:
  0.6 37.3 %copy-start = (bf16[1024,1024]{1,0:T(8,128)(2,1)S(1)}, bf16[1024,1024]{1,0:T(8,128)(2,1)}, u32[]{:S(2)}) copy-start(bf16[1024,1024]{1,0:T(8,128)(2,1)} %param.9) | copy-start | bytes 6291460
  3.4 3.2 %collective-permute-start.2 = (bf16[64,1024]{1,0:T(8,128)(2,1)}, bf16[64,1024]{1,0:T(8,128)(2,1)S(1)}, u32[]{:S(2)}, u32[]{:S(2)}) collective-permute-start(bf16[64,1024]{1,0:T(8,128)(2,1)} %get-tuple-element.78), channel_id=1, source_target_pairs={{0,1},{1,0},{2,3},{3,2},{4,5},{5,4},{6,7},{7,6},{8,9},{9,8},{10,11... | collective-permute-start | bytes 393224 | tf_op jit(solution)/shard_map/ppermute | solution.py:22
  3.9 6.8 %collective-permute-start = (bf16[64,1024]{1,0:T(8,128)(2,1)}, bf16[64,1024]{1,0:T(8,128)(2,1)S(1)}, u32[]{:S(2)}, u32[]{:S(2)}) collective-permute-start(bf16[64,1024]{1,0:T(8,128)(2,1)} %get-tuple-element.73), channel_id=1, source_target_pairs={{0,3},{1,2},{2,1},{3,0},{4,7},{5,6},{6,5},{7,4},{8,11},{9,10},{10,... | collective-permute-start | bytes 393224 | tf_op jit(solution)/shard_map/ppermute | solution.py:22
  6.5 7.1 %collective-permute-start.1 = (bf16[64,1024]{1,0:T(8,128)(2,1)}, bf16[64,1024]{1,0:T(8,128)(2,1)S(1)}, u32[]{:S(2)}, u32[]{:S(2)}) collective-permute-start(bf16[64,1024]{1,0:T(8,128)(2,1)} %get-tuple-element.74), channel_id=1, source_target_pairs={{0,2},{1,3},{2,0},{3,1},{4,6},{5,7},{6,4},{7,5},{8,10},{9,11},{10,... | collective-permute-start | bytes 393224 | tf_op jit(solution)/shard_map/ppermute | solution.py:22
  6.6 8.6 %collective-permute-start.5 = (bf16[64,1024]{1,0:T(8,128)(2,1)}, bf16[64,1024]{1,0:T(8,128)(2,1)S(1)}, u32[]{:S(2)}, u32[]{:S(2)}) collective-permute-start(bf16[64,1024]{1,0:T(8,128)(2,1)} %get-tuple-element.86), channel_id=1, source_target_pairs={{0,1},{1,0},{2,3},{3,2},{4,5},{5,4},{6,7},{7,6},{8,9},{9,8},{10,11... | collective-permute-start | bytes 393224 | tf_op jit(solution)/shard_map/ppermute | solution.py:22
  6.7 7.2 %collective-permute-start.3 = (bf16[16,2048]{1,0:T(8,128)(2,1)}, bf16[16,2048]{1,0:T(8,128)(2,1)S(1)}, u32[]{:S(2)}, u32[]{:S(2)}) collective-permute-start(bf16[16,2048]{1,0:T(8,128)(2,1)} %get-tuple-element.80), channel_id=1, source_target_pairs={{0,12},{1,13},{2,14},{3,15},{4,8},{5,9},{6,10},{7,11},{8,4},{9,5},... | collective-permute-start | bytes 196616 | tf_op jit(solution)/shard_map/ppermute | solution.py:22
  10.7 4.5 %collective-permute-start.4 = (bf16[16,2048]{1,0:T(8,128)(2,1)}, bf16[16,2048]{1,0:T(8,128)(2,1)S(1)}, u32[]{:S(2)}, u32[]{:S(2)}) collective-permute-start(bf16[16,2048]{1,0:T(8,128)(2,1)} %get-tuple-element.81), channel_id=1, source_target_pairs={{0,4},{1,5},{2,6},{3,7},{4,0},{5,1},{6,2},{7,3},{8,12},{9,13},{10,... | collective-permute-start | bytes 196616 | tf_op jit(solution)/shard_map/ppermute | solution.py:22
  16.1 13.5 %collective-permute-start.6 = (bf16[48,1024]{1,0:T(8,128)(2,1)S(1)}, bf16[48,1024]{1,0:T(8,128)(2,1)S(1)}, u32[]{:S(2)}, u32[]{:S(2)}) collective-permute-start(bf16[48,1024]{1,0:T(8,128)(2,1)S(1)} %pad_maximum_fusion.9), channel_id=1, source_target_pairs={{0,12},{1,13},{2,14},{3,15},{4,8},{5,9},{6,10},{7,11},{8,4},{9,5},... | collective-permute-start | bytes 294920 | tf_op jit(solution)/shard_map/ppermute | solution.py:22
  18.6 11.1 %collective-permute-start.7 = (bf16[64,1024]{1,0:T(8,128)(2,1)S(1)}, bf16[64,1024]{1,0:T(8,128)(2,1)S(1)}, u32[]{:S(2)}, u32[]{:S(2)}) collective-permute-start(bf16[64,1024]{1,0:T(8,128)(2,1)S(1)} %pad_maximum_fusion.7), channel_id=1, source_target_pairs={{0,8},{1,9},{2,10},{3,11},{4,12},{5,13},{6,14},{7,15},{8,0},{9,1},... | collective-permute-start | bytes 393224 | tf_op jit(solution)/shard_map/ppermute | solution.py:22
  19.2 8.6 %collective-permute-start.8 = (bf16[64,1024]{1,0:T(8,128)(2,1)S(1)}, bf16[64,1024]{1,0:T(8,128)(2,1)S(1)}, u32[]{:S(2)}, u32[]{:S(2)}) collective-permute-start(bf16[64,1024]{1,0:T(8,128)(2,1)S(1)} %copy-done.5), channel_id=1, source_target_pairs={{0,3},{1,2},{2,1},{3,0},{4,7},{5,6},{6,5},{7,4},{8,11},{9,10},{10,... | collective-permute-start | bytes 393224 | tf_op jit(solution)/shard_map/ppermute | solution.py:22
  19.5 8.4 %collective-permute-start.9 = (bf16[64,1024]{1,0:T(8,128)(2,1)S(1)}, bf16[64,1024]{1,0:T(8,128)(2,1)S(1)}, u32[]{:S(2)}, u32[]{:S(2)}) collective-permute-start(bf16[64,1024]{1,0:T(8,128)(2,1)S(1)} %copy-done.4), channel_id=1, source_target_pairs={{0,2},{1,3},{2,0},{3,1},{4,6},{5,7},{6,4},{7,5},{8,10},{9,11},{10,... | collective-permute-start | bytes 393224 | tf_op jit(solution)/shard_map/ppermute | solution.py:22
  20.8 5.7 %collective-permute-start.10 = (bf16[64,1024]{1,0:T(8,128)(2,1)S(1)}, bf16[64,1024]{1,0:T(8,128)(2,1)S(1)}, u32[]{:S(2)}, u32[]{:S(2)}) collective-permute-start(bf16[64,1024]{1,0:T(8,128)(2,1)S(1)} %pad_maximum_fusion.5), channel_id=1, source_target_pairs={{0,16},{16,0},{1,17},{17,1},{2,18},{18,2},{3,19},{19,3},{4,20},{20... | collective-permute-start | bytes 393224 | tf_op jit(solution)/shard_map/ppermute | solution.py:105
  26.5 7.6 %collective-permute-start.11 = (bf16[48,1024]{1,0:T(8,128)(2,1)S(1)}, bf16[48,1024]{1,0:T(8,128)(2,1)S(1)}, u32[]{:S(2)}, u32[]{:S(2)}) collective-permute-start(bf16[48,1024]{1,0:T(8,128)(2,1)S(1)} %pad_maximum_fusion.10), channel_id=1, source_target_pairs={{0,4},{1,5},{2,6},{3,7},{4,0},{5,1},{6,2},{7,3},{8,12},{9,13},{10,... | collective-permute-start | bytes 294920 | tf_op jit(solution)/shard_map/ppermute | solution.py:22
  28.0 8.3 %collective-permute-start.12 = (bf16[128,1024]{1,0:T(8,128)(2,1)S(1)}, bf16[128,1024]{1,0:T(8,128)(2,1)S(1)}, u32[]{:S(2)}, u32[]{:S(2)}) collective-permute-start(bf16[128,1024]{1,0:T(8,128)(2,1)S(1)} %slice_dynamic-update-slice_fusion.1), channel_id=1, source_target_pairs={{0,16},{16,0},{1,17},{17,1},{2,18},{18,2},{3,19},{19,3},{4,20},{20... | collective-permute-start | bytes 786440 | tf_op jit(solution)/shard_map/ppermute | solution.py:105
  29.7 12.3 %collective-permute-start.14 = (bf16[48,1024]{1,0:T(8,128)(2,1)S(1)}, bf16[48,1024]{1,0:T(8,128)(2,1)S(1)}, u32[]{:S(2)}, u32[]{:S(2)}) collective-permute-start(bf16[48,1024]{1,0:T(8,128)(2,1)S(1)} %pad_maximum_fusion.11), channel_id=1, source_target_pairs={{0,12},{1,13},{2,14},{3,15},{4,8},{5,9},{6,10},{7,11},{8,4},{9,5},... | collective-permute-start | bytes 294920 | tf_op jit(solution)/shard_map/ppermute | solution.py:22
  32.1 10.6 %collective-permute-start.15 = (bf16[64,1024]{1,0:T(8,128)(2,1)S(1)}, bf16[64,1024]{1,0:T(8,128)(2,1)S(1)}, u32[]{:S(2)}, u32[]{:S(2)}) collective-permute-start(bf16[64,1024]{1,0:T(8,128)(2,1)S(1)} %pad_maximum_fusion.8), channel_id=1, source_target_pairs={{0,8},{1,9},{2,10},{3,11},{4,12},{5,13},{6,14},{7,15},{8,0},{9,1},... | collective-permute-start | bytes 393224 | tf_op jit(solution)/shard_map/ppermute | solution.py:22
  32.5 9.5 %collective-permute-start.16 = (bf16[48,1024]{1,0:T(8,128)(2,1)S(1)}, bf16[48,1024]{1,0:T(8,128)(2,1)S(1)}, u32[]{:S(2)}, u32[]{:S(2)}) collective-permute-start(bf16[48,1024]{1,0:T(8,128)(2,1)S(1)} %pad_maximum_fusion.12), channel_id=1, source_target_pairs={{0,4},{1,5},{2,6},{3,7},{4,0},{5,1},{6,2},{7,3},{8,12},{9,13},{10,... | collective-permute-start | bytes 294920 | tf_op jit(solution)/shard_map/ppermute | solution.py:22
  36.3 11.6 %collective-permute-start.13 = (bf16[160,1024]{1,0:T(8,128)(2,1)S(1)}, bf16[160,1024]{1,0:T(8,128)(2,1)S(1)}, u32[]{:S(2)}, u32[]{:S(2)}) collective-permute-start(bf16[160,1024]{1,0:T(8,128)(2,1)S(1)} %pad_maximum_fusion.1), channel_id=1, source_target_pairs={{0,16},{16,0},{1,17},{17,1},{2,18},{18,2},{3,19},{19,3},{4,20},{20... | collective-permute-start | bytes 983048 | tf_op jit(solution)/shard_map/ppermute | solution.py:105
  43.3 8.9 %collective-permute-start.17 = (bf16[160,1024]{1,0:T(8,128)(2,1)S(1)}, bf16[160,1024]{1,0:T(8,128)(2,1)S(1)}, u32[]{:S(2)}, u32[]{:S(2)}) collective-permute-start(bf16[160,1024]{1,0:T(8,128)(2,1)S(1)} %pad_maximum_fusion.2), channel_id=1, source_target_pairs={{0,16},{16,0},{1,17},{17,1},{2,18},{18,2},{3,19},{19,3},{4,20},{20... | collective-permute-start | bytes 983048 | tf_op jit(solution)/shard_map/ppermute | solution.py:105
  56.9 2.0 %collective-permute-start.18 = (bf16[256,1024]{1,0:T(8,128)(2,1)S(1)}, bf16[256,1024]{1,0:T(8,128)(2,1)S(1)}, u32[]{:S(2)}, u32[]{:S(2)}) collective-permute-start(bf16[256,1024]{1,0:T(8,128)(2,1)S(1)} %fusion.35), channel_id=1, source_target_pairs={{0,1},{1,0},{2,3},{3,2},{4,5},{5,4},{6,7},{7,6},{8,9},{9,8},{10,11... | collective-permute-start | bytes 1572872 | tf_op jit(solution)/shard_map/ppermute | solution.py:22
  59.3 8.4 %collective-permute-start.19 = (bf16[128,1024]{1,0:T(8,128)(2,1)S(1)}, bf16[128,1024]{1,0:T(8,128)(2,1)S(1)}, u32[]{:S(2)}, u32[]{:S(2)}) collective-permute-start(bf16[128,1024]{1,0:T(8,128)(2,1)S(1)} %slice.215), channel_id=1, source_target_pairs={{0,2},{1,3},{2,0},{3,1},{4,6},{5,7},{6,4},{7,5},{8,10},{9,11},{10,... | collective-permute-start | bytes 786440 | tf_op jit(solution)/shard_map/ppermute | solution.py:22
  67.8 7.1 %collective-permute-start.22 = (bf16[32,1024]{1,0:T(8,128)(2,1)S(1)}, bf16[32,1024]{1,0:T(8,128)(2,1)S(1)}, u32[]{:S(2)}, u32[]{:S(2)}) collective-permute-start(bf16[32,1024]{1,0:T(8,128)(2,1)S(1)} %get-tuple-element.151), channel_id=1, source_target_pairs={{0,12},{1,13},{2,14},{3,15},{4,8},{5,9},{6,10},{7,11},{8,4},{9,5},... | collective-permute-start | bytes 196616 | tf_op jit(solution)/shard_map/ppermute | solution.py:22
  70.7 5.7 %collective-permute-start.21 = (bf16[32,1024]{1,0:T(8,128)(2,1)S(1)}, bf16[32,1024]{1,0:T(8,128)(2,1)S(1)}, u32[]{:S(2)}, u32[]{:S(2)}) collective-permute-start(bf16[32,1024]{1,0:T(8,128)(2,1)S(1)} %get-tuple-element.152), channel_id=1, source_target_pairs={{0,8},{1,9},{2,10},{3,11},{4,12},{5,13},{6,14},{7,15},{8,0},{9,1},... | collective-permute-start | bytes 196616 | tf_op jit(solution)/shard_map/ppermute | solution.py:22
  70.7 5.7 %collective-permute-start.20 = (bf16[32,1024]{1,0:T(8,128)(2,1)S(1)}, bf16[32,1024]{1,0:T(8,128)(2,1)S(1)}, u32[]{:S(2)}, u32[]{:S(2)}) collective-permute-start(bf16[32,1024]{1,0:T(8,128)(2,1)S(1)} %get-tuple-element.150), channel_id=1, source_target_pairs={{0,4},{1,5},{2,6},{3,7},{4,0},{5,1},{6,2},{7,3},{8,12},{9,13},{10,... | collective-permute-start | bytes 196616 | tf_op jit(solution)/shard_map/ppermute | solution.py:22
  (5 other events, 55.3 us)

commit v5 on v4

--- a/solution.py
+++ b/solution.py
@@ -180,7 +180,9 @@
         for cells, second in zip(*came)
     ]
     grads_far, early, own_forward = fence((grads_far, early, forward(features)))
-    grads_far, early, own_forward = fence((stack(*grads_far), early, own_forward))
+    grads_far, early, own_forward, features = fence(
+        (stack(*grads_far), early, own_forward, features)
+    )
     grads_far_copies = copies(grads_far)
 
     share = model_width // dp_count

time: 77.4 us -> 77.4 us (level)
  local copies, waits for them, and re-layouts: 3.02 us -> 2.09 us
  waiting for transfers between devices: 20.2 us -> 21 us
    unnamed x19, local copies, waits for them, and re-layouts: 1.97 us -> 1.04 us
    ppermute x4, waiting for transfers between devices: 7.25 us -> 8.16 us  [copies(): pieces.append(lax.ppermute(rows, 'dp', ring))]
  transfers between devices with their start and end apart: 23 -> 23, of which waited for: 10 -> 10; matrix products, arithmetic and copies ran while one was open for 20% -> 21% of each run, Pallas kernels for 0% -> 0%
where the time goes in v5:
time: 77.4 us; the launch traced here: 77.2 us
  starting transfers between devices  28.8 us (37%)
  waiting for transfers between devices  21 us (27%)
  matrix products  18.8 us (24%)
  Pallas kernels  2.74 us (4%)
  other arithmetic  2.57 us (3%)
  local copies, waits for them, and re-layouts  2.09 us (3%)
  between operations  1.1 us (1%)
    ppermute x19, starting transfers between devices, swap(): return lax.ppermute(piece, 'expert', pairs)  23.5 us
    ppermute x19, waiting for transfers between devices, swap(): return lax.ppermute(piece, 'expert', pairs)  12.9 us
    ppermute x4, waiting for transfers between devices, copies(): pieces.append(lax.ppermute(rows, 'dp', ring))  8.16 us
    ppermute x4, starting transfers between devices, copies(): pieces.append(lax.ppermute(rows, 'dp', ring))  5.39 us
    dot_general x2, matrix products, rows_product(): lax.dot_general(jnp.concatenate(left, axis=0), jnp.concatenate(right, axi...  5.2 us
    dot_general x2, matrix products, forward(): pre_exp = jnp.dot(norm_rows, w_up, preferred_element_type=jnp.float32)  3.21 us
    dot_general x2, matrix products, backward(): act_grad = jnp.dot(grad_rows, w_down, preferred_element_type=jnp.float32)  2.96 us
    dot_general x2, matrix products, backward(): lax.dot_general(pre_grad, w_up, contract_last, preferred_element_type=jnp...  2.91 us
  transfers between devices with their start and end apart: 23, of which 10 were waited for; matrix products, arithmetic and copies ran while one was open for 21% of the time, Pallas kernels for 0%

profile of v5, /device:TPU:0, one launch (start us, length us, event | category | flops | bytes accessed | tf_op | source)
XLA Modules:
  0.0 77.2 jit_solution(18125543331321104139)
XLA Ops:
  0.6 2.7 %shard_map.85 = (bf16[64,1024]{1,0:T(8,128)(2,1)}, bf16[64,1024]{1,0:T(8,128)(2,1)}, bf16[64,1024]{1,0:T(8,128)(2,1)}, bf16[64,1024]{1,0:T(8,128)(2,1)}, bf16[64...) custom-call(s32[1]{0:T(128)} %bitcast.me_ref, ...), custom_call_target="tpu_custom_call" | custom-call | tf_op jit(solution)/shard_map/pallas_call | solution.py:85
  3.9 2.6 %collective-permute-start = (bf16[64,1024]{1,0:T(8,128)(2,1)}, bf16[64,1024]{1,0:T(8,128)(2,1)S(1)}, u32[]{:S(2)}, u32[]{:S(2)}) collective-permute-start(bf16[64,1024]{1,0:T(8,128)(2,1)} %get-tuple-element.74), channel_id=1, source_target_pairs={{0,3},{1,2},{2,1},{3,0},{4,7},{5,6},{6,5},{7,4},{8,11},{9,10},{10,... | collective-permute-start | bytes 393224 | tf_op jit(solution)/shard_map/ppermute | solution.py:22
  6.7 4.0 %collective-permute-start.3 = (bf16[16,2048]{1,0:T(8,128)(2,1)}, bf16[16,2048]{1,0:T(8,128)(2,1)S(1)}, u32[]{:S(2)}, u32[]{:S(2)}) collective-permute-start(bf16[16,2048]{1,0:T(8,128)(2,1)} %get-tuple-element.81), channel_id=1, source_target_pairs={{0,12},{1,13},{2,14},{3,15},{4,8},{5,9},{6,10},{7,11},{8,4},{9,5},... | collective-permute-start | bytes 196616 | tf_op jit(solution)/shard_map/ppermute | solution.py:22
  10.7 2.9 %collective-permute-done.1 = bf16[64,1024]{1,0:T(8,128)(2,1)S(1)} collective-permute-done((bf16[64,1024]{1,0:T(8,128)(2,1)}, bf16[64,1024]{1,0:T(8,128)(2,1)S(1)}, u32[]{:S(2)}, u32[]{:S(2)}) %collective-permute-start.1) | collective-permute-done | bytes 131104 | tf_op jit(solution)/shard_map/ppermute | solution.py:22
  16.1 2.4 %collective-permute-start.6 = (bf16[48,1024]{1,0:T(8,128)(2,1)S(1)}, bf16[48,1024]{1,0:T(8,128)(2,1)S(1)}, u32[]{:S(2)}, u32[]{:S(2)}) collective-permute-start(bf16[48,1024]{1,0:T(8,128)(2,1)S(1)} %pad_maximum_fusion.9), channel_id=1, source_target_pairs={{0,12},{1,13},{2,14},{3,15},{4,8},{5,9},{6,10},{7,11},{8,4},{9,5},... | collective-permute-start | bytes 294920 | tf_op jit(solution)/shard_map/ppermute | solution.py:22
  20.8 1.5 %collective-permute-start.10 = (bf16[64,1024]{1,0:T(8,128)(2,1)S(1)}, bf16[64,1024]{1,0:T(8,128)(2,1)S(1)}, u32[]{:S(2)}, u32[]{:S(2)}) collective-permute-start(bf16[64,1024]{1,0:T(8,128)(2,1)S(1)} %pad_maximum_fusion.5), channel_id=1, source_target_pairs={{0,16},{16,0},{1,17},{17,1},{2,18},{18,2},{3,19},{19,3},{4,20},{20... | collective-permute-start | bytes 393224 | tf_op jit(solution)/shard_map/ppermute | solution.py:105
  22.3 4.2 %collective-permute-done.10 = bf16[64,1024]{1,0:T(8,128)(2,1)S(1)} collective-permute-done((bf16[64,1024]{1,0:T(8,128)(2,1)S(1)}, bf16[64,1024]{1,0:T(8,128)(2,1)S(1)}, u32[]{:S(2)}, u32[]{:S(2)}) %collective-permute-start.10) | collective-permute-done | bytes 131104 | tf_op jit(solution)/shard_map/ppermute | solution.py:105
  28.0 1.7 %collective-permute-start.12 = (bf16[128,1024]{1,0:T(8,128)(2,1)S(1)}, bf16[128,1024]{1,0:T(8,128)(2,1)S(1)}, u32[]{:S(2)}, u32[]{:S(2)}) collective-permute-start(bf16[128,1024]{1,0:T(8,128)(2,1)S(1)} %slice_dynamic-update-slice_fusion.1), channel_id=1, source_target_pairs={{0,16},{16,0},{1,17},{17,1},{2,18},{18,2},{3,19},{19,3},{4,20},{20... | collective-permute-start | bytes 786440 | tf_op jit(solution)/shard_map/ppermute | solution.py:105
  29.7 2.4 %collective-permute-start.14 = (bf16[48,1024]{1,0:T(8,128)(2,1)S(1)}, bf16[48,1024]{1,0:T(8,128)(2,1)S(1)}, u32[]{:S(2)}, u32[]{:S(2)}) collective-permute-start(bf16[48,1024]{1,0:T(8,128)(2,1)S(1)} %pad_maximum_fusion.11), channel_id=1, source_target_pairs={{0,12},{1,13},{2,14},{3,15},{4,8},{5,9},{6,10},{7,11},{8,4},{9,5},... | collective-permute-start | bytes 294920 | tf_op jit(solution)/shard_map/ppermute | solution.py:22
  32.5 1.6 %collective-permute-start.16 = (bf16[48,1024]{1,0:T(8,128)(2,1)S(1)}, bf16[48,1024]{1,0:T(8,128)(2,1)S(1)}, u32[]{:S(2)}, u32[]{:S(2)}) collective-permute-start(bf16[48,1024]{1,0:T(8,128)(2,1)S(1)} %pad_maximum_fusion.12), channel_id=1, source_target_pairs={{0,4},{1,5},{2,6},{3,7},{4,0},{5,1},{6,2},{7,3},{8,12},{9,13},{10,... | collective-permute-start | bytes 294920 | tf_op jit(solution)/shard_map/ppermute | solution.py:22
  34.1 2.1 %collective-permute-done.12 = bf16[128,1024]{1,0:T(8,128)(2,1)S(1)} collective-permute-done((bf16[128,1024]{1,0:T(8,128)(2,1)S(1)}, bf16[128,1024]{1,0:T(8,128)(2,1)S(1)}, u32[]{:S(2)}, u32[]{:S(2)}) %collective-permute-start.12) | collective-permute-done | bytes 262176 | tf_op jit(solution)/shard_map/ppermute | solution.py:105
  36.3 1.6 %collective-permute-start.13 = (bf16[160,1024]{1,0:T(8,128)(2,1)S(1)}, bf16[160,1024]{1,0:T(8,128)(2,1)S(1)}, u32[]{:S(2)}, u32[]{:S(2)}) collective-permute-start(bf16[160,1024]{1,0:T(8,128)(2,1)S(1)} %pad_maximum_fusion.1), channel_id=1, source_target_pairs={{0,16},{16,0},{1,17},{17,1},{2,18},{18,2},{3,19},{19,3},{4,20},{20... | collective-permute-start | bytes 983048 | tf_op jit(solution)/shard_map/ppermute | solution.py:105
  40.2 1.8 %add_multiply_fusion = (f32[256,2048]{1,0:T(8,128)S(1)}, bf16[256,2048]{1,0:T(8,128)(2,1)S(1)}) fusion(bf16[256,1024]{1,0:T(8,128)(2,1)S(1)} %multiply_convert_fusion.5, bf16[1,1024,2048]{2,1,0:T(8,128)(2,1)S(1)} %copy-done.3), kind=kOutput, calls=%fused_computation.31 | convolution fusion | flops 1078460416 | bytes 7864320 | tf_op jit(solution)/shard_map/dot_general | solution.py:114
  48.4 1.4 %multiply_convert_fusion = (bf16[256,2048]{1,0:T(8,128)(2,1)S(1)}, f32[256,2048]{1,0:T(8,128)S(1)}) fusion(bf16[256,1024]{1,0:T(8,128)(2,1)S(1)} %multiply_convert_fusion.3, bf16[1,1024,2048]{2,1,0:T(8,128)(2,1)S(1)} %copy-done.3), kind=kOutput, calls=%fused_computation.26 | convolution fusion | flops 1076363264 | bytes 7864320 | tf_op jit(solution)/shard_map/dot_general | solution.py:114
  50.4 1.8 %collective-permute-done.17 = bf16[160,1024]{1,0:T(8,128)(2,1)S(1)} collective-permute-done((bf16[160,1024]{1,0:T(8,128)(2,1)S(1)}, bf16[160,1024]{1,0:T(8,128)(2,1)S(1)}, u32[]{:S(2)}, u32[]{:S(2)}) %collective-permute-start.17) | collective-permute-done | bytes 327712 | tf_op jit(solution)/shard_map/ppermute | solution.py:105
  52.3 1.7 %fusion.20 = bf16[256,2048]{1,0:T(8,128)(2,1)S(1)} fusion(bf16[256,1024]{1,0:T(8,128)(2,1)S(1)} %constant_dynamic-update-slice_fusion.12, bf16[1,1024,2048]{2,1,0:T(8,128)(2,1)S(1)} %copy-done.1, f32[256,2048]{1,0:T(8,128)S(1)} %get-tuple-element.201), kind=kOutput, calls=%fused_computation.18 | convolution fusion | flops 1078460416 | bytes 7864320 | tf_op jit(solution)/shard_map/dot_general | solution.py:212
  53.9 1.5 %multiply_reduce_fusion = (f32[256]{0:T(256)S(1)}, f32[256,1024]{1,0:T(8,128)S(1)}) fusion(f32[256,1024]{1,0:T(8,128)S(1)} %get-tuple-element.197, bf16[256,1024]{1,0:T(8,128)(2,1)S(1)} %constant_dynamic-update-slice_fusion.10, bf16[256,2048]{1,0:T(8,128)(2,1)S(1)} %fusion.20, bf16[1,1024,2048]{2,1,0:T(8,128)(2,1)S(1)} %copy-done.3), kind=kOutput, calls=%fused_computation.41 | convolution fusion | flops 1075838720 | bytes 7865344 | tf_op jit(solution)/shard_map/dot_general | solution.py:214
  57.4 1.5 %collective-permute-done.18 = bf16[256,1024]{1,0:T(8,128)(2,1)S(1)} collective-permute-done((bf16[256,1024]{1,0:T(8,128)(2,1)S(1)}, bf16[256,1024]{1,0:T(8,128)(2,1)S(1)}, u32[]{:S(2)}, u32[]{:S(2)}) %collective-permute-start.18) | collective-permute-done | bytes 524320 | tf_op jit(solution)/shard_map/ppermute | solution.py:22
  60.5 2.6 %fusion.18 = bf16[1,512,2048]{2,1,0:T(8,128)(2,1)} fusion(bf16[256,2048]{1,0:T(8,128)(2,1)S(1)} %fusion.20, bf16[256,2048]{1,0:T(8,128)(2,1)S(1)} %fusion.23, bf16[256,512]{1,0:T(8,128)(2,1)S(1)} %constant_dynamic-slice_fusion.2, bf16[256,512]{1,0:T(8,128)(2,1)S(1)} %constant_dynamic-slice_fusion.3), kind=kOutput, calls=%fused_computation.16 | convolution fusion | flops 1080033280 | bytes 4718592 | tf_op jit(solution)/shard_map/dot_general | solution.py:266
  63.1 4.6 %collective-permute-done.19 = bf16[128,1024]{1,0:T(8,128)(2,1)S(1)} collective-permute-done((bf16[128,1024]{1,0:T(8,128)(2,1)S(1)}, bf16[128,1024]{1,0:T(8,128)(2,1)S(1)}, u32[]{:S(2)}, u32[]{:S(2)}) %collective-permute-start.19) | collective-permute-done | bytes 262176 | tf_op jit(solution)/shard_map/ppermute | solution.py:22
  67.8 2.4 %collective-permute-start.22 = (bf16[32,1024]{1,0:T(8,128)(2,1)S(1)}, bf16[32,1024]{1,0:T(8,128)(2,1)S(1)}, u32[]{:S(2)}, u32[]{:S(2)}) collective-permute-start(bf16[32,1024]{1,0:T(8,128)(2,1)S(1)} %get-tuple-element.153), channel_id=1, source_target_pairs={{0,12},{1,13},{2,14},{3,15},{4,8},{5,9},{6,10},{7,11},{8,4},{9,5},... | collective-permute-start | bytes 196616 | tf_op jit(solution)/shard_map/ppermute | solution.py:22
  70.5 1.7 %collective-permute-start.20 = (bf16[32,1024]{1,0:T(8,128)(2,1)S(1)}, bf16[32,1024]{1,0:T(8,128)(2,1)S(1)}, u32[]{:S(2)}, u32[]{:S(2)}) collective-permute-start(bf16[32,1024]{1,0:T(8,128)(2,1)S(1)} %get-tuple-element.152), channel_id=1, source_target_pairs={{0,4},{1,5},{2,6},{3,7},{4,0},{5,1},{6,2},{7,3},{8,12},{9,13},{10,... | collective-permute-start | bytes 196616 | tf_op jit(solution)/shard_map/ppermute | solution.py:22
  72.2 2.6 %fusion.19 = bf16[1,512,2048]{2,1,0:T(8,128)(2,1)} fusion(bf16[256,2048]{1,0:T(8,128)(2,1)S(1)} %get-tuple-element.200, bf16[256,2048]{1,0:T(8,128)(2,1)S(1)} %get-tuple-element.144, bf16[256,512]{1,0:T(8,128)(2,1)S(1)} %constant_dynamic-slice_fusion, bf16[256,512]{1,0:T(8,128)(2,1)S(1)} %constant_dynamic-slice_fusion.1), kind=kOutput, calls=%fused_computation.17 | convolution fusion | flops 1080033280 | bytes 4718592 | tf_op jit(solution)/shard_map/dot_general | solution.py:266
  74.8 1.6 %collective-permute-done.21 = bf16[32,1024]{1,0:T(8,128)(2,1)S(1)} collective-permute-done((bf16[32,1024]{1,0:T(8,128)(2,1)S(1)}, bf16[32,1024]{1,0:T(8,128)(2,1)S(1)}, u32[]{:S(2)}, u32[]{:S(2)}) %collective-permute-start.21) | collective-permute-done | bytes 65568 | tf_op jit(solution)/shard_map/ppermute | solution.py:22
  (97 shorter events, 21.1 us)
Async XLA Ops:
  0.6 37.3 %copy-start = (bf16[1024,1024]{1,0:T(8,128)(2,1)S(1)}, bf16[1024,1024]{1,0:T(8,128)(2,1)}, u32[]{:S(2)}) copy-start(bf16[1024,1024]{1,0:T(8,128)(2,1)} %param.9) | copy-start | bytes 6291460
  3.4 3.2 %collective-permute-start.2 = (bf16[64,1024]{1,0:T(8,128)(2,1)}, bf16[64,1024]{1,0:T(8,128)(2,1)S(1)}, u32[]{:S(2)}, u32[]{:S(2)}) collective-permute-start(bf16[64,1024]{1,0:T(8,128)(2,1)} %get-tuple-element.79), channel_id=1, source_target_pairs={{0,1},{1,0},{2,3},{3,2},{4,5},{5,4},{6,7},{7,6},{8,9},{9,8},{10,11... | collective-permute-start | bytes 393224 | tf_op jit(solution)/shard_map/ppermute | solution.py:22
  3.9 6.8 %collective-permute-start = (bf16[64,1024]{1,0:T(8,128)(2,1)}, bf16[64,1024]{1,0:T(8,128)(2,1)S(1)}, u32[]{:S(2)}, u32[]{:S(2)}) collective-permute-start(bf16[64,1024]{1,0:T(8,128)(2,1)} %get-tuple-element.74), channel_id=1, source_target_pairs={{0,3},{1,2},{2,1},{3,0},{4,7},{5,6},{6,5},{7,4},{8,11},{9,10},{10,... | collective-permute-start | bytes 393224 | tf_op jit(solution)/shard_map/ppermute | solution.py:22
  6.5 7.1 %collective-permute-start.1 = (bf16[64,1024]{1,0:T(8,128)(2,1)}, bf16[64,1024]{1,0:T(8,128)(2,1)S(1)}, u32[]{:S(2)}, u32[]{:S(2)}) collective-permute-start(bf16[64,1024]{1,0:T(8,128)(2,1)} %get-tuple-element.75), channel_id=1, source_target_pairs={{0,2},{1,3},{2,0},{3,1},{4,6},{5,7},{6,4},{7,5},{8,10},{9,11},{10,... | collective-permute-start | bytes 393224 | tf_op jit(solution)/shard_map/ppermute | solution.py:22
  6.6 8.6 %collective-permute-start.5 = (bf16[64,1024]{1,0:T(8,128)(2,1)}, bf16[64,1024]{1,0:T(8,128)(2,1)S(1)}, u32[]{:S(2)}, u32[]{:S(2)}) collective-permute-start(bf16[64,1024]{1,0:T(8,128)(2,1)} %get-tuple-element.87), channel_id=1, source_target_pairs={{0,1},{1,0},{2,3},{3,2},{4,5},{5,4},{6,7},{7,6},{8,9},{9,8},{10,11... | collective-permute-start | bytes 393224 | tf_op jit(solution)/shard_map/ppermute | solution.py:22
  6.7 7.2 %collective-permute-start.3 = (bf16[16,2048]{1,0:T(8,128)(2,1)}, bf16[16,2048]{1,0:T(8,128)(2,1)S(1)}, u32[]{:S(2)}, u32[]{:S(2)}) collective-permute-start(bf16[16,2048]{1,0:T(8,128)(2,1)} %get-tuple-element.81), channel_id=1, source_target_pairs={{0,12},{1,13},{2,14},{3,15},{4,8},{5,9},{6,10},{7,11},{8,4},{9,5},... | collective-permute-start | bytes 196616 | tf_op jit(solution)/shard_map/ppermute | solution.py:22
  10.7 4.5 %collective-permute-start.4 = (bf16[16,2048]{1,0:T(8,128)(2,1)}, bf16[16,2048]{1,0:T(8,128)(2,1)S(1)}, u32[]{:S(2)}, u32[]{:S(2)}) collective-permute-start(bf16[16,2048]{1,0:T(8,128)(2,1)} %get-tuple-element.82), channel_id=1, source_target_pairs={{0,4},{1,5},{2,6},{3,7},{4,0},{5,1},{6,2},{7,3},{8,12},{9,13},{10,... | collective-permute-start | bytes 196616 | tf_op jit(solution)/shard_map/ppermute | solution.py:22
  16.1 13.5 %collective-permute-start.6 = (bf16[48,1024]{1,0:T(8,128)(2,1)S(1)}, bf16[48,1024]{1,0:T(8,128)(2,1)S(1)}, u32[]{:S(2)}, u32[]{:S(2)}) collective-permute-start(bf16[48,1024]{1,0:T(8,128)(2,1)S(1)} %pad_maximum_fusion.9), channel_id=1, source_target_pairs={{0,12},{1,13},{2,14},{3,15},{4,8},{5,9},{6,10},{7,11},{8,4},{9,5},... | collective-permute-start | bytes 294920 | tf_op jit(solution)/shard_map/ppermute | solution.py:22
  18.6 11.1 %collective-permute-start.7 = (bf16[64,1024]{1,0:T(8,128)(2,1)S(1)}, bf16[64,1024]{1,0:T(8,128)(2,1)S(1)}, u32[]{:S(2)}, u32[]{:S(2)}) collective-permute-start(bf16[64,1024]{1,0:T(8,128)(2,1)S(1)} %pad_maximum_fusion.7), channel_id=1, source_target_pairs={{0,8},{1,9},{2,10},{3,11},{4,12},{5,13},{6,14},{7,15},{8,0},{9,1},... | collective-permute-start | bytes 393224 | tf_op jit(solution)/shard_map/ppermute | solution.py:22
  19.2 8.6 %collective-permute-start.8 = (bf16[64,1024]{1,0:T(8,128)(2,1)S(1)}, bf16[64,1024]{1,0:T(8,128)(2,1)S(1)}, u32[]{:S(2)}, u32[]{:S(2)}) collective-permute-start(bf16[64,1024]{1,0:T(8,128)(2,1)S(1)} %copy-done.5), channel_id=1, source_target_pairs={{0,3},{1,2},{2,1},{3,0},{4,7},{5,6},{6,5},{7,4},{8,11},{9,10},{10,... | collective-permute-start | bytes 393224 | tf_op jit(solution)/shard_map/ppermute | solution.py:22
  19.5 8.4 %collective-permute-start.9 = (bf16[64,1024]{1,0:T(8,128)(2,1)S(1)}, bf16[64,1024]{1,0:T(8,128)(2,1)S(1)}, u32[]{:S(2)}, u32[]{:S(2)}) collective-permute-start(bf16[64,1024]{1,0:T(8,128)(2,1)S(1)} %copy-done.4), channel_id=1, source_target_pairs={{0,2},{1,3},{2,0},{3,1},{4,6},{5,7},{6,4},{7,5},{8,10},{9,11},{10,... | collective-permute-start | bytes 393224 | tf_op jit(solution)/shard_map/ppermute | solution.py:22
  20.8 5.7 %collective-permute-start.10 = (bf16[64,1024]{1,0:T(8,128)(2,1)S(1)}, bf16[64,1024]{1,0:T(8,128)(2,1)S(1)}, u32[]{:S(2)}, u32[]{:S(2)}) collective-permute-start(bf16[64,1024]{1,0:T(8,128)(2,1)S(1)} %pad_maximum_fusion.5), channel_id=1, source_target_pairs={{0,16},{16,0},{1,17},{17,1},{2,18},{18,2},{3,19},{19,3},{4,20},{20... | collective-permute-start | bytes 393224 | tf_op jit(solution)/shard_map/ppermute | solution.py:105
  26.5 7.6 %collective-permute-start.11 = (bf16[48,1024]{1,0:T(8,128)(2,1)S(1)}, bf16[48,1024]{1,0:T(8,128)(2,1)S(1)}, u32[]{:S(2)}, u32[]{:S(2)}) collective-permute-start(bf16[48,1024]{1,0:T(8,128)(2,1)S(1)} %pad_maximum_fusion.10), channel_id=1, source_target_pairs={{0,4},{1,5},{2,6},{3,7},{4,0},{5,1},{6,2},{7,3},{8,12},{9,13},{10,... | collective-permute-start | bytes 294920 | tf_op jit(solution)/shard_map/ppermute | solution.py:22
  28.0 8.3 %collective-permute-start.12 = (bf16[128,1024]{1,0:T(8,128)(2,1)S(1)}, bf16[128,1024]{1,0:T(8,128)(2,1)S(1)}, u32[]{:S(2)}, u32[]{:S(2)}) collective-permute-start(bf16[128,1024]{1,0:T(8,128)(2,1)S(1)} %slice_dynamic-update-slice_fusion.1), channel_id=1, source_target_pairs={{0,16},{16,0},{1,17},{17,1},{2,18},{18,2},{3,19},{19,3},{4,20},{20... | collective-permute-start | bytes 786440 | tf_op jit(solution)/shard_map/ppermute | solution.py:105
  29.7 12.3 %collective-permute-start.14 = (bf16[48,1024]{1,0:T(8,128)(2,1)S(1)}, bf16[48,1024]{1,0:T(8,128)(2,1)S(1)}, u32[]{:S(2)}, u32[]{:S(2)}) collective-permute-start(bf16[48,1024]{1,0:T(8,128)(2,1)S(1)} %pad_maximum_fusion.11), channel_id=1, source_target_pairs={{0,12},{1,13},{2,14},{3,15},{4,8},{5,9},{6,10},{7,11},{8,4},{9,5},... | collective-permute-start | bytes 294920 | tf_op jit(solution)/shard_map/ppermute | solution.py:22
  32.1 10.6 %collective-permute-start.15 = (bf16[64,1024]{1,0:T(8,128)(2,1)S(1)}, bf16[64,1024]{1,0:T(8,128)(2,1)S(1)}, u32[]{:S(2)}, u32[]{:S(2)}) collective-permute-start(bf16[64,1024]{1,0:T(8,128)(2,1)S(1)} %pad_maximum_fusion.8), channel_id=1, source_target_pairs={{0,8},{1,9},{2,10},{3,11},{4,12},{5,13},{6,14},{7,15},{8,0},{9,1},... | collective-permute-start | bytes 393224 | tf_op jit(solution)/shard_map/ppermute | solution.py:22
  32.5 9.5 %collective-permute-start.16 = (bf16[48,1024]{1,0:T(8,128)(2,1)S(1)}, bf16[48,1024]{1,0:T(8,128)(2,1)S(1)}, u32[]{:S(2)}, u32[]{:S(2)}) collective-permute-start(bf16[48,1024]{1,0:T(8,128)(2,1)S(1)} %pad_maximum_fusion.12), channel_id=1, source_target_pairs={{0,4},{1,5},{2,6},{3,7},{4,0},{5,1},{6,2},{7,3},{8,12},{9,13},{10,... | collective-permute-start | bytes 294920 | tf_op jit(solution)/shard_map/ppermute | solution.py:22
  36.3 10.6 %collective-permute-start.13 = (bf16[160,1024]{1,0:T(8,128)(2,1)S(1)}, bf16[160,1024]{1,0:T(8,128)(2,1)S(1)}, u32[]{:S(2)}, u32[]{:S(2)}) collective-permute-start(bf16[160,1024]{1,0:T(8,128)(2,1)S(1)} %pad_maximum_fusion.1), channel_id=1, source_target_pairs={{0,16},{16,0},{1,17},{17,1},{2,18},{18,2},{3,19},{19,3},{4,20},{20... | collective-permute-start | bytes 983048 | tf_op jit(solution)/shard_map/ppermute | solution.py:105
  42.7 9.5 %collective-permute-start.17 = (bf16[160,1024]{1,0:T(8,128)(2,1)S(1)}, bf16[160,1024]{1,0:T(8,128)(2,1)S(1)}, u32[]{:S(2)}, u32[]{:S(2)}) collective-permute-start(bf16[160,1024]{1,0:T(8,128)(2,1)S(1)} %pad_maximum_fusion.2), channel_id=1, source_target_pairs={{0,16},{16,0},{1,17},{17,1},{2,18},{18,2},{3,19},{19,3},{4,20},{20... | collective-permute-start | bytes 983048 | tf_op jit(solution)/shard_map/ppermute | solution.py:105
  56.9 2.0 %collective-permute-start.18 = (bf16[256,1024]{1,0:T(8,128)(2,1)S(1)}, bf16[256,1024]{1,0:T(8,128)(2,1)S(1)}, u32[]{:S(2)}, u32[]{:S(2)}) collective-permute-start(bf16[256,1024]{1,0:T(8,128)(2,1)S(1)} %fusion.35), channel_id=1, source_target_pairs={{0,1},{1,0},{2,3},{3,2},{4,5},{5,4},{6,7},{7,6},{8,9},{9,8},{10,11... | collective-permute-start | bytes 1572872 | tf_op jit(solution)/shard_map/ppermute | solution.py:22
  59.3 8.4 %collective-permute-start.19 = (bf16[128,1024]{1,0:T(8,128)(2,1)S(1)}, bf16[128,1024]{1,0:T(8,128)(2,1)S(1)}, u32[]{:S(2)}, u32[]{:S(2)}) collective-permute-start(bf16[128,1024]{1,0:T(8,128)(2,1)S(1)} %slice.215), channel_id=1, source_target_pairs={{0,2},{1,3},{2,0},{3,1},{4,6},{5,7},{6,4},{7,5},{8,10},{9,11},{10,... | collective-permute-start | bytes 786440 | tf_op jit(solution)/shard_map/ppermute | solution.py:22
  67.8 7.1 %collective-permute-start.22 = (bf16[32,1024]{1,0:T(8,128)(2,1)S(1)}, bf16[32,1024]{1,0:T(8,128)(2,1)S(1)}, u32[]{:S(2)}, u32[]{:S(2)}) collective-permute-start(bf16[32,1024]{1,0:T(8,128)(2,1)S(1)} %get-tuple-element.153), channel_id=1, source_target_pairs={{0,12},{1,13},{2,14},{3,15},{4,8},{5,9},{6,10},{7,11},{8,4},{9,5},... | collective-permute-start | bytes 196616 | tf_op jit(solution)/shard_map/ppermute | solution.py:22
  70.2 6.3 %collective-permute-start.21 = (bf16[32,1024]{1,0:T(8,128)(2,1)S(1)}, bf16[32,1024]{1,0:T(8,128)(2,1)S(1)}, u32[]{:S(2)}, u32[]{:S(2)}) collective-permute-start(bf16[32,1024]{1,0:T(8,128)(2,1)S(1)} %get-tuple-element.154), channel_id=1, source_target_pairs={{0,8},{1,9},{2,10},{3,11},{4,12},{5,13},{6,14},{7,15},{8,0},{9,1},... | collective-permute-start | bytes 196616 | tf_op jit(solution)/shard_map/ppermute | solution.py:22
  70.5 5.9 %collective-permute-start.20 = (bf16[32,1024]{1,0:T(8,128)(2,1)S(1)}, bf16[32,1024]{1,0:T(8,128)(2,1)S(1)}, u32[]{:S(2)}, u32[]{:S(2)}) collective-permute-start(bf16[32,1024]{1,0:T(8,128)(2,1)S(1)} %get-tuple-element.152), channel_id=1, source_target_pairs={{0,4},{1,5},{2,6},{3,7},{4,0},{5,1},{6,2},{7,3},{8,12},{9,13},{10,... | collective-permute-start | bytes 196616 | tf_op jit(solution)/shard_map/ppermute | solution.py:22
  (5 other events, 56.4 us)
